TPU v7x, 128 devices: a whole 4x4x4 slice. The times are simulated.
128 devices in a mesh: gy: 16 (over x, z), gx: 8 (over y, core).
Axes of the slice: x: 4, y: 4, z: 4, core: 2. Of those that a mesh axis runs over, the one named last changes fastest.
Arguments:
- coarse: bfloat16 [256, 70, 128], P(('gy', 'gx')), may hold values from -6 to 6
- enc_weight: bfloat16 [70, 128], replicated, may hold values from -0.75 to 0.75
- enc_bias: float32 [128], replicated, may hold values from -3 to 3
- block_ids: int32 [128, 16], P(('gy', 'gx')), may hold values from 0 to 255, as said below
- interp_index: int32 [128, 16], P(('gy', 'gx')), may hold values from 0 to 3
- interp_table: bfloat16 [4, 8192, 128], replicated, may hold values from -0.125 to 0.125
- noise_index: int32 [1], replicated, may hold values from 0 to 63
- noise_table: float32 [64, 128], replicated, may hold values from -6 to 6
- fine: bfloat16 [1024, 1024, 128], P('gy', 'gx'), may hold values from -6 to 6
- conv_weight: bfloat16 [9, 128, 128], replicated, may hold values from -0.1875 to 0.1875
- cotangent: bfloat16 [1024, 1024, 128], P('gy', 'gx'), may hold values from -6 to 6
Outputs:
- output: bfloat16 [1024, 1024, 128], P('gy', 'gx')
- grad_fine: bfloat16 [1024, 1024, 128], P('gy', 'gx')
- grad_coarse: float32 [256, 70, 128], P(('gy', 'gx'))
- grad_enc_weight: float32 [70, 128], replicated
- grad_enc_bias: float32 [128], replicated
- grad_conv: float32 [9, 128, 128], replicated
Inputs may be any that keep to these rules, and one draw needn't show every extreme that they name: `block_ids`: band b holds blocks b * 16 to (b + 1) * 16 - 1; the blocks named by a tile of fine tile row r lie in bands r - 1, r or r + 1.
All inputs are finite; a program needn't handle non-finite values.
Results may differ from a plain program's by a relative error of at most 0.0055.
Values may be sent and summed in bfloat16 or wider, within the bound.
No kernel may reach another device: no remote copies, remote signals or barrier semaphores. Data moves between devices by JAX's collectives and lax.ppermute only.
A program may use at most 192 MiB of HBM per device.

v0:
```python
import jax
import jax.numpy as jnp
from jax import lax
from jax.sharding import PartitionSpec as P


def padded_2(block, sides, width):
    for axis, dim in sides:
        count = lax.axis_size(axis)
        forward = [(i, i + 1) for i in range(count - 1)]
        backward = [(target, source) for source, target in forward]
        low = lax.ppermute(
            lax.slice_in_dim(block, block.shape[dim] - width, None, axis=dim), axis, forward
        )
        high = lax.ppermute(lax.slice_in_dim(block, 0, width, axis=dim), axis, backward)
        block = jnp.concatenate([low, block, high], axis=dim)
    return block


def from_behind(value, axis, steps):
    count = lax.axis_size(axis)
    first, last = (max(0, -steps), min(count, count - steps))
    return lax.ppermute(value, axis, [(source, source + steps) for source in range(first, last)])


def silu_grad(value):
    sig = jax.nn.sigmoid(value)
    return sig * (1.0 + value * (1.0 - sig))


def encode(blocks, enc_weight, enc_bias):
    return (
        jnp.einsum("nvb,vc->nbc", blocks, enc_weight, preferred_element_type=jnp.float32) + enc_bias
    )


def owner_grads(owned, pre_own, coarse, weight_f, hp):
    grad_pre = owned * silu_grad(pre_own)
    grad_coarse = jnp.einsum("vc,nbc->nvb", weight_f, grad_pre, precision=hp)
    grad_weight = jnp.einsum("nvb,nbc->vc", coarse.astype(jnp.float32), grad_pre, precision=hp)
    grad_bias = jnp.sum(grad_pre, axis=(0, 1))
    return (grad_coarse, grad_weight, grad_bias)


def body(
    coarse,
    enc_weight,
    enc_bias,
    block_ids,
    interp_index,
    interp_table,
    noise_index,
    noise_table,
    fine,
    conv_weight,
    cotangent,
):
    hp = lax.Precision.HIGHEST
    rowblk = coarse.shape[0] * lax.axis_size("gx")
    tile_h, tile_w, chans = fine.shape
    cells = tile_h * tile_w
    slots = block_ids.shape[1]
    weight_f = enc_weight.astype(jnp.float32)
    band_base = lax.axis_index("gy") * rowblk
    which = interp_index[0]
    pre_own = encode(coarse, enc_weight, enc_bias)
    enc_own = jax.nn.silu(pre_own).astype(jnp.bfloat16)
    band_row = lax.all_gather(enc_own, "gx", axis=0, tiled=True)
    window = padded_2(band_row, (("gy", 0),), rowblk)
    local_ids = block_ids[0] - band_base + rowblk

    def add_slot(slot, total):
        matrix = lax.dynamic_index_in_dim(interp_table, which[slot], 0, keepdims=False)
        block = lax.dynamic_index_in_dim(window, local_ids[slot], 0, keepdims=False)
        return total + jnp.dot(matrix, block, preferred_element_type=jnp.float32)

    lifted = lax.fori_loop(0, slots, add_slot, jnp.zeros((cells, chans), jnp.float32))
    level = noise_table.shape[0]
    embed = jnp.sum(
        jnp.where((jnp.arange(level) == noise_index[0])[:, None], noise_table, 0.0), axis=0
    )
    act = fine.astype(jnp.float32) + lifted.reshape(tile_h, tile_w, chans) + embed
    smooth = jax.nn.silu(act).astype(jnp.bfloat16)
    padded = padded_2(smooth, (("gy", 0), ("gx", 1)), 1)
    conv = jnp.zeros((cells, chans), jnp.float32)
    for tap in range(9):
        dy, dx = (tap // 3, tap % 3)
        part = padded[dy : dy + tile_h, dx : dx + tile_w].reshape(cells, chans)
        conv = conv + jnp.dot(part, conv_weight[tap], preferred_element_type=jnp.float32)
    output = (act + conv.reshape(tile_h, tile_w, chans)).astype(jnp.bfloat16)
    cot_pad = padded_2(cotangent, (("gy", 0), ("gx", 1)), 1)
    cot_flat = cotangent.reshape(cells, chans)
    back = jnp.zeros((cells, chans), jnp.float32)
    taps = []
    for tap in range(9):
        dy, dx = (tap // 3, tap % 3)
        part = cot_pad[2 - dy : 2 - dy + tile_h, 2 - dx : 2 - dx + tile_w].reshape(cells, chans)
        back = back + jnp.dot(part, conv_weight[tap].T, preferred_element_type=jnp.float32)
        near = padded[dy : dy + tile_h, dx : dx + tile_w].reshape(cells, chans)
        taps.append(
            lax.dot_general(
                near, cot_flat, (((0,), (0,)), ((), ())), preferred_element_type=jnp.float32
            )
        )
    grad_conv = jnp.stack(taps)
    grad_fine = (
        cotangent.astype(jnp.float32) + silu_grad(act) * back.reshape(tile_h, tile_w, chans)
    ).astype(jnp.bfloat16)
    grad_flat = grad_fine.reshape(cells, chans)
    slot_rows = window.shape[0]

    def add_term(slot, total):
        matrix = lax.dynamic_index_in_dim(interp_table, which[slot], 0, keepdims=False)
        term = lax.dot_general(
            matrix, grad_flat, (((0,), (0,)), ((), ())), preferred_element_type=jnp.float32
        )
        return total.at[local_ids[slot]].add(term)

    window_grad = lax.fori_loop(
        0, slots, add_term, jnp.zeros((slot_rows,) + window.shape[1:], jnp.float32)
    )
    from_below_grad = from_behind(window_grad[:rowblk].astype(jnp.bfloat16), "gy", -1).astype(
        jnp.float32
    )
    from_above_grad = from_behind(window_grad[2 * rowblk :].astype(jnp.bfloat16), "gy", 1).astype(
        jnp.float32
    )
    band_total = window_grad[rowblk : 2 * rowblk] + from_below_grad + from_above_grad
    owned = lax.psum_scatter(band_total, "gx", scatter_dimension=0, tiled=True)
    grad_coarse, grad_weight, grad_bias = owner_grads(owned, pre_own, coarse, weight_f, hp)
    grad_conv, grad_weight, grad_bias = lax.psum((grad_conv, grad_weight, grad_bias), ("gy", "gx"))
    return (output, grad_fine, grad_coarse, grad_weight, grad_bias, grad_conv)


def solution(mesh):
    placed = (
        P(("gy", "gx"), None, None),
        P(),
        P(),
        P(("gy", "gx"), None),
        P(("gy", "gx"), None),
        P(),
        P(),
        P(),
        P("gy", "gx", None),
        P(),
        P("gy", "gx", None),
    )
    return jax.shard_map(
        body,
        mesh=mesh,
        in_specs=placed,
        out_specs=(
            P("gy", "gx", None),
            P("gy", "gx", None),
            P(("gy", "gx"), None, None),
            P(),
            P(),
            P(),
        ),
        check_vma=False,
    )
```

profile of v0, /device:TPU:1, one launch (start us, length us, event | category | flops | bytes accessed | tf_op | source)
XLA Modules:
  0.0 739.7 jit_solution(2058343672814599123)
XLA Ops:
  10.4 15.0 %all_gather.3 = bf16[16,128,128]{2,1,0:T(8,128)(2,1)S(1)} all-gather(bf16[2,128,128]{2,1,0:T(8,128)(2,1)S(1)} %get-tuple-element.349), channel_id=1, replica_groups=mesh['gy'=16,'gx'=8] {'gx'}, dimensions={0}, use_global_device_ids=true | all-gather | bytes 589824 | tf_op jit(solution)/shard_map/all_gather | solution.py:68
  31.6 4.1 collective-permute-start.6
  39.2 4.1 copy.63
  43.3 4.2 copy.46
  56.7 7.9 %pad_maximum_fusion.4 = (bf16[64,128,128]{2,1,0:T(8,128)(2,1)S(1)}, bf16[64,128,128]{2,1,0:T(8,128)(2,1)S(1)}, bf16[64,128,128]{2,1,0:T(8,128)(2,1)S(1)}, bf16[6...) fusion(bf16[66,1,128]{2,1,0:T(2,128)(2,1)S(1)} %collective-permute-done.8, ...), kind=kLoop, calls=%fused_computation.57 | loop fusion | flops 25165824 | bytes 14779392 | tf_op jit(solution)/shard_map/concatenate | solution.py:16
  72.0 5.7 copy.64
  78.9 169.0 %while.29 = (s32[]{:T(128)}, f32[8192,128]{1,0:T(8,128)}, s32[16]{0:T(128)S(1)}, bf16[4,8192,128]{2,1,0:T(8,128)(2,1)}, s32[16]{0:T(128)S(1)}, /*index=5*/bf16[4...) while((s32[]{:T(128)}, f32[8192,128]{1,0:T(8,128)}, s32[16]{0:T(128)S(1)}, ...), condition=%wide.region_1.2_spmd.clone, body=%wide.region_0.1_spmd.clone.sunk | while | flops 270532608 | bytes 10518739 | solution.py:77
  84.0 4.3 convolution_add_fusion.17
  93.4 5.6 convolution_add_fusion.17
  104.1 5.6 convolution_add_fusion.17
  114.7 5.6 convolution_add_fusion.17
  125.3 5.6 convolution_add_fusion.17
  136.0 5.6 convolution_add_fusion.17
  146.6 5.6 convolution_add_fusion.17
  157.2 5.6 convolution_add_fusion.17
  167.9 5.6 convolution_add_fusion.17
  178.5 5.6 convolution_add_fusion.17
  189.2 5.6 convolution_add_fusion.17
  199.8 5.6 convolution_add_fusion.17
  210.5 5.6 convolution_add_fusion.17
  221.1 5.6 convolution_add_fusion.17
  231.8 5.6 convolution_add_fusion.17
  242.4 5.6 convolution_add_fusion.17
  248.0 5.6 copy.48
  253.6 6.9 add_convert_fusion
  260.5 4.3 collective-permute-start.2
  266.6 4.1 copy.68
  272.6 160.3 %while.28 = (s32[]{:T(128)}, f32[48,128,128]{2,1,0:T(8,128)}, s32[16]{0:T(128)S(1)}, s32[16]{0:T(128)S(1)}, bf16[4,8192,128]{2,1,0:T(8,128)(2,1)}, /*index=5*/bf...) while((s32[]{:T(128)}, f32[48,128,128]{2,1,0:T(8,128)}, ...), condition=%wide.region_5.6_spmd, body=%wide.region_3.5_spmd.sunk | while | flops 268468256 | bytes 4326634 | solution.py:119
  278.4 4.2 fusion.152
  288.4 4.2 fusion.152
  298.4 4.2 fusion.152
  308.4 4.3 fusion.152
  318.5 4.3 fusion.152
  328.5 4.3 fusion.152
  338.5 4.3 fusion.152
  348.5 4.3 fusion.152
  358.6 4.3 fusion.152
  368.6 4.3 fusion.152
  378.6 4.3 fusion.152
  388.6 4.2 fusion.152
  398.6 4.3 fusion.152
  408.6 4.2 fusion.152
  418.7 4.2 fusion.152
  428.7 4.3 fusion.152
  440.1 5.7 collective-permute-start.11
  451.5 4.1 collective-permute-start.4
  462.0 4.1 copy.52
  466.1 4.1 copy.60
  474.1 8.0 %pad_maximum_fusion = (bf16[66,129,128]{1,2,0:T(8,128)(2,1)}, bf16[66,129,128]{1,2,0:T(8,128)(2,1)S(1)}) fusion(bf16[66,1,128]{1,2,0:T(8,128)(2,1)} %copy.54, bf16[1,128,128]{1,2,0:T(8,128)(2,1)S(1)} %collective-permute-done.3, bf16[64,128,128]{1,2,0:T(8,128)(2,1)S(1)} %get-tuple-element.316, bf16[1,128,128]{1,2,0:T(8,128)(2,1)S(1)} %collective-permute-done.2, ...), kind=kLoop, calls=%fused_computation.32 | loop fusion | flops 17436672 | bytes 6555648 | tf_op jit(solution)/shard_map/concatenate | solution.py:16
  487.6 4.1 copy.51
  491.7 4.4 fusion.76
  496.1 7.7 %fusion.107 = (bf16[64,128,128]{1,2,0:T(8,128)(2,1)}, bf16[64,128,128]{1,2,0:T(8,128)(2,1)}, bf16[64,128,128]{1,2,0:T(8,128)(2,1)}) fusion(bf16[66,129,128]{1,2,0:T(8,128)(2,1)} %get-tuple-element.334), kind=kLoop, calls=%fused_computation.146 | loop fusion | bytes 12582912 | tf_op jit(solution)/shard_map/slice | solution.py:88
  503.8 4.1 copy.55
  507.9 4.1 copy.56
  512.0 4.1 copy.58
  516.0 4.1 copy.59
  520.1 4.3 copy.61
  540.4 5.7 copy.62
  548.9 5.5 add_convert_fusion.1
  557.2 3.8 fusion.52
  561.0 4.3 copy.67
  579.4 12.5 %reduce-scatter.2.cloned.1.call-done = f32[2,128,128]{2,1,0:T(8,128)} async-done(((f32[16,128,128]{2,1,0:T(8,128)}), f32[2,128,128]{2,1,0:T(8,128)}) %reduce-scatter.2.cloned.1.call-update) | async-done | bytes 131088 | tf_op jit(solution)/shard_map/reduce_scatter | solution.py:129
  594.0 68.4 %all-reduce = (f32[70,128]{1,0:T(8,128)}, f32[128]{0:T(128)}) all-reduce(f32[70,128]{1,0:T(8,128)S(1)} %convolution_bitcast_fusion.8, f32[128]{0:T(128)S(1)} %get-tuple-element.313), channel_id=1, replica_groups=mesh['gy'=16,'gx'=8] {'gy','gx'}, use_global_device_ids=true, to_apply=%region_7.8 | all-reduce | flops 9088 | bytes 72704 | tf_op jit(solution)/shard_map/psum | solution.py:131
  662.4 67.6 %all-reduce.3.cloned.1.call-done = f32[9,128,128]{2,1,0:T(8,128)} async-done(((f32[9,128,128]{2,1,0:T(8,128)}), f32[9,128,128]{2,1,0:T(8,128)}) %all-reduce.3.cloned.1.call-update) | async-done | bytes 589840 | tf_op jit(solution)/shard_map/psum | solution.py:131
  (205 shorter events, 149.8 us)
Async XLA Ops:
  8.0 0.7 copy-start
  8.0 583.9 %reduce-scatter.2.cloned.1.call-start = ((), (), s32[]{:S(2)}) async-start(), calls=%async_computation.1 | async-start | bytes 1179648 | tf_op jit(solution)/shard_map/reduce_scatter | solution.py:129
  25.3 52.4 %collective-permute-start = (bf16[16,128,128]{2,1,0:T(8,128)(2,1)S(1)}, bf16[16,128,128]{2,1,0:T(8,128)(2,1)S(1)}, u32[]{:S(2)}, u32[]{:S(2)}) collective-permute-start(bf16[16,128,128]{2,1,0:T(8,128)(2,1)S(1)} %all_gather.3), channel_id=1, source_target_pairs={{0,8},{8,16},{16,24},{24,32},{32,40},{40,48},{48,56},{56,64},{64,7... | collective-permute-start | bytes 1572872 | tf_op jit(solution)/shard_map/ppermute | solution.py:12
  28.9 48.8 %collective-permute-start.1 = (bf16[16,128,128]{2,1,0:T(8,128)(2,1)S(1)}, bf16[16,128,128]{2,1,0:T(8,128)(2,1)}, u32[]{:S(2)}, u32[]{:S(2)}) collective-permute-start(bf16[16,128,128]{2,1,0:T(8,128)(2,1)S(1)} %all_gather.3), channel_id=1, source_target_pairs={{8,0},{16,8},{24,16},{32,24},{40,32},{48,40},{56,48},{64,56},{72,6... | collective-permute-start | bytes 1572872 | tf_op jit(solution)/shard_map/ppermute | solution.py:15
  31.6 15.9 %collective-permute-start.6 = (bf16[1,128,128]{2,1,0:T(8,128)(2,1)S(1)}, bf16[1,128,128]{2,1,0:T(8,128)(2,1)S(1)}, u32[]{:S(2)}, u32[]{:S(2)}) collective-permute-start(bf16[1,128,128]{2,1,0:T(8,128)(2,1)S(1)} %get-tuple-element.342), channel_id=1, source_target_pairs={{0,8},{8,16},{16,24},{24,32},{32,40},{40,48},{48,56},{56,64},{64,7... | collective-permute-start | bytes 98312 | tf_op jit(solution)/shard_map/ppermute | solution.py:12
  35.7 11.8 %collective-permute-start.7 = (bf16[1,128,128]{2,1,0:T(8,128)(2,1)}, bf16[1,128,128]{2,1,0:T(8,128)(2,1)S(1)}, u32[]{:S(2)}, u32[]{:S(2)}) collective-permute-start(bf16[1,128,128]{2,1,0:T(8,128)(2,1)} %get-tuple-element.341), channel_id=1, source_target_pairs={{8,0},{16,8},{24,16},{32,24},{40,32},{48,40},{56,48},{64,56},{72,6... | collective-permute-start | bytes 98312 | tf_op jit(solution)/shard_map/ppermute | solution.py:15
  43.3 4.2 copy-start.1
  47.5 7.7 %copy-start.13 = (bf16[9,128,128]{2,1,0:T(8,128)(2,1)S(1)}, bf16[9,128,128]{2,1,0:T(8,128)(2,1)}, u32[]{:S(2)}) copy-start(bf16[9,128,128]{2,1,0:T(8,128)(2,1)} %param.26) | copy-start | bytes 884740
  49.3 7.3 collective-permute-start.8
  52.1 4.6 collective-permute-start.9
  77.7 1.2 copy-start.22
  260.5 185.3 %collective-permute-start.2 = (bf16[1,128,128]{1,2,0:T(8,128)(2,1)S(1)}, bf16[1,128,128]{1,2,0:T(8,128)(2,1)S(1)}, u32[]{:S(2)}, u32[]{:S(2)}) collective-permute-start(bf16[1,128,128]{1,2,0:T(8,128)(2,1)S(1)} %get-tuple-element.345), channel_id=1, source_target_pairs={{0,8},{8,16},{16,24},{24,32},{32,40},{40,48},{48,56},{56,64},{64,7... | collective-permute-start | bytes 98312 | tf_op jit(solution)/shard_map/ppermute | solution.py:12
  264.7 181.1 %collective-permute-start.3 = (bf16[1,128,128]{1,2,0:T(8,128)(2,1)S(1)}, bf16[1,128,128]{1,2,0:T(8,128)(2,1)S(1)}, u32[]{:S(2)}, u32[]{:S(2)}) collective-permute-start(bf16[1,128,128]{1,2,0:T(8,128)(2,1)S(1)} %get-tuple-element.346), channel_id=1, source_target_pairs={{8,0},{16,8},{24,16},{32,24},{40,32},{48,40},{56,48},{64,56},{72,6... | collective-permute-start | bytes 98312 | tf_op jit(solution)/shard_map/ppermute | solution.py:15
  270.6 2.0 copy-start.21
  438.8 115.6 %collective-permute-start.10 = (bf16[16,128,128]{2,1,0:T(8,128)(2,1)}, bf16[16,128,128]{2,1,0:T(8,128)(2,1)}, u32[]{:S(2)}, u32[]{:S(2)}) collective-permute-start(bf16[16,128,128]{2,1,0:T(8,128)(2,1)} %get-tuple-element.347), channel_id=1, source_target_pairs={{8,0},{16,8},{24,16},{32,24},{40,32},{48,40},{56,48},{64,56},{72,6... | collective-permute-start | bytes 1572872 | tf_op jit(solution)/shard_map/ppermute | solution.py:23
  440.1 114.3 %collective-permute-start.11 = (bf16[16,128,128]{2,1,0:T(8,128)(2,1)S(1)}, bf16[16,128,128]{2,1,0:T(8,128)(2,1)}, u32[]{:S(2)}, u32[]{:S(2)}) collective-permute-start(bf16[16,128,128]{2,1,0:T(8,128)(2,1)S(1)} %get-tuple-element.348), channel_id=1, source_target_pairs={{0,8},{8,16},{16,24},{24,32},{32,40},{40,48},{48,56},{56,64},{64,7... | collective-permute-start | bytes 1572872 | tf_op jit(solution)/shard_map/ppermute | solution.py:23
  445.8 28.3 %copy-start.17 = (bf16[1,128,128]{1,2,0:T(8,128)(2,1)}, bf16[1,128,128]{1,2,0:T(8,128)(2,1)S(1)}, u32[]{:S(2)}) copy-start(bf16[1,128,128]{1,2,0:T(8,128)(2,1)S(1)} %collective-permute-done.2) | copy-start | bytes 98308
  445.8 28.3 %copy-start.15 = (bf16[1,128,128]{1,2,0:T(8,128)(2,1)}, bf16[1,128,128]{1,2,0:T(8,128)(2,1)S(1)}, u32[]{:S(2)}) copy-start(bf16[1,128,128]{1,2,0:T(8,128)(2,1)S(1)} %collective-permute-done.3) | copy-start | bytes 98308
  451.5 18.7 %collective-permute-start.4 = (bf16[66,1,128]{2,0,1:T(8,128)(2,1)S(1)}, bf16[66,1,128]{2,0,1:T(8,128)(2,1)S(1)}, u32[]{:S(2)}, u32[]{:S(2)}) collective-permute-start(bf16[66,1,128]{2,0,1:T(8,128)(2,1)S(1)} %copy.49), channel_id=1, source_target_pairs={{0,1},{1,2},{2,3},{3,4},{4,5},{5,6},{6,7},{8,9},{9,10},{10,11},{11... | collective-permute-start | bytes 50696 | tf_op jit(solution)/shard_map/ppermute | solution.py:12
  457.8 14.4 %collective-permute-start.5 = (bf16[66,1,128]{2,0,1:T(8,128)(2,1)S(1)}, bf16[66,1,128]{2,0,1:T(8,128)(2,1)S(1)}, u32[]{:S(2)}, u32[]{:S(2)}) collective-permute-start(bf16[66,1,128]{2,0,1:T(8,128)(2,1)S(1)} %copy.53), channel_id=1, source_target_pairs={{1,0},{2,1},{3,2},{4,3},{5,4},{6,5},{7,6},{9,8},{10,9},{11,10},{12... | collective-permute-start | bytes 50696 | tf_op jit(solution)/shard_map/ppermute | solution.py:15
  474.1 8.0 %copy-start.2 = (bf16[64,128,128]{2,1,0:T(8,128)(2,1)S(1)}, bf16[64,128,128]{2,1,0:T(8,128)(2,1)}, u32[]{:S(2)}) copy-start(bf16[64,128,128]{2,1,0:T(8,128)(2,1)} %param.27) | copy-start | bytes 6291460
  482.1 2.0 copy-start.5
  524.4 3.7 copy-start.12
  528.1 1.6 copy-start.11
  529.7 1.6 copy-start.6
  531.3 1.6 copy-start.9
  532.9 1.6 copy-start.10
  534.5 1.6 copy-start.7
  536.0 1.6 copy-start.8
  540.4 5.7 copy-start.18
  546.1 2.8 copy-start.4
  557.1 172.9 %all-reduce.3.cloned.1.call-start = ((), (), s32[]{:S(2)}) async-start(), calls=%async_computation.2 | async-start | bytes 1179648 | tf_op jit(solution)/shard_map/psum | solution.py:131
  565.3 3.1 copy-start.3
  572.3 2.3 copy-start.16
  575.3 16.6 %copy-start.19 = (f32[2,128,128]{2,1,0:T(8,128)S(1)}, f32[2,128,128]{2,1,0:T(8,128)}, u32[]{:S(2)}) copy-start(f32[2,128,128]{2,1,0:T(8,128)} %get-tuple-element.350) | copy-start | bytes 393220
  575.3 18.5 %copy-start.20 = (bf16[2,70,128]{2,0,1:T(2,128)(2,1)S(1)}, bf16[2,70,128]{2,0,1:T(2,128)(2,1)}, u32[]{:S(2)}) copy-start(bf16[2,70,128]{2,0,1:T(2,128)(2,1)} %param.17) | copy-start | bytes 107524
  578.5 0.8 copy-start.14
Sparse Core Ops, SparseCore 0:
  557.3 34.5 reduce-scatter.1
Sparse Core Ops, SparseCore 1:
  579.4 150.6 all-reduce.2
where the time goes:
time: 747 us; the launch traced here: 740 us
  matrix products  202 us (27%)
  local copies, waits for them, and re-layouts  145 us (19%)
  loops' own time  125 us (17%)
  blocking collectives  83.4 us (11%)
  waiting for transfers between devices  80.2 us (11%)
  other arithmetic  52.5 us (7%)
  starting transfers between devices  35.3 us (5%)
  between operations  16.9 us (2%)
    dot_general x16, matrix products, add_slot(): return total + jnp.dot(matrix, block, preferred_element_type=jnp.float32)  88 us
    psum x1, blocking collectives, body(): lax.psum((grad_conv, grad_weight, grad_bias), ('gy', 'gx'))  68.4 us
    dot_general x16, matrix products, add_term(): lax.dot_general(matrix, grad_flat, (((0,), (0,)), ((), ())), preferred_el...  68.1 us
    psum x1, waiting for transfers between devices, body(): lax.psum((grad_conv, grad_weight, grad_bias), ('gy', 'gx'))  67.6 us
    another operation x1, loops' own time, body(): lax.fori_loop(0, slots, add_slot, jnp.zeros((cells, chans), jnp.float32))  62.3 us
    another operation x1, loops' own time, body(): lax.fori_loop(0, slots, add_term, jnp.zeros((slot_rows,) + window.shape[1...  62.2 us
    slice x10, local copies, waits for them, and re-layouts, body(): part = padded[dy:dy + tile_h, dx:dx + tile_w].reshape(cells, chans)  44 us
    unnamed x53, local copies, waits for them, and re-layouts  27.8 us
  transfers between devices with their start and end apart: 14, of which 2 were waited for; matrix products, arithmetic and copies ran while one was open for 36% of the time, Pallas kernels for 0%

commit v1 on v0

v1 whole, which is shorter than its diff:
```python
import functools

import jax
import jax.numpy as jnp
from jax import lax
from jax.experimental import pallas as pl
from jax.experimental.pallas import tpu as pltpu
from jax.sharding import PartitionSpec as P

BF = jnp.bfloat16
F32 = jnp.float32
VP = 80
META = 16
CHUNK = 8
PACK = 16
VMEM = pl.BlockSpec(memory_space=pltpu.VMEM)
SMEM = pl.BlockSpec(memory_space=pltpu.SMEM)
HBM = pl.BlockSpec(memory_space=pl.ANY)


def mm(a, b):
    return jnp.dot(a, b, preferred_element_type=F32)


def mm_t(a, b):
    return lax.dot_general(a, b, (((1,), (1,)), ((), ())), preferred_element_type=F32)


def t_mm(a, b):
    return lax.dot_general(a, b, (((0,), (0,)), ((), ())), preferred_element_type=F32)


def sigmoid(v):
    return 0.5 * jnp.tanh(0.5 * v) + 0.5


def shifted_rows(x_ref, top_ref, bot_ref, left_ref, right_ref, pad_ref):
    def emit(row, r, parity, half):
        row = row.astype(F32)
        cell = lax.broadcasted_iota(jnp.int32, row.shape, 0)
        size = row.shape[0]
        low = jnp.where(cell == 0, left_ref[r], pltpu.roll(row, 1, 0))
        high = jnp.where(cell == size - 1, right_ref[r], pltpu.roll(row, size - 1, 0))
        pad_ref[0, parity, half] = low.astype(BF)
        pad_ref[1, parity, half] = row.astype(BF)
        pad_ref[2, parity, half] = high.astype(BF)

    pairs = x_ref.shape[0] // 2
    emit(top_ref[...], 0, 0, 0)
    emit(bot_ref[...], 2 * pairs + 1, 1, pairs)

    def step(m, _):
        emit(x_ref[2 * m], 2 * m + 1, 1, m)
        emit(x_ref[2 * m + 1], 2 * m + 2, 0, m + 1)
        return 0

    lax.fori_loop(0, pairs, step, 0, unroll=2)


def windows(pad_ref, start, count):
    cells, chans = pad_ref.shape[3:]
    return jnp.concatenate(
        [
            pad_ref[d, rho % 2, pl.ds(start + rho // 2, count)].reshape(count * cells, chans)
            for rho in range(4)
            for d in range(3)
        ],
        axis=1,
    )


def back_kernel(cot_ref, top_ref, bot_ref, left_ref, right_ref, w_ref, back_ref, pad_ref, taps_ref):
    cells, chans = cot_ref.shape[1:]
    taps_ref[...] = jnp.zeros_like(taps_ref)
    for dy in range(3):
        for dx in range(3):
            for o in range(2):
                col = ((o + 2 - dy) * 3 + 2 - dx) * chans
                taps_ref[o * chans : (o + 1) * chans, col : col + chans] = w_ref[3 * dy + dx]
    shifted_rows(cot_ref, top_ref, bot_ref, left_ref, right_ref, pad_ref)
    count = 4

    def step(c, _):
        acc = mm_t(windows(pad_ref, c * count, count), taps_ref[...]).astype(BF)
        for o in range(2):
            part = acc[:, o * chans : (o + 1) * chans].reshape(count, cells, chans)
            back_ref[pl.ds(c * count, count), o] = part
        return 0

    lax.fori_loop(0, back_ref.shape[0] // count, step, 0)


def conv_kernel(
    smooth_ref, top_ref, bot_ref, left_ref, right_ref, w_ref, act_ref, out_ref, pad_ref, taps_ref
):
    cells, chans = smooth_ref.shape[1:]
    taps_ref[...] = jnp.zeros_like(taps_ref)
    for dy in range(3):
        for dx in range(3):
            for o in range(2):
                row = ((o + dy) * 3 + dx) * chans
                taps_ref[row : row + chans, o * chans : (o + 1) * chans] = w_ref[3 * dy + dx]
    shifted_rows(smooth_ref, top_ref, bot_ref, left_ref, right_ref, pad_ref)
    count = 4

    def step(c, _):
        acc = mm(windows(pad_ref, c * count, count), taps_ref[...])
        for o in range(2):
            part = acc[:, o * chans : (o + 1) * chans].reshape(count, cells, chans)
            act = act_ref[pl.ds(c * count, count), o].astype(F32)
            out_ref[pl.ds(c * count, count), o] = (act + part).astype(BF)
        return 0

    lax.fori_loop(0, out_ref.shape[0] // count, step, 0)


def main_kernel(
    loc_ref,
    which_ref,
    noise_index_ref,
    noise_ref,
    window_ref,
    weight_ref,
    bias_row_ref,
    bias_col_ref,
    pad_hbm,
    fine_ref,
    cot_ref,
    back_ref,
    table_ref,
    smooth_ref,
    act_ref,
    gfine_ref,
    edges_ref,
    terms_ref,
    shared_ref,
    enc_ref,
    enc16_ref,
    terms_acc,
    flip_ref,
    pad_ref,
    sem,
):
    step = pl.program_id(0)
    steps = pl.num_programs(0)
    rows, cells, chans = fine_ref.shape
    slots = which_ref.shape[1]
    mats = table_ref.shape[0]
    rowblk = 16
    copy = pltpu.make_async_copy(pad_hbm, pad_ref, sem)

    def block(slot):
        at = loc_ref[0, slot]
        band = lax.div(at, rowblk)
        inner = lax.rem(at, rowblk)
        return window_ref[lax.div(inner, 2), band, lax.rem(inner, 2)]

    @pl.when(step == 0)
    def _():
        copy.start()
        enc_ref[...] = jnp.zeros_like(enc_ref)
        terms_acc[...] = jnp.zeros_like(terms_acc)
        for slot in range(slots):
            pre = t_mm(block(slot), weight_ref[...]) + bias_row_ref[...]
            encoded = (pre * sigmoid(pre)).astype(BF).astype(F32)
            enc_ref[which_ref[0, slot]] += encoded
        for w in range(mats):
            high = enc_ref[w].astype(BF)
            low = (enc_ref[w] - high.astype(F32)).astype(BF)
            enc16_ref[w * chans : (w + 1) * chans, :chans] = high
            enc16_ref[w * chans : (w + 1) * chans, chans:] = low

    table = jnp.concatenate([table_ref[w] for w in range(mats)], axis=1)
    both = mm(table, enc16_ref[...])
    lifted = both[:, :chans] + both[:, chans:]
    embed = noise_ref[pl.ds(noise_index_ref[0], 1), :]
    fine = fine_ref[...].reshape(rows * cells, chans).astype(F32)
    act = fine + lifted + embed
    sig = sigmoid(act)
    smooth = act * sig
    slope = sig * (1.0 + act * (1.0 - sig))
    cot = cot_ref[...].reshape(rows * cells, chans).astype(F32)
    back = back_ref[...].reshape(rows * cells, chans).astype(F32)
    gfine = (cot + slope * back).astype(BF)
    act_ref[...] = act.astype(BF).reshape(rows, cells, chans)
    gfine_ref[...] = gfine.reshape(rows, cells, chans)
    smooth3 = smooth.reshape(rows, cells, chans)
    smooth16 = smooth3.astype(BF)
    smooth_ref[...] = smooth16
    edges_ref[0] = smooth3[:, 0:1, :].astype(BF).astype(F32)
    edges_ref[1] = smooth3[:, cells - 1 : cells, :].astype(BF).astype(F32)
    for r in range(rows):
        at = pl.multiple_of((step * (rows // 2) + r // 2) * cells, cells)
        flip_ref[(r % 2) * chans : (r % 2 + 1) * chans, pl.ds(at, cells)] = smooth16[r].T
    terms_acc[...] += mm(gfine.T, table)

    @pl.when(step == steps - 1)
    def _():
        copy.wait()
        for w in range(mats):
            terms_ref[w] = terms_acc[:, w * chans : (w + 1) * chans].astype(BF)
        pairs = flip_ref.shape[1] // cells
        lhs = flip_ref[...]
        for d in range(3):
            found = {}
            for h in range(2):
                rhs = jnp.concatenate(
                    [pad_ref[d, q, h : h + pairs].reshape(pairs * cells, chans) for q in range(2)],
                    axis=1,
                )
                got = mm(lhs, rhs)
                for o in range(2):
                    for q in range(2):
                        found[o, 2 * h + q] = got[
                            o * chans : (o + 1) * chans, q * chans : (q + 1) * chans
                        ]
            for dy in range(3):
                tap = 3 * dy + 2 - d
                total = found[0, 2 - dy] + found[1, 3 - dy]
                shared_ref[tap * chans : (tap + 1) * chans, :] = total.astype(BF)
        base = 9 * chans
        vp = weight_ref.shape[0]

        def slot_grad(slot, totals):
            gweight, gbias = totals
            coarse = block(slot)
            pre = t_mm(weight_ref[...], coarse) + bias_col_ref[...]
            sig = sigmoid(pre)
            slope = sig * (1.0 + pre * (1.0 - sig))
            at = pl.multiple_of(which_ref[0, slot] * chans, chans)
            gpre = (terms_acc[:, pl.ds(at, chans)] * slope).astype(BF)
            ones = jnp.ones((16, chans), BF)
            return (gweight + mm_t(coarse, gpre), gbias + mm_t(ones, gpre))

        totals = (jnp.zeros((vp, chans), F32), jnp.zeros((16, chans), F32))
        gweight, gbias = lax.fori_loop(0, slots, slot_grad, totals, unroll=4)
        shared_ref[base : base + vp, :] = gweight.astype(BF)
        shared_ref[base + vp : base + vp + 16, :] = gbias.astype(BF)
        rest = shared_ref.shape[0] - base - vp - 16
        shared_ref[base + vp + 16 :, :] = jnp.zeros((rest, chans), BF)


def band_kernel(loc_ref, which_ref, above_ref, own_ref, below_ref, out_ref, acc_ref):
    acc_ref[...] = jnp.zeros_like(acc_ref)
    rowblk = acc_ref.shape[0]
    for tile, terms in enumerate((above_ref, own_ref, below_ref)):
        for slot in range(which_ref.shape[1]):
            at = loc_ref[tile, slot]

            @pl.when(jnp.logical_and(at >= 0, at < rowblk))
            def _():
                acc_ref[at] += terms[which_ref[tile, slot]].astype(F32)

    out_ref[...] = acc_ref[...].astype(BF)


def owner_kernel(got_ref, coarse_ref, weight_ref, bias_col_ref, out_ref):
    weight = weight_ref[...]
    for n in range(coarse_ref.shape[0]):
        total = got_ref[0, n].astype(F32)
        for source in range(1, got_ref.shape[0]):
            total = total + got_ref[source, n].astype(F32)
        pre = t_mm(weight, coarse_ref[n]) + bias_col_ref[...]
        sig = sigmoid(pre)
        gpre = total * (sig * (1.0 + pre * (1.0 - sig)))
        high = gpre.astype(BF)
        low = (gpre - high.astype(F32)).astype(BF)
        full = mm(weight, high) + mm(weight, low)
        out_ref[n] = full[: out_ref.shape[1], :]


def sum_kernel(got_ref, out_ref):
    total = jnp.sum(got_ref[...].astype(F32), axis=0).astype(BF)
    out_ref[...] = jnp.broadcast_to(total[None], out_ref.shape)


def params(mib):
    return pltpu.CompilerParams(vmem_limit_bytes=mib * 1024 * 1024)


def shape(dims, dtype=BF):
    return jax.ShapeDtypeStruct(dims, dtype)


def cost(flops, size):
    return pl.CostEstimate(flops=flops, bytes_accessed=size, transcendentals=0)


def body(
    coarse,
    enc_weight,
    enc_bias,
    block_ids,
    interp_index,
    interp_table,
    noise_index,
    noise_table,
    fine,
    conv_weight,
    cotangent,
):
    n_gy, n_gx = lax.axis_size("gy"), lax.axis_size("gx")
    per, variables, chans = coarse.shape
    rows, cells, _ = fine.shape
    rowblk = per * n_gx
    slots = block_ids.shape[1]
    down = [(i, i + 1) for i in range(n_gy - 1)]
    up = [(i + 1, i) for i in range(n_gy - 1)]
    right = [(i, i + 1) for i in range(n_gx - 1)]
    left = [(i + 1, i) for i in range(n_gx - 1)]
    gy = lax.axis_index("gy")

    coarse_pad = jnp.pad(coarse, ((0, 0), (0, VP - variables), (0, 0)))
    own = coarse_pad.reshape(per * VP, chans)
    weight_pad = jnp.pad(enc_weight, ((0, VP - variables), (0, 0)))
    bias_row = enc_bias.reshape(1, chans)
    bias_col = enc_bias.reshape(chans, 1)
    meta = jnp.concatenate([block_ids, interp_index], axis=1).astype(BF)
    meta = jnp.pad(meta, ((0, META - 1), (0, chans - 2 * slots)))

    from_above = lax.ppermute(jnp.concatenate([own, meta, cotangent[rows - 1]]), "gy", down)
    from_below = lax.ppermute(jnp.concatenate([own, meta, cotangent[0]]), "gy", up)
    nown = per * VP
    window = jnp.concatenate([from_above[:nown], own, from_below[:nown]])
    window = jnp.broadcast_to(window[None], (n_gx,) + window.shape)
    window = lax.all_to_all(window, "gx", 0, 0, tiled=True).reshape(n_gx, 3, per, VP, chans)
    above_meta = from_above[nown : nown + 1, : 2 * slots].astype(jnp.int32)
    below_meta = from_below[nown : nown + 1, : 2 * slots].astype(jnp.int32)
    loc_all = jnp.concatenate([above_meta[:, :slots], block_ids, below_meta[:, :slots]]) - gy * rowblk
    which_all = jnp.concatenate([above_meta[:, slots:], interp_index, below_meta[:, slots:]])

    cot_top, cot_bot = from_above[nown + META :], from_below[nown + META :]

    def columns(top, bot, first, last):
        to_left = jnp.concatenate([top[:1], first, bot[:1]])
        to_right = jnp.concatenate([top[cells - 1 :], last, bot[cells - 1 :]])
        from_left = lax.ppermute(to_right, "gx", right).astype(F32)
        from_right = lax.ppermute(to_left, "gx", left).astype(F32)
        return from_left.reshape(rows + 2, 1, chans), from_right.reshape(rows + 2, 1, chans)

    cot_left, cot_right = columns(cot_top, cot_bot, cotangent[:, 0], cotangent[:, cells - 1])

    pairs = rows // 2
    pad_shape = (3, 2, pairs + 1, cells, chans)
    field = (rows, cells, chans)
    conv_flops = 2 * pairs * cells * 12 * chans * 2 * chans
    back, cot_pad = pl.pallas_call(
        back_kernel,
        out_shape=(shape((pairs, 2, cells, chans)), shape(pad_shape)),
        in_specs=[VMEM] * 6,
        out_specs=(VMEM, VMEM),
        scratch_shapes=[pltpu.VMEM((2 * chans, 12 * chans), BF)],
        compiler_params=params(40),
        cost_estimate=cost(conv_flops, 12 << 20),
        name="back",
    )(cotangent, cot_top, cot_bot, cot_left, cot_right, conv_weight)

    steps = rows // CHUNK
    mats = interp_table.shape[0]
    table = interp_table
    rows_spec = pl.BlockSpec((CHUNK, cells, chans), lambda i: (i, 0, 0))
    n_dev = n_gy * n_gx
    smooth, act, grad_fine, edges, terms, shared = pl.pallas_call(
        main_kernel,
        grid=(steps,),
        out_shape=(
            shape(field),
            shape(field),
            shape(field),
            shape((2, rows, 1, chans), F32),
            shape((mats, chans, chans)),
            shape((n_dev * PACK, chans)),
        ),
        in_specs=[
            SMEM,
            SMEM,
            SMEM,
            VMEM,
            VMEM,
            VMEM,
            VMEM,
            VMEM,
            HBM,
            rows_spec,
            rows_spec,
            rows_spec,
            pl.BlockSpec((mats, CHUNK * cells, chans), lambda i: (0, i, 0)),
        ],
        out_specs=(
            rows_spec,
            rows_spec,
            rows_spec,
            pl.BlockSpec((2, CHUNK, 1, chans), lambda i: (0, i, 0, 0)),
            VMEM,
            VMEM,
        ),
        scratch_shapes=[
            pltpu.VMEM((mats, chans, chans), F32),
            pltpu.VMEM((mats * chans, 2 * chans), BF),
            pltpu.VMEM((chans, mats * chans), F32),
            pltpu.VMEM((2 * chans, pairs * cells), BF),
            pltpu.VMEM(pad_shape, BF),
            pltpu.SemaphoreType.DMA,
        ],
        compiler_params=params(48),
        cost_estimate=cost(3 * conv_flops, 24 << 20),
        name="main",
    )(
        loc_all[1:2] + rowblk,
        interp_index,
        noise_index,
        noise_table,
        window,
        weight_pad,
        bias_row,
        bias_col,
        cot_pad,
        fine,
        cotangent,
        back.reshape(field),
        table,
    )

    both = ("gy", "gx")
    parts = lax.all_to_all(shared.reshape(n_dev, PACK, chans), both, 0, 0, tiled=True)

    smooth_top = lax.ppermute(smooth[rows - 1], "gy", down)
    smooth_bot = lax.ppermute(smooth[0], "gy", up)
    terms_above = lax.ppermute(terms, "gy", down)
    terms_below = lax.ppermute(terms, "gy", up)
    band = pl.pallas_call(
        band_kernel,
        out_shape=shape((rowblk, chans, chans)),
        in_specs=[SMEM, SMEM, VMEM, VMEM, VMEM],
        out_specs=VMEM,
        scratch_shapes=[pltpu.VMEM((rowblk, chans, chans), F32)],
        compiler_params=params(16),
        cost_estimate=cost(1 << 22, 1 << 20),
        name="band",
    )(loc_all, which_all, terms_above, terms, terms_below)
    owned = lax.all_to_all(band.reshape(n_gx, per, chans, chans), "gx", 0, 0, tiled=True)
    edges = edges.astype(BF).reshape(2, rows, chans)
    smooth_left, smooth_right = columns(smooth_top, smooth_bot, edges[0], edges[1])
    output = pl.pallas_call(
        conv_kernel,
        out_shape=shape((pairs, 2, cells, chans)),
        in_specs=[VMEM] * 7,
        out_specs=VMEM,
        scratch_shapes=[
            pltpu.VMEM(pad_shape, BF),
            pltpu.VMEM((12 * chans, 2 * chans), BF),
        ],
        compiler_params=params(40),
        cost_estimate=cost(conv_flops, 8 << 20),
        name="conv",
    )(
        smooth,
        smooth_top,
        smooth_bot,
        smooth_left,
        smooth_right,
        conv_weight,
        act.reshape(pairs, 2, cells, chans),
    ).reshape(field)
    grad_coarse = pl.pallas_call(
        owner_kernel,
        out_shape=shape(coarse.shape, F32),
        in_specs=[VMEM] * 4,
        out_specs=VMEM,
        compiler_params=params(16),
        name="owner",
    )(owned, coarse_pad, weight_pad, bias_col)

    summed = pl.pallas_call(
        sum_kernel,
        out_shape=shape((n_dev, PACK, chans)),
        in_specs=[VMEM],
        out_specs=VMEM,
        compiler_params=params(16),
        name="total",
    )(parts)
    total = lax.all_to_all(summed, both, 0, 0, tiled=True).reshape(n_dev * PACK, chans).astype(F32)
    base = 9 * chans
    grad_conv = total[:base].reshape(9, chans, chans)
    grad_weight = total[base : base + variables]
    grad_bias = total[base + VP]
    return (output, grad_fine, grad_coarse, grad_weight, grad_bias, grad_conv)


def solution(mesh):
    placed = (
        P(("gy", "gx"), None, None),
        P(),
        P(),
        P(("gy", "gx"), None),
        P(("gy", "gx"), None),
        P(),
        P(),
        P(),
        P("gy", "gx", None),
        P(),
        P("gy", "gx", None),
    )
    return jax.shard_map(
        body,
        mesh=mesh,
        in_specs=placed,
        out_specs=(
            P("gy", "gx", None),
            P("gy", "gx", None),
            P(("gy", "gx"), None, None),
            P(),
            P(),
            P(),
        ),
        check_vma=False,
    )
```

time: 747 us -> 127 us (0.17)
  matrix products: 202 us -> 0 us
  local copies, waits for them, and re-layouts: 145 us -> 18.4 us
  loops' own time: 125 us -> 0 us
  blocking collectives: 83.4 us -> 0 us
  waiting for transfers between devices: 80.2 us -> 9.12 us
  other arithmetic: 52.5 us -> 2.27 us
  Pallas kernels: 0 us -> 37.6 us
  starting transfers between devices: 35.3 us -> 57.2 us
  between operations: 16.9 us -> 1.68 us
    dot_general x62 -> x0, matrix products: 202 us -> none  [the longest x16 88 us: add_slot(): return total + jnp.dot(matrix, block, preferred_element_type=jnp.float32)]
    another operation x2 -> x0, loops' own time: 125 us -> none  [the longest x1 62.3 us: body(): lax.fori_loop(0, slots, add_slot, jnp.zeros((cells, chans), jnp.float32))]
    psum x1 -> x0, blocking collectives: 68.4 us -> none  [body(): lax.psum((grad_conv, grad_weight, grad_bias), ('gy', 'gx'))]
    psum x1 -> x0, waiting for transfers between devices: 67.6 us -> none  [body(): lax.psum((grad_conv, grad_weight, grad_bias), ('gy', 'gx'))]
    slice x17 -> x13, local copies, waits for them, and re-layouts: 54 us -> 3.45 us  [the longest x1 1.03 us: body(): cotangent[:, 0]]
    pallas_call x0 -> x6, Pallas kernels: none -> 37.6 us  [the longest x1 21 us: body(): pl.pallas_call(main_kernel, grid=(steps,), out_shape=(shape(field), shape...]
    dynamic_slice x64 -> x0, local copies, waits for them, and re-layouts: 37.4 us -> none  [the longest x16 9.41 us: add_slot(): which[slot]]
    all_to_all x0 -> x4, starting transfers between devices: none -> 29 us  [the longest x1 9.85 us: body(): lax.all_to_all(summed, both, 0, 0, tiled=True).reshape(n_dev * PACK, chans)]
  transfers between devices with their start and end apart: 14 -> 14, of which waited for: 2 -> 5; matrix products, arithmetic and copies ran while one was open for 36% -> 5% of each run, Pallas kernels for 0% -> 13%
where the time goes in v1:
time: 127 us; the launch traced here: 126 us
  starting transfers between devices  57.2 us (45%)
  Pallas kernels  37.6 us (30%)
  local copies, waits for them, and re-layouts  18.4 us (14%)
  waiting for transfers between devices  9.12 us (7%)
  other arithmetic  2.27 us (2%)
  between operations  1.68 us (1%)
    pallas_call x1, Pallas kernels, body(): pl.pallas_call(main_kernel, grid=(steps,), out_shape=(shape(field), shape...  21 us
    unnamed x28, local copies, waits for them, and re-layouts  10.4 us
    all_to_all x1, starting transfers between devices, body(): lax.all_to_all(summed, both, 0, 0, tiled=True).reshape(n_dev * PACK, chans)  9.85 us
    all_to_all x1, starting transfers between devices, body(): lax.all_to_all(shared.reshape(n_dev, PACK, chans), both, 0, 0, tiled=True)  9.04 us
    ppermute x2, starting transfers between devices, columns(): from_left = lax.ppermute(to_right, 'gx', right).astype(F32)  8.55 us
    pallas_call x1, Pallas kernels, body(): pl.pallas_call(conv_kernel, out_shape=shape((pairs, 2, cells, chans)), in...  7.1 us
    pallas_call x1, Pallas kernels, body(): pl.pallas_call(back_kernel, out_shape=(shape((pairs, 2, cells, chans)), s...  6 us
    all_to_all x1, starting transfers between devices, body(): lax.all_to_all(band.reshape(n_gx, per, chans, chans), 'gx', 0, 0, tiled=T...  5.13 us
  transfers between devices with their start and end apart: 14, of which 5 were waited for; matrix products, arithmetic and copies ran while one was open for 5% of the time, Pallas kernels for 13%

profile of v1, /device:TPU:1, one launch (start us, length us, event | category | flops | bytes accessed | tf_op | source)
XLA Modules:
  0.0 126.3 jit_solution(8370033491007089146)
XLA Ops:
  0.6 0.8 copy.17
  1.4 0.8 slice_bitcast_fusion.3
  2.2 0.7 convert.10
  2.8 0.7 convert.11
  3.5 0.1 fusion.5
  3.6 0.0 copy-start
  3.6 4.5 %collective-permute-start = (bf16[304,128]{1,0:T(8,128)(2,1)S(1)}, bf16[304,128]{1,0:T(8,128)(2,1)S(1)}, u32[]{:S(2)}, u32[]{:S(2)}) collective-permute-start(bf16[304,128]{1,0:T(8,128)(2,1)S(1)} %get-tuple-element.38), channel_id=1, source_target_pairs={{0,8},{8,16},{16,24},{24,32},{32,40},{40,48},{48,56},{56,64},{64,7... | collective-permute-start | bytes 233480 | tf_op jit(solution)/shard_map/ppermute | solution.py:321
  8.1 1.3 %collective-permute-start.1 = (bf16[304,128]{1,0:T(8,128)(2,1)S(1)}, bf16[304,128]{1,0:T(8,128)(2,1)S(1)}, u32[]{:S(2)}, u32[]{:S(2)}) collective-permute-start(bf16[304,128]{1,0:T(8,128)(2,1)S(1)} %get-tuple-element.39), channel_id=1, source_target_pairs={{8,0},{16,8},{24,16},{32,24},{40,32},{48,40},{56,48},{64,56},{72,6... | collective-permute-start | bytes 233480 | tf_op jit(solution)/shard_map/ppermute | solution.py:322
  9.4 1.0 fusion.6
  10.5 0.8 copy.20.bias_col_ref
  11.3 0.7 pad.14.weight_ref
  12.6 0.0 collective-permute-done
  12.7 0.8 collective-permute-done.1
  13.5 5.0 %collective-permute-start.2 = (bf16[66,128]{1,0:T(8,128)(2,1)S(1)}, bf16[66,128]{1,0:T(8,128)(2,1)S(1)}, u32[]{:S(2)}, u32[]{:S(2)}) collective-permute-start(bf16[66,128]{1,0:T(8,128)(2,1)S(1)} %pad_maximum_fusion.4), channel_id=1, source_target_pairs={{0,1},{1,2},{2,3},{3,4},{4,5},{5,6},{6,7},{8,9},{9,10},{10,11},{11... | collective-permute-start | bytes 50696 | tf_op jit(solution)/shard_map/ppermute | solution.py:337
  18.5 1.9 %collective-permute-start.3 = (bf16[66,128]{1,0:T(8,128)(2,1)S(1)}, bf16[66,128]{1,0:T(8,128)(2,1)S(1)}, u32[]{:S(2)}, u32[]{:S(2)}) collective-permute-start(bf16[66,128]{1,0:T(8,128)(2,1)S(1)} %pad_maximum_fusion.5), channel_id=1, source_target_pairs={{1,0},{2,1},{3,2},{4,3},{5,4},{6,5},{7,6},{9,8},{10,9},{11,10},{12... | collective-permute-start | bytes 50696 | tf_op jit(solution)/shard_map/ppermute | solution.py:338
  20.5 0.1 fusion.11
  20.6 1.1 broadcast_in_dim.2
  21.6 5.0 %all-to-all-start = ((bf16[8,480,128]{2,1,0:T(8,128)(2,1)}), bf16[8,480,128]{2,1,0:T(8,128)(2,1)S(1)}, u32[]{:S(2)}, u32[]{:S(2)}) async-start(bf16[8,480,128]{2,1,0:T(8,128)(2,1)} %broadcast_in_dim.2), calls=%async_computation | async-start | bytes 1966080 | tf_op jit(solution)/shard_map/all_to_all | solution.py:326
  26.6 0.7 slice_convert_fusion
  27.3 0.1 fusion.12
  27.4 0.8 slice.132.bot_ref
  28.2 0.0 collective-permute-done.2
  28.2 0.0 collective-permute-done.3
  28.3 0.0 copy-start.3
  28.3 1.0 copy-done.3
  29.3 6.0 %back.1 = (bf16[32,2,128,128]{3,2,1,0:T(8,128)(2,1)S(1)}, bf16[3,2,33,128,128]{4,3,2,1,0:T(8,128)(2,1)S(1)}) custom-call(bf16[64,128,128]{2,1,0:T(8,128)(2,1)S(1)} %copy-done, bf16[128,128]{1,0:T(8,128)(2,1)S(1)} %slice.131.top_ref, bf16[128,128]{1,0:T(8,128)(2,1)S(1)} %slice.132.bot_ref, f32[66,1,128]{2,1,0:T(1,128)S(1)} %reshape.119.left_ref, ...), custom_call_target="tpu_custom_call" | custom-call | flops 3221225472 | bytes 12582912 | tf_op jit(solution)/shard_map/back/pallas_call | solution.py:347
  35.3 0.0 copy-start.8
  35.3 1.3 %copy-done.8 = bf16[32,2,128,128]{3,2,1,0:T(8,128)(2,1)} copy-done((bf16[32,2,128,128]{3,2,1,0:T(8,128)(2,1)}, bf16[32,2,128,128]{3,2,1,0:T(8,128)(2,1)S(1)}, u32[]{:S(2)}) %copy-start.8) | copy-done | bytes 2097176
  36.6 2.7 %copy-done.9 = bf16[3,2,33,128,128]{4,3,2,1,0:T(8,128)(2,1)} copy-done((bf16[3,2,33,128,128]{4,3,2,1,0:T(8,128)(2,1)}, bf16[3,2,33,128,128]{4,3,2,1,0:T(8,128)(2,1)S(1)}, u32[]{:S(2)}) %copy-start.9) | copy-done | bytes 6488088
  39.3 1.7 %all-to-all-done = bf16[8,480,128]{2,1,0:T(8,128)(2,1)S(1)} async-done(((bf16[8,480,128]{2,1,0:T(8,128)(2,1)}), bf16[8,480,128]{2,1,0:T(8,128)(2,1)S(1)}, u32[]{:S(2)}, u32[]{:S(2)}) %all-to-all-start) | async-done | bytes 983072 | tf_op jit(solution)/shard_map/all_to_all | solution.py:326
  41.1 21.0 %main.1 = (bf16[64,128,128]{2,1,0:T(8,128)(2,1)S(1)}, bf16[64,128,128]{2,1,0:T(8,128)(2,1)S(1)}, bf16[64,128,128]{2,1,0:T(8,128)(2,1)}, f32[2,64,1,128]{3,2,1,0:...) custom-call(s32[1,16]{1,0:T(1,128)S(1)} %slice_add_fusion.loc_ref, s32[1,16]{1,0:T(1,128)S(1)} %copy-done.2, ...), custom_call_target="tpu_custom_call" | custom-call | flops 9663676416 | bytes 25165824 | tf_op jit(solution)/shard_map/main/pallas_call | solution.py:363
  62.1 0.0 copy-start.6
  62.1 1.3 %copy-done.6 = bf16[64,128,128]{2,1,0:T(8,128)(2,1)} copy-done((bf16[64,128,128]{2,1,0:T(8,128)(2,1)}, bf16[64,128,128]{2,1,0:T(8,128)(2,1)S(1)}, u32[]{:S(2)}) %copy-start.6) | copy-done | bytes 2097176
  63.4 9.0 %all-to-all-start.2 = ((bf16[128,16,128]{2,1,0:T(8,128)(2,1)}), bf16[128,16,128]{2,1,0:T(8,128)(2,1)S(1)}, u32[]{:S(2)}, u32[]{:S(2)}) async-start(bf16[128,16,128]{2,1,0:T(8,128)(2,1)} %bitcast.18), calls=%async_computation.2 | async-start | bytes 1048576 | tf_op jit(solution)/shard_map/all_to_all | solution.py:425
  72.4 3.4 %collective-permute-start.8 = (bf16[4,128,128]{2,1,0:T(8,128)(2,1)S(1)}, bf16[4,128,128]{2,1,0:T(8,128)(2,1)S(1)}, u32[]{:S(2)}, u32[]{:S(2)}) collective-permute-start(bf16[4,128,128]{2,1,0:T(8,128)(2,1)S(1)} %get-tuple-element.20.own_ref), channel_id=1, source_target_pairs={{0,8},{8,16},{16,24},{24,32},{32,40},{40,48},{48,56},{56,64},{64,7... | collective-permute-start | bytes 393224 | tf_op jit(solution)/shard_map/ppermute | solution.py:429
  75.9 1.3 %collective-permute-start.9 = (bf16[4,128,128]{2,1,0:T(8,128)(2,1)S(1)}, bf16[4,128,128]{2,1,0:T(8,128)(2,1)S(1)}, u32[]{:S(2)}, u32[]{:S(2)}) collective-permute-start(bf16[4,128,128]{2,1,0:T(8,128)(2,1)S(1)} %get-tuple-element.20.own_ref), channel_id=1, source_target_pairs={{8,0},{16,8},{24,16},{32,24},{40,32},{48,40},{56,48},{64,56},{72,6... | collective-permute-start | bytes 393224 | tf_op jit(solution)/shard_map/ppermute | solution.py:430
  77.2 0.6 slice_bitcast_fusion
  77.8 4.0 %collective-permute-start.4 = (bf16[128,128]{1,0:T(8,128)(2,1)}, bf16[128,128]{1,0:T(8,128)(2,1)S(1)}, u32[]{:S(2)}, u32[]{:S(2)}) collective-permute-start(bf16[128,128]{1,0:T(8,128)(2,1)} %get-tuple-element.29), channel_id=1, source_target_pairs={{0,8},{8,16},{16,24},{24,32},{32,40},{40,48},{48,56},{56,64},{64,7... | collective-permute-start | bytes 98312 | tf_op jit(solution)/shard_map/ppermute | solution.py:427
  81.8 1.3 %collective-permute-start.5 = (bf16[128,128]{1,0:T(8,128)(2,1)S(1)}, bf16[128,128]{1,0:T(8,128)(2,1)S(1)}, u32[]{:S(2)}, u32[]{:S(2)}) collective-permute-start(bf16[128,128]{1,0:T(8,128)(2,1)S(1)} %get-tuple-element.28), channel_id=1, source_target_pairs={{8,0},{16,8},{24,16},{32,24},{40,32},{48,40},{56,48},{64,56},{72,6... | collective-permute-start | bytes 98312 | tf_op jit(solution)/shard_map/ppermute | solution.py:428
  83.1 0.0 collective-permute-done.8.above_ref
  83.1 1.0 collective-permute-done.9.below_ref
  84.1 2.2 %band.1 = bf16[16,128,128]{2,1,0:T(8,128)(2,1)} custom-call(s32[3,16]{1,0:T(4,128)S(1)} %add_subtract_fusion.loc_ref, s32[3,16]{1,0:T(4,128)S(1)} %pad_add_fusion.which_ref, bf16[4,128,128]{2,1,0:T(8,128)(2,1)S(1)} %collective-permute-done.8.above_ref, bf16[4,128,128]{2,1,0:T(8,128)(2,1)S(1)} %get-tuple-element.20.own_ref, ...), custom_call_target="tpu_custom_call" | custom-call | flops 4194304 | bytes 1048576 | tf_op jit(solution)/shard_map/band/pallas_call | solution.py:431
  86.2 0.0 all-to-all-done.2.got_ref
  86.2 5.1 %all-to-all-start.1 = ((bf16[8,2,128,128]{3,2,1,0:T(8,128)(2,1)}), bf16[8,2,128,128]{3,2,1,0:T(8,128)(2,1)S(1)}, u32[]{:S(2)}, u32[]{:S(2)}) async-start(bf16[8,2,128,128]{3,2,1,0:T(8,128)(2,1)} %bitcast.17), calls=%async_computation.1 | async-start | bytes 1048576 | tf_op jit(solution)/shard_map/all_to_all | solution.py:441
  91.4 0.0 collective-permute-done.4.top_ref
  91.4 0.0 collective-permute-done.5.bot_ref
  91.4 3.5 %collective-permute-start.6 = (bf16[66,128]{1,0:T(8,128)(2,1)S(1)}, bf16[66,128]{1,0:T(8,128)(2,1)S(1)}, u32[]{:S(2)}, u32[]{:S(2)}) collective-permute-start(bf16[66,128]{1,0:T(8,128)(2,1)S(1)} %pad_maximum_fusion.6), channel_id=1, source_target_pairs={{0,1},{1,2},{2,3},{3,4},{4,5},{5,6},{6,7},{8,9},{9,10},{10,11},{11... | collective-permute-start | bytes 50696 | tf_op jit(solution)/shard_map/ppermute | solution.py:337
  95.0 1.9 %collective-permute-start.7 = (bf16[66,128]{1,0:T(8,128)(2,1)S(1)}, bf16[66,128]{1,0:T(8,128)(2,1)S(1)}, u32[]{:S(2)}, u32[]{:S(2)}) collective-permute-start(bf16[66,128]{1,0:T(8,128)(2,1)S(1)} %pad_maximum_fusion.7), channel_id=1, source_target_pairs={{1,0},{2,1},{3,2},{4,3},{5,4},{6,5},{7,6},{9,8},{10,9},{11,10},{12... | collective-permute-start | bytes 50696 | tf_op jit(solution)/shard_map/ppermute | solution.py:338
  96.9 1.0 total.1
  97.9 3.0 %all-to-all-done.1.got_ref = bf16[8,2,128,128]{3,2,1,0:T(8,128)(2,1)S(1)} async-done(((bf16[8,2,128,128]{3,2,1,0:T(8,128)(2,1)}), bf16[8,2,128,128]{3,2,1,0:T(8,128)(2,1)S(1)}, u32[]{:S(2)}, u32[]{:S(2)}) %all-to-all-start.1) | async-done | bytes 524320 | tf_op jit(solution)/shard_map/all_to_all | solution.py:441
  100.8 9.8 %all-to-all-start.3 = ((bf16[128,16,128]{2,1,0:T(8,128)(2,1)}), bf16[128,16,128]{2,1,0:T(8,128)(2,1)S(1)}, u32[]{:S(2)}, u32[]{:S(2)}) async-start(bf16[128,16,128]{2,1,0:T(8,128)(2,1)} %total.1), calls=%async_computation.3 | async-start | bytes 1048576 | tf_op jit(solution)/shard_map/all_to_all | solution.py:482
  110.7 0.0 collective-permute-done.6
  110.8 0.0 collective-permute-done.7
  110.8 0.0 copy-start.4
  110.8 1.0 copy-done.4
  111.8 1.6 %copy-done.7 = bf16[64,128,128]{2,1,0:T(8,128)(2,1)S(1)} copy-done((bf16[64,128,128]{2,1,0:T(8,128)(2,1)S(1)}, bf16[64,128,128]{2,1,0:T(8,128)(2,1)}, u32[]{:S(2)}) %copy-start.7) | copy-done | bytes 2097176
  113.4 7.1 %conv.1 = bf16[32,2,128,128]{3,2,1,0:T(8,128)(2,1)} custom-call(bf16[64,128,128]{2,1,0:T(8,128)(2,1)S(1)} %get-tuple-element.16.smooth_ref, bf16[128,128]{1,0:T(8,128)(2,1)S(1)} %collective-permute-done.4.top_ref, bf16[128,128]{1,0:T(8,128)(2,1)S(1)} %collective-permute-done.5.bot_ref, f32[66,1,128]{2,1,0:T(1,128)S(1)} %copy.22.left_ref, ...), custom_call_target="tpu_custom_call" | custom-call | flops 3221225472 | bytes 8388608 | tf_op jit(solution)/shard_map/conv/pallas_call | solution.py:444
  120.5 0.4 owner.1
  120.9 0.7 copy.24
  121.6 2.7 %all-to-all-done.3 = bf16[128,16,128]{2,1,0:T(8,128)(2,1)S(1)} async-done(((bf16[128,16,128]{2,1,0:T(8,128)(2,1)}), bf16[128,16,128]{2,1,0:T(8,128)(2,1)S(1)}, u32[]{:S(2)}, u32[]{:S(2)}) %all-to-all-start.3) | async-done | bytes 524320 | tf_op jit(solution)/shard_map/all_to_all | solution.py:482
  124.2 0.1 convert_element_type.37
  124.3 0.6 slice.143
  124.9 0.5 slice_bitcast_fusion.6
  125.4 0.9 slice.145
  (40 shorter events, 0.3 us)
Async XLA Ops:
  3.6 23.8 %copy-start.11 = (s32[1,16]{1,0:T(1,128)S(1)}, s32[1,16]{1,0:T(1,128)}, u32[]{:S(2)}) copy-start(s32[1,16]{1,0:T(1,128)} %param.14) | copy-start | bytes 196
  3.6 24.7 %copy-start = (bf16[64,128,128]{2,1,0:T(8,128)(2,1)S(1)}, bf16[64,128,128]{2,1,0:T(8,128)(2,1)}, u32[]{:S(2)}) copy-start(bf16[64,128,128]{2,1,0:T(8,128)(2,1)} %cot_ref.3) | copy-start | bytes 6291460
  3.6 9.0 %collective-permute-start = (bf16[304,128]{1,0:T(8,128)(2,1)S(1)}, bf16[304,128]{1,0:T(8,128)(2,1)S(1)}, u32[]{:S(2)}, u32[]{:S(2)}) collective-permute-start(bf16[304,128]{1,0:T(8,128)(2,1)S(1)} %get-tuple-element.38), channel_id=1, source_target_pairs={{0,8},{8,16},{16,24},{24,32},{32,40},{40,48},{48,56},{56,64},{64,7... | collective-permute-start | bytes 233480 | tf_op jit(solution)/shard_map/ppermute | solution.py:321
  8.1 5.3 %collective-permute-start.1 = (bf16[304,128]{1,0:T(8,128)(2,1)S(1)}, bf16[304,128]{1,0:T(8,128)(2,1)S(1)}, u32[]{:S(2)}, u32[]{:S(2)}) collective-permute-start(bf16[304,128]{1,0:T(8,128)(2,1)S(1)} %get-tuple-element.39), channel_id=1, source_target_pairs={{8,0},{16,8},{24,16},{32,24},{40,32},{48,40},{56,48},{64,56},{72,6... | collective-permute-start | bytes 233480 | tf_op jit(solution)/shard_map/ppermute | solution.py:322
  13.5 8.2 %copy-start.10 = (bf16[304,128]{1,0:T(8,128)(2,1)}, bf16[304,128]{1,0:T(8,128)(2,1)S(1)}, u32[]{:S(2)}) copy-start(bf16[304,128]{1,0:T(8,128)(2,1)S(1)} %collective-permute-done.1) | copy-start | bytes 233476
  13.5 14.7 %collective-permute-start.2 = (bf16[66,128]{1,0:T(8,128)(2,1)S(1)}, bf16[66,128]{1,0:T(8,128)(2,1)S(1)}, u32[]{:S(2)}, u32[]{:S(2)}) collective-permute-start(bf16[66,128]{1,0:T(8,128)(2,1)S(1)} %pad_maximum_fusion.4), channel_id=1, source_target_pairs={{0,1},{1,2},{2,3},{3,4},{4,5},{5,6},{6,7},{8,9},{9,10},{10,11},{11... | collective-permute-start | bytes 50696 | tf_op jit(solution)/shard_map/ppermute | solution.py:337
  18.5 9.7 %collective-permute-start.3 = (bf16[66,128]{1,0:T(8,128)(2,1)S(1)}, bf16[66,128]{1,0:T(8,128)(2,1)S(1)}, u32[]{:S(2)}, u32[]{:S(2)}) collective-permute-start(bf16[66,128]{1,0:T(8,128)(2,1)S(1)} %pad_maximum_fusion.5), channel_id=1, source_target_pairs={{1,0},{2,1},{3,2},{4,3},{5,4},{6,5},{7,6},{9,8},{10,9},{11,10},{12... | collective-permute-start | bytes 50696 | tf_op jit(solution)/shard_map/ppermute | solution.py:338
  21.6 19.4 %all-to-all-start = ((bf16[8,480,128]{2,1,0:T(8,128)(2,1)}), bf16[8,480,128]{2,1,0:T(8,128)(2,1)S(1)}, u32[]{:S(2)}, u32[]{:S(2)}) async-start(bf16[8,480,128]{2,1,0:T(8,128)(2,1)} %broadcast_in_dim.2), calls=%async_computation | async-start | bytes 1966080 | tf_op jit(solution)/shard_map/all_to_all | solution.py:326
  28.3 1.0 copy-start.3
  29.3 11.8 %copy-start.1 = (f32[128]{0:T(128)S(1)}, f32[128]{0:T(128)}, u32[]{:S(2)}) copy-start(f32[128]{0:T(128)} %param.13) | copy-start | bytes 1540
  29.3 11.8 %copy-start.2 = (s32[1,16]{1,0:T(1,128)S(1)}, s32[1,16]{1,0:T(1,128)}, u32[]{:S(2)}) copy-start(s32[1,16]{1,0:T(1,128)} %which_ref.1) | copy-start | bytes 196
  29.3 11.8 %copy-start.5 = (f32[64,128]{1,0:T(8,128)S(1)}, f32[64,128]{1,0:T(8,128)}, u32[]{:S(2)}) copy-start(f32[64,128]{1,0:T(8,128)} %noise_ref.1) | copy-start | bytes 98308
  35.3 1.3 %copy-start.8 = (bf16[32,2,128,128]{3,2,1,0:T(8,128)(2,1)}, bf16[32,2,128,128]{3,2,1,0:T(8,128)(2,1)S(1)}, u32[]{:S(2)}) copy-start(bf16[32,2,128,128]{3,2,1,0:T(8,128)(2,1)S(1)} %get-tuple-element.15) | copy-start | bytes 6291460
  36.6 2.7 %copy-start.9 = (bf16[3,2,33,128,128]{4,3,2,1,0:T(8,128)(2,1)}, bf16[3,2,33,128,128]{4,3,2,1,0:T(8,128)(2,1)S(1)}, u32[]{:S(2)}) copy-start(bf16[3,2,33,128,128]{4,3,2,1,0:T(8,128)(2,1)S(1)} %get-tuple-element.14.pad_hbm) | copy-start | bytes 19464196
  62.1 1.3 %copy-start.6 = (bf16[64,128,128]{2,1,0:T(8,128)(2,1)}, bf16[64,128,128]{2,1,0:T(8,128)(2,1)S(1)}, u32[]{:S(2)}) copy-start(bf16[64,128,128]{2,1,0:T(8,128)(2,1)S(1)} %get-tuple-element.18) | copy-start | bytes 6291460
  63.4 22.9 %all-to-all-start.2 = ((bf16[128,16,128]{2,1,0:T(8,128)(2,1)}), bf16[128,16,128]{2,1,0:T(8,128)(2,1)S(1)}, u32[]{:S(2)}, u32[]{:S(2)}) async-start(bf16[128,16,128]{2,1,0:T(8,128)(2,1)} %bitcast.18), calls=%async_computation.2 | async-start | bytes 1048576 | tf_op jit(solution)/shard_map/all_to_all | solution.py:425
  72.4 10.7 %collective-permute-start.8 = (bf16[4,128,128]{2,1,0:T(8,128)(2,1)S(1)}, bf16[4,128,128]{2,1,0:T(8,128)(2,1)S(1)}, u32[]{:S(2)}, u32[]{:S(2)}) collective-permute-start(bf16[4,128,128]{2,1,0:T(8,128)(2,1)S(1)} %get-tuple-element.20.own_ref), channel_id=1, source_target_pairs={{0,8},{8,16},{16,24},{24,32},{32,40},{40,48},{48,56},{56,64},{64,7... | collective-permute-start | bytes 393224 | tf_op jit(solution)/shard_map/ppermute | solution.py:429
  75.9 8.2 %collective-permute-start.9 = (bf16[4,128,128]{2,1,0:T(8,128)(2,1)S(1)}, bf16[4,128,128]{2,1,0:T(8,128)(2,1)S(1)}, u32[]{:S(2)}, u32[]{:S(2)}) collective-permute-start(bf16[4,128,128]{2,1,0:T(8,128)(2,1)S(1)} %get-tuple-element.20.own_ref), channel_id=1, source_target_pairs={{8,0},{16,8},{24,16},{32,24},{40,32},{48,40},{56,48},{64,56},{72,6... | collective-permute-start | bytes 393224 | tf_op jit(solution)/shard_map/ppermute | solution.py:430
  77.8 13.6 %collective-permute-start.4 = (bf16[128,128]{1,0:T(8,128)(2,1)}, bf16[128,128]{1,0:T(8,128)(2,1)S(1)}, u32[]{:S(2)}, u32[]{:S(2)}) collective-permute-start(bf16[128,128]{1,0:T(8,128)(2,1)} %get-tuple-element.29), channel_id=1, source_target_pairs={{0,8},{8,16},{16,24},{24,32},{32,40},{40,48},{48,56},{56,64},{64,7... | collective-permute-start | bytes 98312 | tf_op jit(solution)/shard_map/ppermute | solution.py:427
  81.8 9.6 %collective-permute-start.5 = (bf16[128,128]{1,0:T(8,128)(2,1)S(1)}, bf16[128,128]{1,0:T(8,128)(2,1)S(1)}, u32[]{:S(2)}, u32[]{:S(2)}) collective-permute-start(bf16[128,128]{1,0:T(8,128)(2,1)S(1)} %get-tuple-element.28), channel_id=1, source_target_pairs={{8,0},{16,8},{24,16},{32,24},{40,32},{48,40},{56,48},{64,56},{72,6... | collective-permute-start | bytes 98312 | tf_op jit(solution)/shard_map/ppermute | solution.py:428
  86.2 14.6 %all-to-all-start.1 = ((bf16[8,2,128,128]{3,2,1,0:T(8,128)(2,1)}), bf16[8,2,128,128]{3,2,1,0:T(8,128)(2,1)S(1)}, u32[]{:S(2)}, u32[]{:S(2)}) async-start(bf16[8,2,128,128]{3,2,1,0:T(8,128)(2,1)} %bitcast.17), calls=%async_computation.1 | async-start | bytes 1048576 | tf_op jit(solution)/shard_map/all_to_all | solution.py:441
  91.4 19.3 %collective-permute-start.6 = (bf16[66,128]{1,0:T(8,128)(2,1)S(1)}, bf16[66,128]{1,0:T(8,128)(2,1)S(1)}, u32[]{:S(2)}, u32[]{:S(2)}) collective-permute-start(bf16[66,128]{1,0:T(8,128)(2,1)S(1)} %pad_maximum_fusion.6), channel_id=1, source_target_pairs={{0,1},{1,2},{2,3},{3,4},{4,5},{5,6},{6,7},{8,9},{9,10},{10,11},{11... | collective-permute-start | bytes 50696 | tf_op jit(solution)/shard_map/ppermute | solution.py:337
  95.0 15.8 %collective-permute-start.7 = (bf16[66,128]{1,0:T(8,128)(2,1)S(1)}, bf16[66,128]{1,0:T(8,128)(2,1)S(1)}, u32[]{:S(2)}, u32[]{:S(2)}) collective-permute-start(bf16[66,128]{1,0:T(8,128)(2,1)S(1)} %pad_maximum_fusion.7), channel_id=1, source_target_pairs={{1,0},{2,1},{3,2},{4,3},{5,4},{6,5},{7,6},{9,8},{10,9},{11,10},{12... | collective-permute-start | bytes 50696 | tf_op jit(solution)/shard_map/ppermute | solution.py:338
  100.8 23.4 %all-to-all-start.3 = ((bf16[128,16,128]{2,1,0:T(8,128)(2,1)}), bf16[128,16,128]{2,1,0:T(8,128)(2,1)S(1)}, u32[]{:S(2)}, u32[]{:S(2)}) async-start(bf16[128,16,128]{2,1,0:T(8,128)(2,1)} %total.1), calls=%async_computation.3 | async-start | bytes 1048576 | tf_op jit(solution)/shard_map/all_to_all | solution.py:482
  110.8 1.0 copy-start.4
  111.8 1.6 %copy-start.7 = (bf16[64,128,128]{2,1,0:T(8,128)(2,1)S(1)}, bf16[64,128,128]{2,1,0:T(8,128)(2,1)}, u32[]{:S(2)}) copy-start(bf16[64,128,128]{2,1,0:T(8,128)(2,1)} %copy-done.6) | copy-start | bytes 6291460

commit v2 on v0

v2 whole, which is shorter than its diff:
```python
import functools

import jax
import jax.numpy as jnp
from jax import lax
from jax.experimental import pallas as pl
from jax.experimental.pallas import tpu as pltpu
from jax.sharding import PartitionSpec as P

BF = jnp.bfloat16
F32 = jnp.float32
VP = 80
META = 16
CHUNK = 16
PAIRS = 8
PACK = 16
LIMIT = 52
VMEM = pl.BlockSpec(memory_space=pltpu.VMEM)
SMEM = pl.BlockSpec(memory_space=pltpu.SMEM)
HBM = pl.BlockSpec(memory_space=pl.ANY)


def mm(a, b):
    return jnp.dot(a, b, preferred_element_type=F32)


def mm_t(a, b):
    return lax.dot_general(a, b, (((1,), (1,)), ((), ())), preferred_element_type=F32)


def t_mm(a, b):
    return lax.dot_general(a, b, (((0,), (0,)), ((), ())), preferred_element_type=F32)


def sigmoid(v):
    return 0.5 * jnp.tanh(0.5 * v) + 0.5


def put_row(row, r, at, half, left_ref, right_ref, pad_ref):
    row = row.astype(F32)
    size, chans = row.shape
    cell = lax.broadcasted_iota(jnp.int32, row.shape, 0)
    low = jnp.where(cell == 0, left_ref[pl.ds(r, 1), :], pltpu.roll(row, 1, 0))
    high = jnp.where(cell == size - 1, right_ref[pl.ds(r, 1), :], pltpu.roll(row, size - 1, 0))
    lanes = slice(half * chans, (half + 1) * chans)
    pad_ref[0, at, :, lanes] = low.astype(BF)
    pad_ref[1, at, :, lanes] = row.astype(BF)
    pad_ref[2, at, :, lanes] = high.astype(BF)


def place_columns(got_left, got_right, left_ref, right_ref):
    rows = got_left.shape[0] - 32
    left_ref[...] = got_left.astype(F32)
    right_ref[...] = got_right.astype(F32)
    for at in (rows, rows + 16):
        left_ref[at : at + 1, :] = left_ref[at + 15 : at + 16, :]


def put_pairs(x_ref, start, count, left_ref, right_ref, pad_ref):
    for k in range(count):
        m = start + k
        put_row(x_ref[2 * m], 2 * m, m, 1, left_ref, right_ref, pad_ref)
        put_row(x_ref[2 * m + 1], 2 * m + 1, m + 1, 0, left_ref, right_ref, pad_ref)


def windows(pad_ref, start, count):
    cells, lanes = pad_ref.shape[2:]
    return jnp.concatenate(
        [
            pad_ref[d, pl.ds(start + h, count)].reshape(count * cells, lanes)
            for h in range(2)
            for d in range(3)
        ],
        axis=1,
    )


def lane_of(rho, d):
    return ((rho // 2) * 3 + d) * 2 + rho % 2


def start_all(copies):
    for copy in copies:
        copy.start()


def wait_all(copies):
    for copy in copies:
        copy.wait()


def pack_kernel(
    coarse_ref, ids_hbm, which_hbm, cot_hbm, own_ref, all_ref, down_ref, up_ref,
    work_ref, meta_ref, small_ref, sems,
):
    per, variables, chans = coarse_ref.shape
    rows, cells = cot_hbm.shape[:2]
    copies = [
        pltpu.make_async_copy(ids_hbm, small_ref.at[0], sems.at[2]),
        pltpu.make_async_copy(which_hbm, small_ref.at[1], sems.at[3]),
        pltpu.make_async_copy(cot_hbm.at[rows - 1], down_ref.at[pl.ds(META, cells)], sems.at[0]),
        pltpu.make_async_copy(cot_hbm.at[0], up_ref.at[pl.ds(META, cells)], sems.at[1]),
    ]
    start_all(copies)
    work_ref[...] = jnp.zeros_like(work_ref)
    for n in range(per):
        work_ref[n * VP : n * VP + variables, :] = coarse_ref[n].astype(F32)
    work = work_ref[...].astype(BF)
    own_ref[...] = work
    for target in range(all_ref.shape[0]):
        all_ref[target] = work
    meta_ref[...] = jnp.zeros_like(meta_ref)
    wait_all(copies)
    slots = small_ref.shape[2]
    meta_ref[0:1, :slots] = small_ref[0].astype(F32)
    meta_ref[1:2, :slots] = small_ref[1].astype(F32)
    down_ref[:META, :] = meta_ref[...].astype(BF)
    up_ref[:META, :] = meta_ref[...].astype(BF)


def fill_columns(got_left, got_right, above_ref, below_ref, left_ref, right_ref, pad_ref):
    cells = pad_ref.shape[2]
    rows = got_left.shape[0] - 32
    place_columns(got_left, got_right, left_ref, right_ref)
    base = above_ref.shape[0] - cells
    put_row(above_ref[base:, :], rows + 16, 0, 0, left_ref, right_ref, pad_ref)
    put_row(below_ref[base:, :], rows, rows // 2, 1, left_ref, right_ref, pad_ref)


def back_kernel(
    cot_hbm, above_ref, below_ref, left16_ref, right16_ref, w_ref,
    back_hbm, cot_ref, back_ref, pad_ref, taps_ref, left_ref, right_ref, in_sems, out_sems,
):
    pairs, _, cells, chans = back_ref.shape
    count = PAIRS
    groups = pairs // count

    def fetch(g):
        at = pl.ds(g * 2 * count, 2 * count)
        return pltpu.make_async_copy(cot_hbm.at[at], cot_ref.at[at], in_sems.at[g])

    def send(g):
        at = pl.ds(g * count, count)
        return pltpu.make_async_copy(back_ref.at[at], back_hbm.at[at], out_sems.at[g])

    start_all([fetch(g) for g in range(groups)])
    taps_ref[...] = jnp.zeros_like(taps_ref)
    for dy in range(3):
        for dx in range(3):
            for o in range(2):
                col = lane_of(o + 2 - dy, 2 - dx) * chans
                taps_ref[o * chans : (o + 1) * chans, col : col + chans] = w_ref[3 * dy + dx]
    fill_columns(
        left16_ref[...], right16_ref[...], above_ref, below_ref, left_ref, right_ref, pad_ref
    )

    def pad(g, _):
        fetch(g).wait()
        put_pairs(cot_ref, g * count, count, left_ref, right_ref, pad_ref)
        return 0

    lax.fori_loop(0, groups, pad, 0)

    def step(g, _):
        acc = mm_t(windows(pad_ref, g * count, count), taps_ref[...]).astype(BF)
        for o in range(2):
            part = acc[:, o * chans : (o + 1) * chans].reshape(count, cells, chans)
            back_ref[pl.ds(g * count, count), o] = part
        send(g).start()
        return 0

    lax.fori_loop(0, groups, step, 0)
    wait_all([send(g) for g in range(groups)])


def conv_kernel(
    pos_ref, smooth_hbm, above_ref, below_ref, got_left_ref, got_right_ref, w_ref, act_hbm,
    out_hbm, smooth_ref, act_ref, out_ref, pad_ref, taps_ref, left_ref, right_ref, sems,
):
    pairs, _, cells, chans = out_ref.shape
    rows = 2 * pairs
    count = PAIRS
    groups = pairs // count

    def piece(src, dst, kind, g, size):
        at = pl.ds(g * size, size)
        return pltpu.make_async_copy(src.at[at], dst.at[at], sems.at[kind, g])

    def fetch(g):
        return piece(smooth_hbm, smooth_ref, 0, g, 2 * count)

    def fetch_act(g):
        return piece(act_hbm, act_ref, 1, g, count)

    def send(g):
        return piece(out_ref, out_hbm, 2, g, count)

    start_all([fetch(g) for g in range(groups)])
    start_all([fetch_act(g) for g in range(groups)])
    taps_ref[...] = jnp.zeros_like(taps_ref)
    for dy in range(3):
        for dx in range(3):
            for o in range(2):
                row = lane_of(o + dy, dx) * chans
                taps_ref[row : row + chans, o * chans : (o + 1) * chans] = w_ref[3 * dy + dx]
    gx, n_gx = pos_ref[1], pos_ref[2]
    base = got_left_ref.shape[0] - rows - 32
    from_left = jnp.where(gx > 0, got_left_ref[base:, :].astype(F32), 0.0)
    from_right = jnp.where(gx < n_gx - 1, got_right_ref[base:, :].astype(F32), 0.0)
    fill_columns(from_left, from_right, above_ref, below_ref, left_ref, right_ref, pad_ref)

    def pad(g, _):
        fetch(g).wait()
        put_pairs(smooth_ref, g * count, count, left_ref, right_ref, pad_ref)
        return 0

    lax.fori_loop(0, groups, pad, 0)

    def step(g, _):
        fetch_act(g).wait()
        acc = mm(windows(pad_ref, g * count, count), taps_ref[...])
        for o in range(2):
            part = acc[:, o * chans : (o + 1) * chans].reshape(count, cells, chans)
            act = act_ref[pl.ds(g * count, count), o].astype(F32)
            out_ref[pl.ds(g * count, count), o] = (act + part).astype(BF)
        send(g).start()
        return 0

    lax.fori_loop(0, groups, step, 0)
    wait_all([send(g) for g in range(groups)])


def main_kernel(
    pos_ref, ids_ref, which_ref, noise_index_ref, noise_ref, band_above_ref, band_own_ref, band_below_ref, weight_ref,
    bias_col_ref, above_ref, below_ref, left16_ref, right16_ref,
    fine_hbm, cot_hbm, back_hbm, table_hbm,
    smooth_hbm, act_hbm, gfine_hbm, edges_ref, terms_ref, down_ref, up_ref, shared_ref,
    pad_ref, cot_ref, fine_ref, back_ref, table_ref, smooth_ref, act_ref, gfine_ref,
    coarse_ref, slope_ref, gpre_ref, enc_ref, enc16_ref, terms_acc, flip_ref,
    left_ref, right_ref, in_sems, out_sems,
):
    total_rows, cells, chans = fine_ref.shape
    slots = which_ref.shape[1]
    mats = table_ref.shape[0]
    rows = CHUNK
    steps = total_rows // rows
    pairs = total_rows // 2
    rowblk = band_own_ref.shape[0] // VP
    first_band = pos_ref[0] * rowblk - rowblk

    def fetches(step):
        at = pl.ds(step * rows, rows)
        flat = pl.ds(step * rows * cells, rows * cells)
        return [
            pltpu.make_async_copy(table_hbm.at[:, flat], table_ref.at[:, flat], in_sems.at[0, step]),
            pltpu.make_async_copy(fine_hbm.at[at], fine_ref.at[at], in_sems.at[1, step]),
            pltpu.make_async_copy(back_hbm.at[at], back_ref.at[at], in_sems.at[2, step]),
            pltpu.make_async_copy(cot_hbm.at[at], cot_ref.at[at], in_sems.at[3, step]),
        ]

    def sends(step):
        at = pl.ds(step * rows, rows)
        return [
            pltpu.make_async_copy(smooth_ref.at[at], smooth_hbm.at[at], out_sems.at[0, step]),
            pltpu.make_async_copy(act_ref.at[at], act_hbm.at[at], out_sems.at[1, step]),
            pltpu.make_async_copy(gfine_ref.at[at], gfine_hbm.at[at], out_sems.at[2, step]),
        ]

    for step in range(steps):
        start_all(fetches(step))
    enc_ref[...] = jnp.zeros_like(enc_ref)
    terms_acc[...] = jnp.zeros_like(terms_acc)
    group = 4

    def encode(first, _):
        for k in range(group):
            slot = first * group + k
            at = ids_ref[0, slot] - first_band
            band = lax.div(at, rowblk)
            source = pl.ds(pl.multiple_of(lax.rem(at, rowblk) * VP, VP), VP)
            block = jnp.where(
                band == 1,
                band_own_ref[source, :],
                jnp.where(band == 0, band_above_ref[source, :], band_below_ref[source, :]),
            )
            coarse_ref[:, pl.ds(pl.multiple_of(slot * cells, cells), cells)] = block
        size = group * cells
        lanes = pl.ds(pl.multiple_of(first * size, size), size)
        pre = t_mm(weight_ref[...], coarse_ref[:, lanes]) + bias_col_ref[...]
        sig = sigmoid(pre)
        encoded = (pre * sig).astype(BF).astype(F32)
        slope_ref[:, lanes] = sig * (1.0 + pre * (1.0 - sig))
        for k in range(group):
            enc_ref[which_ref[0, first * group + k]] += encoded[:, k * cells : (k + 1) * cells]
        return 0

    lax.fori_loop(0, slots // group, encode, 0)
    for w in range(mats):
        high = enc_ref[w].astype(BF)
        low = (enc_ref[w] - high.astype(F32)).astype(BF)
        enc16_ref[:chans, w * cells : (w + 1) * cells] = high
        enc16_ref[chans:, w * cells : (w + 1) * cells] = low
    embed = noise_ref[pl.ds(noise_index_ref[0], 1), :]
    fill_columns(
        left16_ref[...], right16_ref[...], above_ref, below_ref, left_ref, right_ref, pad_ref
    )

    def chunk(step, _):
        wait_all(fetches(step))
        at = pl.ds(step * rows, rows)
        flat = pl.ds(pl.multiple_of(step * rows * cells, rows * cells), rows * cells)
        table = jnp.concatenate([table_ref[w, flat, :] for w in range(mats)], axis=1)
        both = mm_t(table, enc16_ref[...])
        lifted = both[:, :chans] + both[:, chans:]
        fine = fine_ref[at].reshape(rows * cells, chans).astype(F32)
        act = fine + lifted + embed
        sig = sigmoid(act)
        smooth = act * sig
        slope = sig * (1.0 + act * (1.0 - sig))
        cot = cot_ref[at].reshape(rows * cells, chans).astype(F32)
        back = back_ref[at].reshape(rows * cells, chans).astype(F32)
        gfine = (cot + slope * back).astype(BF)
        act_ref[at] = act.astype(BF).reshape(rows, cells, chans)
        gfine_ref[at] = gfine.reshape(rows, cells, chans)
        smooth3 = smooth.reshape(rows, cells, chans)
        smooth16 = smooth3.astype(BF)
        smooth_ref[at] = smooth16
        for r in range(rows):
            row = pl.ds(step * rows + r, 1)
            edges_ref[0, row, :] = smooth3[r, 0:1, :]
            edges_ref[1, row, :] = smooth3[r, cells - 1 : cells, :]
            lanes = pl.ds(pl.multiple_of((step * (rows // 2) + r // 2) * cells, cells), cells)
            flip_ref[(r % 2) * chans : (r % 2 + 1) * chans, lanes] = smooth16[r].T
        put_pairs(cot_ref, step * (rows // 2), rows // 2, left_ref, right_ref, pad_ref)
        terms_acc[...] += mm(gfine.T, table)
        start_all(sends(step))
        return 0

    lax.fori_loop(0, steps, chunk, 0)

    size = mats * chans
    for w in range(mats):
        terms = terms_acc[:, w * cells : (w + 1) * cells]
        terms_ref[w] = terms
        down_ref[w * chans : (w + 1) * chans, :] = terms.astype(BF)
        up_ref[w * chans : (w + 1) * chans, :] = terms.astype(BF)
    down_ref[size:, :] = smooth_ref[total_rows - 1]
    up_ref[size:, :] = smooth_ref[0]

    def conv_grad(d, _):
        found = []
        for h in range(2):
            rhs = pad_ref[d, h : h + pairs].reshape(pairs * cells, 2 * chans)
            found.append(mm(flip_ref[...], rhs))
        for dy in range(3):
            total = jnp.zeros((chans, chans), F32)
            for o in range(2):
                rho = o + 2 - dy
                lanes = slice(rho % 2 * chans, (rho % 2 + 1) * chans)
                total = total + found[rho // 2][o * chans : (o + 1) * chans, lanes]
            tap = pl.multiple_of((3 * dy + 2 - d) * chans, chans)
            shared_ref[pl.ds(tap, chans), :] = total.astype(BF)
        return 0

    lax.fori_loop(0, 3, conv_grad, 0)

    def slot_grad(slot, gsum):
        lanes = pl.ds(pl.multiple_of(slot * cells, cells), cells)
        gpre = terms_ref[which_ref[0, slot]] * slope_ref[:, lanes]
        gpre_ref[:, lanes] = gpre.astype(BF)
        return gsum + gpre

    gsum = lax.fori_loop(0, slots, slot_grad, jnp.zeros((chans, cells), F32), unroll=2)
    gweight = mm_t(coarse_ref[...], gpre_ref[...])
    ones = jnp.ones((16, cells), BF)
    high = gsum.astype(BF)
    gbias = mm_t(ones, high) + mm_t(ones, (gsum - high.astype(F32)).astype(BF))
    base = 9 * chans
    for part in (gweight, gbias):
        count = part.shape[0]
        high = part.astype(BF)
        shared_ref[base : base + count, :] = high
        shared_ref[base + count : base + 2 * count, :] = (part - high.astype(F32)).astype(BF)
        base += 2 * count
    shared_ref[base:, :] = jnp.zeros((shared_ref.shape[0] - base, chans), BF)
    for step in range(steps):
        wait_all(sends(step))


def band_kernel(
    pos_ref, loc_ref, which_ref, above_ref, own_ref, below_ref, edges_ref,
    mine_ref, *refs,
):
    outs, acc_ref = refs[:-1], refs[-1]
    acc_ref[...] = jnp.zeros_like(acc_ref)
    rowblk, chans, cells = acc_ref.shape

    def slot_terms(slot, _):
        for tile in range(3):
            at, w = loc_ref[tile, slot], which_ref[tile, slot]

            @pl.when(jnp.logical_and(at >= 0, at < rowblk))
            def _():
                if tile == 1:
                    acc_ref[at] += own_ref[w]
                else:
                    terms = (above_ref, below_ref)[tile // 2]
                    rows = pl.ds(pl.multiple_of(w * chans, chans), chans)
                    acc_ref[at] += terms[rows, :].astype(F32)

        return 0

    lax.fori_loop(0, which_ref.shape[1], slot_terms, 0)
    gx, n_gx = pos_ref[1], len(outs) + 1
    per = rowblk // n_gx
    for n in range(per):
        mine_ref[n] = acc_ref[gx * per + n]
    for k, out_ref in enumerate(outs, 1):
        target = lax.rem(gx + k, n_gx)
        for n in range(per):
            out_ref[n * chans : (n + 1) * chans, :] = acc_ref[target * per + n].astype(BF)
    if not outs:
        return
    size = above_ref.shape[0] - cells
    base = per * chans
    edge = edges_ref.shape[1]
    for out_ref, column, first in ((outs[0], 1, cells - 16), (outs[-1], 0, 0)):
        rows = slice(first, first + 16)
        out_ref[base : base + edge, :] = edges_ref[column].astype(BF)
        out_ref[base + edge : base + edge + 16, :] = below_ref[size:, :][rows]
        out_ref[base + edge + 16 :, :] = above_ref[size:, :][rows]


def owner_kernel(mine_ref, coarse_ref, weight_ref, bias_col_ref, *refs):
    gots, out_ref = refs[:-1], refs[-1]
    weight = weight_ref[...]
    chans = weight.shape[1]
    for n in range(out_ref.shape[0]):
        total = mine_ref[n]
        for got_ref in gots:
            total = total + got_ref[n * chans : (n + 1) * chans, :].astype(F32)
        pre = t_mm(weight, coarse_ref[n * VP : (n + 1) * VP, :]) + bias_col_ref[...]
        sig = sigmoid(pre)
        gpre = total * (sig * (1.0 + pre * (1.0 - sig)))
        high = gpre.astype(BF)
        low = (gpre - high.astype(F32)).astype(BF)
        full = mm(weight, high) + mm(weight, low)
        out_ref[n] = full[: out_ref.shape[1], :]


def sum_kernel(got_ref, out_ref):
    total = jnp.sum(got_ref[...].astype(F32), axis=0).astype(BF)
    out_ref[...] = jnp.broadcast_to(total[None], out_ref.shape)


def finish_kernel(got_ref, gconv_ref, gweight_ref, gbias_ref):
    taps, chans, _ = gconv_ref.shape
    variables = gweight_ref.shape[0]
    for tap in range(taps):
        gconv_ref[tap] = got_ref[tap * chans : (tap + 1) * chans, :].astype(F32)
    base = taps * chans
    high = got_ref[base : base + VP, :].astype(F32)
    low = got_ref[base + VP : base + 2 * VP, :].astype(F32)
    gweight_ref[...] = (high + low)[:variables, :]
    base += 2 * VP
    high = got_ref[base : base + 16, :].astype(F32)
    low = got_ref[base + 16 : base + 32, :].astype(F32)
    gbias_ref[...] = (high + low)[:1, :]


def params(mib):
    return pltpu.CompilerParams(vmem_limit_bytes=mib * 1024 * 1024)


def shape(dims, dtype=BF):
    return jax.ShapeDtypeStruct(dims, dtype)


def cost(flops, size):
    return pl.CostEstimate(flops=flops, bytes_accessed=size, transcendentals=0)


def body(
    coarse,
    enc_weight,
    enc_bias,
    block_ids,
    interp_index,
    interp_table,
    noise_index,
    noise_table,
    fine,
    conv_weight,
    cotangent,
):
    n_gy, n_gx = lax.axis_size("gy"), lax.axis_size("gx")
    per, variables, chans = coarse.shape
    rows, cells, _ = fine.shape
    rowblk = per * n_gx
    slots = block_ids.shape[1]
    mats = interp_table.shape[0]
    pairs = rows // 2
    down = [(i, i + 1) for i in range(n_gy - 1)]
    up = [(i + 1, i) for i in range(n_gy - 1)]
    right = [(i, i + 1) for i in range(n_gx - 1)]
    left = [(i + 1, i) for i in range(n_gx - 1)]
    both = ("gy", "gx")
    gy = lax.axis_index("gy")
    pos = jnp.stack([gy, lax.axis_index("gx"), jnp.int32(n_gx)]).astype(jnp.int32)
    nown = per * VP

    own, spread, to_below, to_above = pl.pallas_call(
        pack_kernel,
        out_shape=(
            shape((nown, chans)),
            shape((n_gx, nown, chans)),
            shape((META + cells, chans)),
            shape((META + cells, chans)),
        ),
        in_specs=[VMEM, HBM, HBM, HBM],
        out_specs=(VMEM,) * 4,
        scratch_shapes=[
            pltpu.VMEM((nown, chans), F32),
            pltpu.VMEM((META, chans), F32),
            pltpu.VMEM((2, 1, slots), jnp.int32),
            pltpu.SemaphoreType.DMA((4,)),
        ],
        compiler_params=params(LIMIT),
        name="pack",
    )(coarse, block_ids, interp_index, cotangent)
    band_own = lax.all_to_all(spread, "gx", 0, 0, tiled=True).reshape(rowblk * VP, chans)
    from_above = lax.ppermute(to_below, "gy", down)
    from_below = lax.ppermute(to_above, "gy", up)
    to_left = jnp.concatenate(
        [cotangent[:, 0], from_below[META : META + 16], from_above[META : META + 16]]
    )
    to_right = jnp.concatenate(
        [
            cotangent[:, cells - 1],
            from_below[META + cells - 16 :],
            from_above[META + cells - 16 :],
        ]
    )
    cot_left = lax.ppermute(to_right, "gx", right)
    cot_right = lax.ppermute(to_left, "gx", left)
    band_above = lax.ppermute(band_own, "gy", down)
    band_below = lax.ppermute(band_own, "gy", up)

    weight_pad = jnp.pad(enc_weight, ((0, VP - variables), (0, 0)))
    bias_col = enc_bias.reshape(chans, 1)
    pad_shape = (3, pairs + 1, cells, 2 * chans)
    field = (rows, cells, chans)
    paired = (pairs, 2, cells, chans)
    columns = pltpu.VMEM((rows + 32, chans), F32)
    conv_flops = 2 * pairs * cells * 12 * chans * 2 * chans
    groups = pairs // PAIRS
    back = pl.pallas_call(
        back_kernel,
        out_shape=shape(paired),
        in_specs=[HBM] + [VMEM] * 5,
        out_specs=HBM,
        scratch_shapes=[
            pltpu.VMEM(field, BF),
            pltpu.VMEM(paired, BF),
            pltpu.VMEM(pad_shape, BF),
            pltpu.VMEM((2 * chans, 12 * chans), BF),
            columns,
            columns,
            pltpu.SemaphoreType.DMA((groups,)),
            pltpu.SemaphoreType.DMA((groups,)),
        ],
        compiler_params=params(LIMIT),
        cost_estimate=cost(conv_flops, 12 << 20),
        name="back",
    )(cotangent, from_above, from_below, cot_left, cot_right, conv_weight)

    n_dev = n_gy * n_gx
    steps = rows // CHUNK
    smooth, act, grad_fine, edges, terms, to_below, to_above, shared = pl.pallas_call(
        main_kernel,
        out_shape=(
            shape(field),
            shape(field),
            shape(field),
            shape((2, rows, chans), F32),
            shape((mats, chans, chans), F32),
            shape((mats * chans + cells, chans)),
            shape((mats * chans + cells, chans)),
            shape((n_dev * PACK, chans)),
        ),
        in_specs=[SMEM] * 4 + [VMEM] * 10 + [HBM] * 4,
        out_specs=(HBM,) * 3 + (VMEM,) * 5,
        scratch_shapes=[
            pltpu.VMEM(pad_shape, BF),
            pltpu.VMEM(field, BF),
            pltpu.VMEM(field, BF),
            pltpu.VMEM(field, BF),
            pltpu.VMEM(interp_table.shape, BF),
            pltpu.VMEM(field, BF),
            pltpu.VMEM(field, BF),
            pltpu.VMEM(field, BF),
            pltpu.VMEM((VP, slots * chans), BF),
            pltpu.VMEM((chans, slots * chans), F32),
            pltpu.VMEM((chans, slots * chans), BF),
            pltpu.VMEM((mats, chans, chans), F32),
            pltpu.VMEM((2 * chans, mats * chans), BF),
            pltpu.VMEM((chans, mats * chans), F32),
            pltpu.VMEM((2 * chans, pairs * cells), BF),
            columns,
            columns,
            pltpu.SemaphoreType.DMA((4, steps)),
            pltpu.SemaphoreType.DMA((3, steps)),
        ],
        compiler_params=params(LIMIT),
        cost_estimate=cost(3 * conv_flops, 24 << 20),
        name="main",
    )(
        pos,
        block_ids,
        interp_index,
        noise_index,
        noise_table,
        band_above,
        band_own,
        band_below,
        weight_pad,
        bias_col,
        from_above,
        from_below,
        cot_left,
        cot_right,
        fine,
        cotangent,
        back.reshape(field),
        interp_table,
    )

    parts = lax.all_to_all(shared.reshape(n_dev, PACK, chans), both, 0, 0, tiled=True)

    below2 = lax.ppermute(to_above, "gy", up)
    above2 = lax.ppermute(to_below, "gy", down)
    above_meta = from_above[:2, :slots].astype(jnp.int32)
    below_meta = from_below[:2, :slots].astype(jnp.int32)
    loc_all = jnp.concatenate([above_meta[:1], block_ids, below_meta[:1]]) - gy * rowblk
    which_all = jnp.concatenate([above_meta[1:], interp_index, below_meta[1:]])
    plain, full = per * chans, per * chans + rows + 32
    lengths = [full if k in (1, n_gx - 1) else plain for k in range(1, n_gx)]
    mine, *sent = pl.pallas_call(
        band_kernel,
        out_shape=[shape((per, chans, chans), F32)] + [shape((n, chans)) for n in lengths],
        in_specs=[SMEM] * 3 + [VMEM] * 4,
        out_specs=[VMEM] * n_gx,
        scratch_shapes=[pltpu.VMEM((rowblk, chans, chans), F32)],
        compiler_params=params(8),
        cost_estimate=cost(1 << 22, 1 << 20),
        name="band",
    )(pos, loc_all, which_all, above2, terms, below2, edges)
    got = [
        lax.ppermute(part, "gx", [(i, (i + k) % n_gx) for i in range(n_gx)])
        for k, part in enumerate(sent, 1)
    ]

    summed = pl.pallas_call(
        sum_kernel,
        out_shape=shape((n_dev, PACK, chans)),
        in_specs=[VMEM],
        out_specs=VMEM,
        compiler_params=params(8),
        name="total",
    )(parts)
    total = lax.all_to_all(summed, both, 0, 0, tiled=True).reshape(n_dev * PACK, chans)

    output = pl.pallas_call(
        conv_kernel,
        out_shape=shape(paired),
        in_specs=[SMEM, HBM] + [VMEM] * 5 + [HBM],
        out_specs=HBM,
        scratch_shapes=[
            pltpu.VMEM(field, BF),
            pltpu.VMEM(paired, BF),
            pltpu.VMEM(paired, BF),
            pltpu.VMEM(pad_shape, BF),
            pltpu.VMEM((12 * chans, 2 * chans), BF),
            columns,
            columns,
            pltpu.SemaphoreType.DMA((3, groups)),
        ],
        compiler_params=params(LIMIT),
        cost_estimate=cost(conv_flops, 8 << 20),
        name="conv",
    )(pos, smooth, above2, below2, got[0], got[-1], conv_weight, act.reshape(paired))
    output, mine = lax.optimization_barrier((output, mine))
    grad_coarse = pl.pallas_call(
        owner_kernel,
        out_shape=shape(coarse.shape, F32),
        in_specs=[VMEM] * (3 + n_gx),
        out_specs=VMEM,
        compiler_params=params(8),
        name="owner",
    )(mine, own, weight_pad, bias_col, *got)
    grad_conv, grad_weight, grad_bias = pl.pallas_call(
        finish_kernel,
        out_shape=(
            shape((9, chans, chans), F32),
            shape((variables, chans), F32),
            shape((1, chans), F32),
        ),
        in_specs=[VMEM],
        out_specs=(VMEM,) * 3,
        compiler_params=params(8),
        name="finish",
    )(total)
    return (
        output.reshape(field),
        grad_fine,
        grad_coarse,
        grad_weight,
        grad_bias.reshape(chans),
        grad_conv,
    )


def solution(mesh):
    placed = (
        P(("gy", "gx"), None, None),
        P(),
        P(),
        P(("gy", "gx"), None),
        P(("gy", "gx"), None),
        P(),
        P(),
        P(),
        P("gy", "gx", None),
        P(),
        P("gy", "gx", None),
    )
    return jax.shard_map(
        body,
        mesh=mesh,
        in_specs=placed,
        out_specs=(
            P("gy", "gx", None),
            P("gy", "gx", None),
            P(("gy", "gx"), None, None),
            P(),
            P(),
            P(),
        ),
        check_vma=False,
    )
```

time: 747 us -> 107 us (0.14)
  matrix products: 202 us -> 0 us
  local copies, waits for them, and re-layouts: 145 us -> 3.97 us
  loops' own time: 125 us -> 0 us
  blocking collectives: 83.4 us -> 0 us
  waiting for transfers between devices: 80.2 us -> 10 us
  other arithmetic: 52.5 us -> 0.12 us
  Pallas kernels: 0 us -> 34.7 us
  starting transfers between devices: 35.3 us -> 55.6 us
  between operations: 16.9 us -> 1.67 us
    dot_general x62 -> x0, matrix products: 202 us -> none  [the longest x16 88 us: add_slot(): return total + jnp.dot(matrix, block, preferred_element_type=jnp.float32)]
    another operation x2 -> x0, loops' own time: 125 us -> none  [the longest x1 62.3 us: body(): lax.fori_loop(0, slots, add_slot, jnp.zeros((cells, chans), jnp.float32))]
    psum x1 -> x0, blocking collectives: 68.4 us -> none  [body(): lax.psum((grad_conv, grad_weight, grad_bias), ('gy', 'gx'))]
    psum x1 -> x0, waiting for transfers between devices: 67.6 us -> none  [body(): lax.psum((grad_conv, grad_weight, grad_bias), ('gy', 'gx'))]
    slice x17 -> x5, local copies, waits for them, and re-layouts: 54 us -> 1.04 us  [the longest x1 1.03 us: body(): cotangent[:, 0]]
    dynamic_slice x64 -> x0, local copies, waits for them, and re-layouts: 37.4 us -> none  [the longest x16 9.41 us: add_slot(): which[slot]]
    pallas_call x0 -> x8, Pallas kernels: none -> 34.7 us  [the longest x1 14.8 us: body(): pl.pallas_call(main_kernel, out_shape=(shape(field), shape(field), shape(...]
    unnamed x53 -> x20, local copies, waits for them, and re-layouts: 27.8 us -> 2.81 us
  transfers between devices with their start and end apart: 14 -> 18, of which waited for: 2 -> 3; matrix products, arithmetic and copies ran while one was open for 36% -> 2% of each run, Pallas kernels for 0% -> 16%
where the time goes in v2:
time: 107 us; the launch traced here: 106 us
  starting transfers between devices  55.6 us (52%)
  Pallas kernels  34.7 us (32%)
  waiting for transfers between devices  10 us (9%)
  local copies, waits for them, and re-layouts  3.97 us (4%)
  between operations  1.67 us (2%)
    pallas_call x1, Pallas kernels, body(): pl.pallas_call(main_kernel, out_shape=(shape(field), shape(field), shape(...  14.8 us
    all_to_all x1, starting transfers between devices, body(): lax.all_to_all(shared.reshape(n_dev, PACK, chans), both, 0, 0, tiled=True)  13.6 us
    ppermute x7, starting transfers between devices, body(): lax.ppermute(part, 'gx', [(i, (i + k) % n_gx) for i in range(n_gx)])  10.3 us
    all_to_all x1, waiting for transfers between devices, body(): lax.all_to_all(shared.reshape(n_dev, PACK, chans), both, 0, 0, tiled=True)  8.76 us
    pallas_call x1, Pallas kernels, body(): pl.pallas_call(conv_kernel, out_shape=shape(paired), in_specs=[SMEM, HBM]...  7.54 us
    pallas_call x1, Pallas kernels, body(): pl.pallas_call(back_kernel, out_shape=shape(paired), in_specs=[HBM] + [VM...  7.07 us
    all_to_all x1, starting transfers between devices, body(): lax.all_to_all(spread, 'gx', 0, 0, tiled=True).reshape(rowblk * VP, chans)  5.53 us
    ppermute x1, starting transfers between devices, body(): from_above = lax.ppermute(to_below, 'gy', down)  5 us
  transfers between devices with their start and end apart: 18, of which 3 were waited for; matrix products, arithmetic and copies ran while one was open for 2% of the time, Pallas kernels for 16%

profile of v2, /device:TPU:1, one launch (start us, length us, event | category | flops | bytes accessed | tf_op | source)
XLA Modules:
  0.0 106.0 jit_solution(11120286220932024592)
XLA Ops:
  0.6 0.0 copy-start.7
  0.6 0.0 copy-start.6
  0.7 0.8 copy.17.coarse_ref
  1.4 0.0 copy-start
  1.4 0.7 copy-done
  2.1 0.0 copy-start.2
  2.1 0.7 copy-done.2
  2.8 1.6 %pack.1 = (bf16[160,128]{1,0:T(8,128)(2,1)S(1)}, bf16[8,160,128]{2,1,0:T(8,128)(2,1)}, bf16[144,128]{1,0:T(8,128)(2,1)S(1)}, bf16[144,128]{1,0:T(8,128)(2,1)S(1)}) custom-call(bf16[2,70,128]{2,1,0:T(8,128)(2,1)S(1)} %copy.17.coarse_ref, s32[1,16]{1,0:T(1,128)S(1)} %copy-done, s32[1,16]{1,0:T(1,128)S(1)} %copy-done.2, bf16[64,128,128]{2,1,0:T(8,128)(2,1)} %cot_hbm.5), custom_call_target="tpu_custom_call" | custom-call | tf_op jit(solution)/shard_map/pack/pallas_call | solution.py:512
  4.3 1.3 %collective-permute-start.3 = (bf16[144,128]{1,0:T(8,128)(2,1)S(1)}, bf16[144,128]{1,0:T(8,128)(2,1)S(1)}, u32[]{:S(2)}, u32[]{:S(2)}) collective-permute-start(bf16[144,128]{1,0:T(8,128)(2,1)S(1)} %get-tuple-element.33), channel_id=1, source_target_pairs={{8,0},{16,8},{24,16},{32,24},{40,32},{48,40},{56,48},{64,56},{72,6... | collective-permute-start | bytes 110600 | tf_op jit(solution)/shard_map/ppermute | solution.py:533
  5.6 5.0 %collective-permute-start.2 = (bf16[144,128]{1,0:T(8,128)(2,1)S(1)}, bf16[144,128]{1,0:T(8,128)(2,1)S(1)}, u32[]{:S(2)}, u32[]{:S(2)}) collective-permute-start(bf16[144,128]{1,0:T(8,128)(2,1)S(1)} %get-tuple-element.32), channel_id=1, source_target_pairs={{0,8},{8,16},{16,24},{24,32},{32,40},{40,48},{48,56},{56,64},{64,7... | collective-permute-start | bytes 110600 | tf_op jit(solution)/shard_map/ppermute | solution.py:532
  10.6 5.5 %all-to-all-start = ((bf16[8,160,128]{2,1,0:T(8,128)(2,1)}), bf16[8,160,128]{2,1,0:T(8,128)(2,1)S(1)}, u32[]{:S(2)}, u32[]{:S(2)}) async-start(bf16[8,160,128]{2,1,0:T(8,128)(2,1)} %get-tuple-element.31), calls=%async_computation | async-start | bytes 655360 | tf_op jit(solution)/shard_map/all_to_all | solution.py:531
  16.2 1.0 fusion
  17.2 0.0 collective-permute-done.3.below_ref
  17.3 0.0 collective-permute-done.2.above_ref
  17.3 3.5 %collective-permute-start.4 = (bf16[96,128]{1,0:T(8,128)(2,1)S(1)}, bf16[96,128]{1,0:T(8,128)(2,1)S(1)}, u32[]{:S(2)}, u32[]{:S(2)}) collective-permute-start(bf16[96,128]{1,0:T(8,128)(2,1)S(1)} %pad_maximum_fusion), channel_id=1, source_target_pairs={{0,1},{1,2},{2,3},{3,4},{4,5},{5,6},{6,7},{8,9},{9,10},{10,11},{11... | collective-permute-start | bytes 73736 | tf_op jit(solution)/shard_map/ppermute | solution.py:544
  20.9 1.9 %collective-permute-start.5 = (bf16[96,128]{1,0:T(8,128)(2,1)S(1)}, bf16[96,128]{1,0:T(8,128)(2,1)S(1)}, u32[]{:S(2)}, u32[]{:S(2)}) collective-permute-start(bf16[96,128]{1,0:T(8,128)(2,1)S(1)} %pad_maximum_fusion.1), channel_id=1, source_target_pairs={{1,0},{2,1},{3,2},{4,3},{5,4},{6,5},{7,6},{9,8},{10,9},{11,10},{12... | collective-permute-start | bytes 73736 | tf_op jit(solution)/shard_map/ppermute | solution.py:545
  22.8 0.5 all-to-all-done
  23.3 3.6 %collective-permute-start = (bf16[1280,128]{1,0:T(8,128)(2,1)S(1)}, bf16[1280,128]{1,0:T(8,128)(2,1)S(1)}, u32[]{:S(2)}, u32[]{:S(2)}) collective-permute-start(bf16[1280,128]{1,0:T(8,128)(2,1)S(1)} %bitcast.17), channel_id=1, source_target_pairs={{0,8},{8,16},{16,24},{24,32},{32,40},{40,48},{48,56},{56,64},{64,7... | collective-permute-start | bytes 983048 | tf_op jit(solution)/shard_map/ppermute | solution.py:546
  26.9 1.3 %collective-permute-start.1 = (bf16[1280,128]{1,0:T(8,128)(2,1)S(1)}, bf16[1280,128]{1,0:T(8,128)(2,1)S(1)}, u32[]{:S(2)}, u32[]{:S(2)}) collective-permute-start(bf16[1280,128]{1,0:T(8,128)(2,1)S(1)} %bitcast.18), channel_id=1, source_target_pairs={{8,0},{16,8},{24,16},{32,24},{40,32},{48,40},{56,48},{64,56},{72,6... | collective-permute-start | bytes 983048 | tf_op jit(solution)/shard_map/ppermute | solution.py:547
  28.2 0.1 pad_add_fusion.1.pos_ref
  28.2 0.0 copy-done.7
  28.2 0.1 copy.20.bias_col_ref
  29.0 0.0 copy-done.6
  29.0 0.0 copy-start.1
  29.0 0.0 copy-start.3
  29.1 0.0 copy-start.5
  29.1 0.0 collective-permute-done.4.left16_ref
  29.1 0.0 collective-permute-done.5.right16_ref
  29.1 0.0 copy-done.4
  29.1 7.1 %back.1 = bf16[32,2,128,128]{3,2,1,0:T(8,128)(2,1)} custom-call(bf16[64,128,128]{2,1,0:T(8,128)(2,1)} %cot_hbm.5, bf16[144,128]{1,0:T(8,128)(2,1)S(1)} %collective-permute-done.2.above_ref, bf16[144,128]{1,0:T(8,128)(2,1)S(1)} %collective-permute-done.3.below_ref, bf16[96,128]{1,0:T(8,128)(2,1)S(1)} %collective-permute-done.4.left16_ref, ...), custom_call_target="tpu_custom_call" | custom-call | flops 3221225472 | bytes 12582912 | tf_op jit(solution)/shard_map/back/pallas_call | solution.py:557
  36.2 0.0 collective-permute-done.band_above_ref
  36.2 0.7 collective-permute-done.1.band_below_ref
  36.9 0.0 copy-done.1
  36.9 0.0 copy-done.3
  36.9 0.0 copy-done.5
  36.9 14.8 %main.1 = (bf16[64,128,128]{2,1,0:T(8,128)(2,1)}, bf16[64,128,128]{2,1,0:T(8,128)(2,1)}, bf16[64,128,128]{2,1,0:T(8,128)(2,1)}, f32[2,64,128]{2,1,0:T(8,128)S(1)...) custom-call(s32[3]{0:T(128)S(1)} %pad_add_fusion.1.pos_ref, ...), custom_call_target="tpu_custom_call" | custom-call | flops 9663676416 | bytes 25165824 | tf_op jit(solution)/shard_map/main/pallas_call | solution.py:579
  51.7 13.6 %all-to-all-start.1 = ((bf16[128,16,128]{2,1,0:T(8,128)(2,1)}), bf16[128,16,128]{2,1,0:T(8,128)(2,1)S(1)}, u32[]{:S(2)}, u32[]{:S(2)}) async-start(bf16[128,16,128]{2,1,0:T(8,128)(2,1)} %bitcast.20), calls=%async_computation.1 | async-start | bytes 1048576 | tf_op jit(solution)/shard_map/all_to_all | solution.py:638
  65.3 3.4 %collective-permute-start.6 = (bf16[640,128]{1,0:T(8,128)(2,1)S(1)}, bf16[640,128]{1,0:T(8,128)(2,1)S(1)}, u32[]{:S(2)}, u32[]{:S(2)}) collective-permute-start(bf16[640,128]{1,0:T(8,128)(2,1)S(1)} %get-tuple-element.35), channel_id=1, source_target_pairs={{0,8},{8,16},{16,24},{24,32},{32,40},{40,48},{48,56},{56,64},{64,7... | collective-permute-start | bytes 491528 | tf_op jit(solution)/shard_map/ppermute | solution.py:641
  68.8 1.3 %collective-permute-start.7 = (bf16[640,128]{1,0:T(8,128)(2,1)S(1)}, bf16[640,128]{1,0:T(8,128)(2,1)S(1)}, u32[]{:S(2)}, u32[]{:S(2)}) collective-permute-start(bf16[640,128]{1,0:T(8,128)(2,1)S(1)} %get-tuple-element.36), channel_id=1, source_target_pairs={{8,0},{16,8},{24,16},{32,24},{40,32},{48,40},{56,48},{64,56},{72,6... | collective-permute-start | bytes 491528 | tf_op jit(solution)/shard_map/ppermute | solution.py:640
  70.1 8.8 %all-to-all-done.1.got_ref = bf16[128,16,128]{2,1,0:T(8,128)(2,1)S(1)} async-done(((bf16[128,16,128]{2,1,0:T(8,128)(2,1)}), bf16[128,16,128]{2,1,0:T(8,128)(2,1)S(1)}, u32[]{:S(2)}, u32[]{:S(2)}) %all-to-all-start.1) | async-done | bytes 524320 | tf_op jit(solution)/shard_map/all_to_all | solution.py:638
  78.8 1.0 total.1
  79.8 4.9 %all-to-all-start.2 = ((bf16[128,16,128]{2,1,0:T(8,128)(2,1)}), bf16[128,16,128]{2,1,0:T(8,128)(2,1)S(1)}, u32[]{:S(2)}, u32[]{:S(2)}) async-start(bf16[128,16,128]{2,1,0:T(8,128)(2,1)} %total.1), calls=%async_computation.2 | async-start | bytes 1048576 | tf_op jit(solution)/shard_map/all_to_all | solution.py:671
  84.7 0.0 collective-permute-done.6.above_ref
  84.7 0.0 collective-permute-done.7.below_ref
  84.7 1.5 %band.1 = (f32[2,128,128]{2,1,0:T(8,128)S(1)}, bf16[352,128]{1,0:T(8,128)(2,1)S(1)}, bf16[256,128]{1,0:T(8,128)(2,1)S(1)}, bf16[256,128]{1,0:T(8,128)(2,1)S(1)},...) custom-call(s32[3]{0:T(128)S(1)} %pad_add_fusion.1.pos_ref, ...), custom_call_target="tpu_custom_call" | custom-call | flops 4194304 | bytes 1048576 | tf_op jit(solution)/shard_map/band/pallas_call | solution.py:648
  86.2 1.6 %collective-permute-start.8 = (bf16[352,128]{1,0:T(8,128)(2,1)S(1)}, bf16[352,128]{1,0:T(8,128)(2,1)S(1)}, u32[]{:S(2)}, u32[]{:S(2)}) collective-permute-start(bf16[352,128]{1,0:T(8,128)(2,1)S(1)} %get-tuple-element.39), channel_id=1, source_target_pairs={{0,1},{1,2},{2,3},{3,4},{4,5},{5,6},{6,7},{7,0},{8,9},{9,10},{10,1... | collective-permute-start | bytes 270344 | tf_op jit(solution)/shard_map/ppermute | solution.py:659
  87.8 0.0 collective-permute-start.9
  87.8 1.2 %collective-permute-start.10 = (bf16[256,128]{1,0:T(8,128)(2,1)S(1)}, bf16[256,128]{1,0:T(8,128)(2,1)S(1)}, u32[]{:S(2)}, u32[]{:S(2)}) collective-permute-start(bf16[256,128]{1,0:T(8,128)(2,1)S(1)} %get-tuple-element.47), channel_id=1, source_target_pairs={{0,2},{1,3},{2,4},{3,5},{4,6},{5,7},{6,0},{7,1},{8,10},{9,11},{10,... | collective-permute-start | bytes 196616 | tf_op jit(solution)/shard_map/ppermute | solution.py:659
  89.0 3.3 %collective-permute-start.11 = (bf16[256,128]{1,0:T(8,128)(2,1)S(1)}, bf16[256,128]{1,0:T(8,128)(2,1)S(1)}, u32[]{:S(2)}, u32[]{:S(2)}) collective-permute-start(bf16[256,128]{1,0:T(8,128)(2,1)S(1)} %get-tuple-element.48), channel_id=1, source_target_pairs={{0,3},{1,4},{2,5},{3,6},{4,7},{5,0},{6,1},{7,2},{8,11},{9,12},{10,... | collective-permute-start | bytes 196616 | tf_op jit(solution)/shard_map/ppermute | solution.py:659
  92.3 0.8 collective-permute-start.12
  93.1 0.0 collective-permute-done.8.got_left_ref.refs_0_
  93.1 3.3 %collective-permute-start.13 = (bf16[256,128]{1,0:T(8,128)(2,1)S(1)}, bf16[256,128]{1,0:T(8,128)(2,1)S(1)}, u32[]{:S(2)}, u32[]{:S(2)}) collective-permute-start(bf16[256,128]{1,0:T(8,128)(2,1)S(1)} %get-tuple-element.50), channel_id=1, source_target_pairs={{0,5},{1,6},{2,7},{3,0},{4,1},{5,2},{6,3},{7,4},{8,13},{9,14},{10,... | collective-permute-start | bytes 196616 | tf_op jit(solution)/shard_map/ppermute | solution.py:659
  96.4 0.0 collective-permute-done.9.got_right_ref.refs_6_
  96.4 0.1 collective-permute-start.14
  96.5 7.5 %conv.1 = bf16[32,2,128,128]{3,2,1,0:T(8,128)(2,1)} custom-call(s32[3]{0:T(128)S(1)} %pad_add_fusion.1.pos_ref, bf16[64,128,128]{2,1,0:T(8,128)(2,1)} %get-tuple-element.34.smooth_hbm, bf16[640,128]{1,0:T(8,128)(2,1)S(1)} %collective-permute-done.6.above_ref, bf16[640,128]{1,0:T(8,128)(2,1)S(1)} %collective-permute-done.7.below_ref, ...), custom_call_target="tpu_custom_call" | custom-call | flops 3221225472 | bytes 8388608 | tf_op jit(solution)/shard_map/conv/pallas_call | solution.py:673
  104.0 0.0 collective-permute-done.10.refs_1_
  104.0 0.0 collective-permute-done.11.refs_2_
  104.0 0.0 collective-permute-done.12.refs_3_
  104.0 0.0 collective-permute-done.13.refs_4_
  104.1 0.0 collective-permute-done.14.refs_5_
  104.1 0.4 owner.1
  104.5 0.7 copy.22
  105.2 0.0 all-to-all-done.2
  105.2 0.9 finish.1
  (13 shorter events, 0.1 us)
Async XLA Ops:
  0.6 27.6 %copy-start.7 = (f32[128]{0:T(128)S(1)}, f32[128]{0:T(128)}, u32[]{:S(2)}) copy-start(f32[128]{0:T(128)} %param.13) | copy-start | bytes 1540
  0.6 28.4 %copy-start.6 = (bf16[70,128]{1,0:T(8,128)(2,1)S(1)}, bf16[70,128]{1,0:T(8,128)(2,1)}, u32[]{:S(2)}) copy-start(bf16[70,128]{1,0:T(8,128)(2,1)} %param.12) | copy-start | bytes 53764
  1.4 0.7 copy-start
  2.1 0.7 copy-start.2
  2.7 26.3 %copy-start.4 = (bf16[9,128,128]{2,1,0:T(8,128)(2,1)S(1)}, bf16[9,128,128]{2,1,0:T(8,128)(2,1)}, u32[]{:S(2)}) copy-start(bf16[9,128,128]{2,1,0:T(8,128)(2,1)} %w_ref.3) | copy-start | bytes 884740
  4.3 12.9 %collective-permute-start.3 = (bf16[144,128]{1,0:T(8,128)(2,1)S(1)}, bf16[144,128]{1,0:T(8,128)(2,1)S(1)}, u32[]{:S(2)}, u32[]{:S(2)}) collective-permute-start(bf16[144,128]{1,0:T(8,128)(2,1)S(1)} %get-tuple-element.33), channel_id=1, source_target_pairs={{8,0},{16,8},{24,16},{32,24},{40,32},{48,40},{56,48},{64,56},{72,6... | collective-permute-start | bytes 110600 | tf_op jit(solution)/shard_map/ppermute | solution.py:533
  5.6 11.6 %collective-permute-start.2 = (bf16[144,128]{1,0:T(8,128)(2,1)S(1)}, bf16[144,128]{1,0:T(8,128)(2,1)S(1)}, u32[]{:S(2)}, u32[]{:S(2)}) collective-permute-start(bf16[144,128]{1,0:T(8,128)(2,1)S(1)} %get-tuple-element.32), channel_id=1, source_target_pairs={{0,8},{8,16},{16,24},{24,32},{32,40},{40,48},{48,56},{56,64},{64,7... | collective-permute-start | bytes 110600 | tf_op jit(solution)/shard_map/ppermute | solution.py:532
  10.6 12.6 %all-to-all-start = ((bf16[8,160,128]{2,1,0:T(8,128)(2,1)}), bf16[8,160,128]{2,1,0:T(8,128)(2,1)S(1)}, u32[]{:S(2)}, u32[]{:S(2)}) async-start(bf16[8,160,128]{2,1,0:T(8,128)(2,1)} %get-tuple-element.31), calls=%async_computation | async-start | bytes 655360 | tf_op jit(solution)/shard_map/all_to_all | solution.py:531
  17.3 11.8 %collective-permute-start.4 = (bf16[96,128]{1,0:T(8,128)(2,1)S(1)}, bf16[96,128]{1,0:T(8,128)(2,1)S(1)}, u32[]{:S(2)}, u32[]{:S(2)}) collective-permute-start(bf16[96,128]{1,0:T(8,128)(2,1)S(1)} %pad_maximum_fusion), channel_id=1, source_target_pairs={{0,1},{1,2},{2,3},{3,4},{4,5},{5,6},{6,7},{8,9},{9,10},{10,11},{11... | collective-permute-start | bytes 73736 | tf_op jit(solution)/shard_map/ppermute | solution.py:544
  20.9 8.2 %collective-permute-start.5 = (bf16[96,128]{1,0:T(8,128)(2,1)S(1)}, bf16[96,128]{1,0:T(8,128)(2,1)S(1)}, u32[]{:S(2)}, u32[]{:S(2)}) collective-permute-start(bf16[96,128]{1,0:T(8,128)(2,1)S(1)} %pad_maximum_fusion.1), channel_id=1, source_target_pairs={{1,0},{2,1},{3,2},{4,3},{5,4},{6,5},{7,6},{9,8},{10,9},{11,10},{12... | collective-permute-start | bytes 73736 | tf_op jit(solution)/shard_map/ppermute | solution.py:545
  23.3 12.9 %collective-permute-start = (bf16[1280,128]{1,0:T(8,128)(2,1)S(1)}, bf16[1280,128]{1,0:T(8,128)(2,1)S(1)}, u32[]{:S(2)}, u32[]{:S(2)}) collective-permute-start(bf16[1280,128]{1,0:T(8,128)(2,1)S(1)} %bitcast.17), channel_id=1, source_target_pairs={{0,8},{8,16},{16,24},{24,32},{32,40},{40,48},{48,56},{56,64},{64,7... | collective-permute-start | bytes 983048 | tf_op jit(solution)/shard_map/ppermute | solution.py:546
  26.9 10.0 %collective-permute-start.1 = (bf16[1280,128]{1,0:T(8,128)(2,1)S(1)}, bf16[1280,128]{1,0:T(8,128)(2,1)S(1)}, u32[]{:S(2)}, u32[]{:S(2)}) collective-permute-start(bf16[1280,128]{1,0:T(8,128)(2,1)S(1)} %bitcast.18), channel_id=1, source_target_pairs={{8,0},{16,8},{24,16},{32,24},{40,32},{48,40},{56,48},{64,56},{72,6... | collective-permute-start | bytes 983048 | tf_op jit(solution)/shard_map/ppermute | solution.py:547
  29.0 7.9 %copy-start.1 = (s32[1,16]{1,0:T(1,128)S(1)}, s32[1,16]{1,0:T(1,128)}, u32[]{:S(2)}) copy-start(s32[1,16]{1,0:T(1,128)} %ids_ref.1) | copy-start | bytes 196
  29.0 7.8 %copy-start.3 = (s32[1,16]{1,0:T(1,128)S(1)}, s32[1,16]{1,0:T(1,128)}, u32[]{:S(2)}) copy-start(s32[1,16]{1,0:T(1,128)} %which_ref.1) | copy-start | bytes 196
  29.1 7.8 %copy-start.5 = (f32[64,128]{1,0:T(8,128)S(1)}, f32[64,128]{1,0:T(8,128)}, u32[]{:S(2)}) copy-start(f32[64,128]{1,0:T(8,128)} %noise_ref.1) | copy-start | bytes 98308
  51.7 27.1 %all-to-all-start.1 = ((bf16[128,16,128]{2,1,0:T(8,128)(2,1)}), bf16[128,16,128]{2,1,0:T(8,128)(2,1)S(1)}, u32[]{:S(2)}, u32[]{:S(2)}) async-start(bf16[128,16,128]{2,1,0:T(8,128)(2,1)} %bitcast.20), calls=%async_computation.1 | async-start | bytes 1048576 | tf_op jit(solution)/shard_map/all_to_all | solution.py:638
  65.3 19.4 %collective-permute-start.6 = (bf16[640,128]{1,0:T(8,128)(2,1)S(1)}, bf16[640,128]{1,0:T(8,128)(2,1)S(1)}, u32[]{:S(2)}, u32[]{:S(2)}) collective-permute-start(bf16[640,128]{1,0:T(8,128)(2,1)S(1)} %get-tuple-element.35), channel_id=1, source_target_pairs={{0,8},{8,16},{16,24},{24,32},{32,40},{40,48},{48,56},{56,64},{64,7... | collective-permute-start | bytes 491528 | tf_op jit(solution)/shard_map/ppermute | solution.py:641
  68.8 15.9 %collective-permute-start.7 = (bf16[640,128]{1,0:T(8,128)(2,1)S(1)}, bf16[640,128]{1,0:T(8,128)(2,1)S(1)}, u32[]{:S(2)}, u32[]{:S(2)}) collective-permute-start(bf16[640,128]{1,0:T(8,128)(2,1)S(1)} %get-tuple-element.36), channel_id=1, source_target_pairs={{8,0},{16,8},{24,16},{32,24},{40,32},{48,40},{56,48},{64,56},{72,6... | collective-permute-start | bytes 491528 | tf_op jit(solution)/shard_map/ppermute | solution.py:640
  79.8 25.4 %all-to-all-start.2 = ((bf16[128,16,128]{2,1,0:T(8,128)(2,1)}), bf16[128,16,128]{2,1,0:T(8,128)(2,1)S(1)}, u32[]{:S(2)}, u32[]{:S(2)}) async-start(bf16[128,16,128]{2,1,0:T(8,128)(2,1)} %total.1), calls=%async_computation.2 | async-start | bytes 1048576 | tf_op jit(solution)/shard_map/all_to_all | solution.py:671
  86.2 6.9 %collective-permute-start.8 = (bf16[352,128]{1,0:T(8,128)(2,1)S(1)}, bf16[352,128]{1,0:T(8,128)(2,1)S(1)}, u32[]{:S(2)}, u32[]{:S(2)}) collective-permute-start(bf16[352,128]{1,0:T(8,128)(2,1)S(1)} %get-tuple-element.39), channel_id=1, source_target_pairs={{0,1},{1,2},{2,3},{3,4},{4,5},{5,6},{6,7},{7,0},{8,9},{9,10},{10,1... | collective-permute-start | bytes 270344 | tf_op jit(solution)/shard_map/ppermute | solution.py:659
  87.8 8.6 %collective-permute-start.9 = (bf16[352,128]{1,0:T(8,128)(2,1)S(1)}, bf16[352,128]{1,0:T(8,128)(2,1)S(1)}, u32[]{:S(2)}, u32[]{:S(2)}) collective-permute-start(bf16[352,128]{1,0:T(8,128)(2,1)S(1)} %get-tuple-element.40), channel_id=1, source_target_pairs={{0,7},{1,0},{2,1},{3,2},{4,3},{5,4},{6,5},{7,6},{8,15},{9,8},{10,9... | collective-permute-start | bytes 270344 | tf_op jit(solution)/shard_map/ppermute | solution.py:659
  87.8 16.2 %collective-permute-start.10 = (bf16[256,128]{1,0:T(8,128)(2,1)S(1)}, bf16[256,128]{1,0:T(8,128)(2,1)S(1)}, u32[]{:S(2)}, u32[]{:S(2)}) collective-permute-start(bf16[256,128]{1,0:T(8,128)(2,1)S(1)} %get-tuple-element.47), channel_id=1, source_target_pairs={{0,2},{1,3},{2,4},{3,5},{4,6},{5,7},{6,0},{7,1},{8,10},{9,11},{10,... | collective-permute-start | bytes 196616 | tf_op jit(solution)/shard_map/ppermute | solution.py:659
  89.0 15.0 %collective-permute-start.11 = (bf16[256,128]{1,0:T(8,128)(2,1)S(1)}, bf16[256,128]{1,0:T(8,128)(2,1)S(1)}, u32[]{:S(2)}, u32[]{:S(2)}) collective-permute-start(bf16[256,128]{1,0:T(8,128)(2,1)S(1)} %get-tuple-element.48), channel_id=1, source_target_pairs={{0,3},{1,4},{2,5},{3,6},{4,7},{5,0},{6,1},{7,2},{8,11},{9,12},{10,... | collective-permute-start | bytes 196616 | tf_op jit(solution)/shard_map/ppermute | solution.py:659
  92.3 11.7 %collective-permute-start.12 = (bf16[256,128]{1,0:T(8,128)(2,1)S(1)}, bf16[256,128]{1,0:T(8,128)(2,1)S(1)}, u32[]{:S(2)}, u32[]{:S(2)}) collective-permute-start(bf16[256,128]{1,0:T(8,128)(2,1)S(1)} %get-tuple-element.49), channel_id=1, source_target_pairs={{0,4},{1,5},{2,6},{3,7},{4,0},{5,1},{6,2},{7,3},{8,12},{9,13},{10,... | collective-permute-start | bytes 196616 | tf_op jit(solution)/shard_map/ppermute | solution.py:659
  93.1 11.0 %collective-permute-start.13 = (bf16[256,128]{1,0:T(8,128)(2,1)S(1)}, bf16[256,128]{1,0:T(8,128)(2,1)S(1)}, u32[]{:S(2)}, u32[]{:S(2)}) collective-permute-start(bf16[256,128]{1,0:T(8,128)(2,1)S(1)} %get-tuple-element.50), channel_id=1, source_target_pairs={{0,5},{1,6},{2,7},{3,0},{4,1},{5,2},{6,3},{7,4},{8,13},{9,14},{10,... | collective-permute-start | bytes 196616 | tf_op jit(solution)/shard_map/ppermute | solution.py:659
  96.4 7.7 %collective-permute-start.14 = (bf16[256,128]{1,0:T(8,128)(2,1)S(1)}, bf16[256,128]{1,0:T(8,128)(2,1)S(1)}, u32[]{:S(2)}, u32[]{:S(2)}) collective-permute-start(bf16[256,128]{1,0:T(8,128)(2,1)S(1)} %get-tuple-element.51), channel_id=1, source_target_pairs={{0,6},{1,7},{2,0},{3,1},{4,2},{5,3},{6,4},{7,5},{8,14},{9,15},{10,... | collective-permute-start | bytes 196616 | tf_op jit(solution)/shard_map/ppermute | solution.py:659

commit v3 on v2

--- a/solution.py
+++ b/solution.py
@@ -296,10 +296,7 @@
 
     lax.fori_loop(0, slots // group, encode, 0)
     for w in range(mats):
-        high = enc_ref[w].astype(BF)
-        low = (enc_ref[w] - high.astype(F32)).astype(BF)
-        enc16_ref[:chans, w * cells : (w + 1) * cells] = high
-        enc16_ref[chans:, w * cells : (w + 1) * cells] = low
+        enc16_ref[:, w * cells : (w + 1) * cells] = enc_ref[w].astype(BF)
     embed = noise_ref[pl.ds(noise_index_ref[0], 1), :]
     fill_columns(
         left16_ref[...], right16_ref[...], above_ref, below_ref, left_ref, right_ref, pad_ref
@@ -310,8 +307,7 @@
         at = pl.ds(step * rows, rows)
         flat = pl.ds(pl.multiple_of(step * rows * cells, rows * cells), rows * cells)
         table = jnp.concatenate([table_ref[w, flat, :] for w in range(mats)], axis=1)
-        both = mm_t(table, enc16_ref[...])
-        lifted = both[:, :chans] + both[:, chans:]
+        lifted = mm_t(table, enc16_ref[...])
         fine = fine_ref[at].reshape(rows * cells, chans).astype(F32)
         act = fine + lifted + embed
         sig = sigmoid(act)
@@ -333,10 +329,11 @@
             flip_ref[(r % 2) * chans : (r % 2 + 1) * chans, lanes] = smooth16[r].T
         put_pairs(cot_ref, step * (rows // 2), rows // 2, left_ref, right_ref, pad_ref)
         terms_acc[...] += mm(gfine.T, table)
+        return 0
+
+    lax.fori_loop(0, steps, chunk, 0)
+    for step in range(steps):
         start_all(sends(step))
-        return 0
-
-    lax.fori_loop(0, steps, chunk, 0)
 
     size = mats * chans
     for w in range(mats):
@@ -347,7 +344,7 @@
     down_ref[size:, :] = smooth_ref[total_rows - 1]
     up_ref[size:, :] = smooth_ref[0]
 
-    def conv_grad(d, _):
+    def conv_grad(d):
         found = []
         for h in range(2):
             rhs = pad_ref[d, h : h + pairs].reshape(pairs * cells, 2 * chans)
@@ -358,11 +355,11 @@
                 rho = o + 2 - dy
                 lanes = slice(rho % 2 * chans, (rho % 2 + 1) * chans)
                 total = total + found[rho // 2][o * chans : (o + 1) * chans, lanes]
-            tap = pl.multiple_of((3 * dy + 2 - d) * chans, chans)
+            tap = (3 * dy + 2 - d) * chans
             shared_ref[pl.ds(tap, chans), :] = total.astype(BF)
-        return 0
-
-    lax.fori_loop(0, 3, conv_grad, 0)
+
+    for d in range(3):
+        conv_grad(d)
 
     def slot_grad(slot, gsum):
         lanes = pl.ds(pl.multiple_of(slot * cells, cells), cells)
@@ -603,7 +600,7 @@
             pltpu.VMEM((chans, slots * chans), F32),
             pltpu.VMEM((chans, slots * chans), BF),
             pltpu.VMEM((mats, chans, chans), F32),
-            pltpu.VMEM((2 * chans, mats * chans), BF),
+            pltpu.VMEM((chans, mats * chans), BF),
             pltpu.VMEM((chans, mats * chans), F32),
             pltpu.VMEM((2 * chans, pairs * cells), BF),
             columns,

time: 107 us -> 105 us (0.981)
  Pallas kernels: 34.7 us -> 33.2 us
    pallas_call x1, Pallas kernels: 14.8 us -> 13.2 us  [body(): pl.pallas_call(main_kernel, out_shape=(shape(field), shape(field), shape(...]
  transfers between devices with their start and end apart: 18 -> 18, of which waited for: 3 -> 3; matrix products, arithmetic and copies ran while one was open for 2% -> 2% of each run, Pallas kernels for 16% -> 17%
where the time goes in v3:
time: 105 us; the launch traced here: 104 us
  starting transfers between devices  55.5 us (53%)
  Pallas kernels  33.2 us (32%)
  waiting for transfers between devices  10 us (10%)
  local copies, waits for them, and re-layouts  3.97 us (4%)
  between operations  1.68 us (2%)
    all_to_all x1, starting transfers between devices, body(): lax.all_to_all(shared.reshape(n_dev, PACK, chans), both, 0, 0, tiled=True)  13.6 us
    pallas_call x1, Pallas kernels, body(): pl.pallas_call(main_kernel, out_shape=(shape(field), shape(field), shape(...  13.2 us
    ppermute x7, starting transfers between devices, body(): lax.ppermute(part, 'gx', [(i, (i + k) % n_gx) for i in range(n_gx)])  10.2 us
    all_to_all x1, waiting for transfers between devices, body(): lax.all_to_all(shared.reshape(n_dev, PACK, chans), both, 0, 0, tiled=True)  8.76 us
    pallas_call x1, Pallas kernels, body(): pl.pallas_call(conv_kernel, out_shape=shape(paired), in_specs=[SMEM, HBM]...  7.54 us
    pallas_call x1, Pallas kernels, body(): pl.pallas_call(back_kernel, out_shape=shape(paired), in_specs=[HBM] + [VM...  7.07 us
    all_to_all x1, starting transfers between devices, body(): lax.all_to_all(spread, 'gx', 0, 0, tiled=True).reshape(rowblk * VP, chans)  5.53 us
    ppermute x1, starting transfers between devices, body(): from_above = lax.ppermute(to_below, 'gy', down)  5 us
  transfers between devices with their start and end apart: 18, of which 3 were waited for; matrix products, arithmetic and copies ran while one was open for 2% of the time, Pallas kernels for 17%

profile of v3, /device:TPU:1, one launch (start us, length us, event | category | flops | bytes accessed | tf_op | source)
XLA Modules:
  0.0 104.4 jit_solution(16687922142690009662)
XLA Ops:
  0.6 0.0 copy-start.7
  0.6 0.0 copy-start.6
  0.7 0.8 copy.17.coarse_ref
  1.4 0.0 copy-start
  1.4 0.7 copy-done
  2.1 0.0 copy-start.2
  2.1 0.7 copy-done.2
  2.8 1.6 %pack.1 = (bf16[160,128]{1,0:T(8,128)(2,1)S(1)}, bf16[8,160,128]{2,1,0:T(8,128)(2,1)}, bf16[144,128]{1,0:T(8,128)(2,1)S(1)}, bf16[144,128]{1,0:T(8,128)(2,1)S(1)}) custom-call(bf16[2,70,128]{2,1,0:T(8,128)(2,1)S(1)} %copy.17.coarse_ref, s32[1,16]{1,0:T(1,128)S(1)} %copy-done, s32[1,16]{1,0:T(1,128)S(1)} %copy-done.2, bf16[64,128,128]{2,1,0:T(8,128)(2,1)} %cot_hbm.5), custom_call_target="tpu_custom_call" | custom-call | tf_op jit(solution)/shard_map/pack/pallas_call | solution.py:509
  4.3 1.3 %collective-permute-start.3 = (bf16[144,128]{1,0:T(8,128)(2,1)S(1)}, bf16[144,128]{1,0:T(8,128)(2,1)S(1)}, u32[]{:S(2)}, u32[]{:S(2)}) collective-permute-start(bf16[144,128]{1,0:T(8,128)(2,1)S(1)} %get-tuple-element.33), channel_id=1, source_target_pairs={{8,0},{16,8},{24,16},{32,24},{40,32},{48,40},{56,48},{64,56},{72,6... | collective-permute-start | bytes 110600 | tf_op jit(solution)/shard_map/ppermute | solution.py:530
  5.6 5.0 %collective-permute-start.2 = (bf16[144,128]{1,0:T(8,128)(2,1)S(1)}, bf16[144,128]{1,0:T(8,128)(2,1)S(1)}, u32[]{:S(2)}, u32[]{:S(2)}) collective-permute-start(bf16[144,128]{1,0:T(8,128)(2,1)S(1)} %get-tuple-element.32), channel_id=1, source_target_pairs={{0,8},{8,16},{16,24},{24,32},{32,40},{40,48},{48,56},{56,64},{64,7... | collective-permute-start | bytes 110600 | tf_op jit(solution)/shard_map/ppermute | solution.py:529
  10.6 5.5 %all-to-all-start = ((bf16[8,160,128]{2,1,0:T(8,128)(2,1)}), bf16[8,160,128]{2,1,0:T(8,128)(2,1)S(1)}, u32[]{:S(2)}, u32[]{:S(2)}) async-start(bf16[8,160,128]{2,1,0:T(8,128)(2,1)} %get-tuple-element.31), calls=%async_computation | async-start | bytes 655360 | tf_op jit(solution)/shard_map/all_to_all | solution.py:528
  16.2 1.0 fusion
  17.2 0.0 collective-permute-done.3.below_ref
  17.3 0.0 collective-permute-done.2.above_ref
  17.3 3.5 %collective-permute-start.4 = (bf16[96,128]{1,0:T(8,128)(2,1)S(1)}, bf16[96,128]{1,0:T(8,128)(2,1)S(1)}, u32[]{:S(2)}, u32[]{:S(2)}) collective-permute-start(bf16[96,128]{1,0:T(8,128)(2,1)S(1)} %pad_maximum_fusion), channel_id=1, source_target_pairs={{0,1},{1,2},{2,3},{3,4},{4,5},{5,6},{6,7},{8,9},{9,10},{10,11},{11... | collective-permute-start | bytes 73736 | tf_op jit(solution)/shard_map/ppermute | solution.py:541
  20.9 1.9 %collective-permute-start.5 = (bf16[96,128]{1,0:T(8,128)(2,1)S(1)}, bf16[96,128]{1,0:T(8,128)(2,1)S(1)}, u32[]{:S(2)}, u32[]{:S(2)}) collective-permute-start(bf16[96,128]{1,0:T(8,128)(2,1)S(1)} %pad_maximum_fusion.1), channel_id=1, source_target_pairs={{1,0},{2,1},{3,2},{4,3},{5,4},{6,5},{7,6},{9,8},{10,9},{11,10},{12... | collective-permute-start | bytes 73736 | tf_op jit(solution)/shard_map/ppermute | solution.py:542
  22.8 0.5 all-to-all-done
  23.3 3.6 %collective-permute-start = (bf16[1280,128]{1,0:T(8,128)(2,1)S(1)}, bf16[1280,128]{1,0:T(8,128)(2,1)S(1)}, u32[]{:S(2)}, u32[]{:S(2)}) collective-permute-start(bf16[1280,128]{1,0:T(8,128)(2,1)S(1)} %bitcast.17), channel_id=1, source_target_pairs={{0,8},{8,16},{16,24},{24,32},{32,40},{40,48},{48,56},{56,64},{64,7... | collective-permute-start | bytes 983048 | tf_op jit(solution)/shard_map/ppermute | solution.py:543
  26.9 1.3 %collective-permute-start.1 = (bf16[1280,128]{1,0:T(8,128)(2,1)S(1)}, bf16[1280,128]{1,0:T(8,128)(2,1)S(1)}, u32[]{:S(2)}, u32[]{:S(2)}) collective-permute-start(bf16[1280,128]{1,0:T(8,128)(2,1)S(1)} %bitcast.18), channel_id=1, source_target_pairs={{8,0},{16,8},{24,16},{32,24},{40,32},{48,40},{56,48},{64,56},{72,6... | collective-permute-start | bytes 983048 | tf_op jit(solution)/shard_map/ppermute | solution.py:544
  28.2 0.1 pad_add_fusion.1.pos_ref
  28.2 0.0 copy-done.7
  28.2 0.1 copy.20.bias_col_ref
  29.0 0.0 copy-done.6
  29.0 0.0 copy-start.1
  29.0 0.0 copy-start.3
  29.1 0.0 copy-start.5
  29.1 0.0 collective-permute-done.4.left16_ref
  29.1 0.0 collective-permute-done.5.right16_ref
  29.1 0.0 copy-done.4
  29.1 7.1 %back.1 = bf16[32,2,128,128]{3,2,1,0:T(8,128)(2,1)} custom-call(bf16[64,128,128]{2,1,0:T(8,128)(2,1)} %cot_hbm.5, bf16[144,128]{1,0:T(8,128)(2,1)S(1)} %collective-permute-done.2.above_ref, bf16[144,128]{1,0:T(8,128)(2,1)S(1)} %collective-permute-done.3.below_ref, bf16[96,128]{1,0:T(8,128)(2,1)S(1)} %collective-permute-done.4.left16_ref, ...), custom_call_target="tpu_custom_call" | custom-call | flops 3221225472 | bytes 12582912 | tf_op jit(solution)/shard_map/back/pallas_call | solution.py:554
  36.2 0.0 collective-permute-done.band_above_ref
  36.2 0.7 collective-permute-done.1.band_below_ref
  36.9 0.0 copy-done.1
  36.9 0.0 copy-done.3
  36.9 0.0 copy-done.5
  36.9 13.2 %main.1 = (bf16[64,128,128]{2,1,0:T(8,128)(2,1)}, bf16[64,128,128]{2,1,0:T(8,128)(2,1)}, bf16[64,128,128]{2,1,0:T(8,128)(2,1)}, f32[2,64,128]{2,1,0:T(8,128)S(1)...) custom-call(s32[3]{0:T(128)S(1)} %pad_add_fusion.1.pos_ref, ...), custom_call_target="tpu_custom_call" | custom-call | flops 9663676416 | bytes 25165824 | tf_op jit(solution)/shard_map/main/pallas_call | solution.py:576
  50.1 13.6 %all-to-all-start.1 = ((bf16[128,16,128]{2,1,0:T(8,128)(2,1)}), bf16[128,16,128]{2,1,0:T(8,128)(2,1)S(1)}, u32[]{:S(2)}, u32[]{:S(2)}) async-start(bf16[128,16,128]{2,1,0:T(8,128)(2,1)} %bitcast.20), calls=%async_computation.1 | async-start | bytes 1048576 | tf_op jit(solution)/shard_map/all_to_all | solution.py:635
  63.8 3.4 %collective-permute-start.6 = (bf16[640,128]{1,0:T(8,128)(2,1)S(1)}, bf16[640,128]{1,0:T(8,128)(2,1)S(1)}, u32[]{:S(2)}, u32[]{:S(2)}) collective-permute-start(bf16[640,128]{1,0:T(8,128)(2,1)S(1)} %get-tuple-element.35), channel_id=1, source_target_pairs={{0,8},{8,16},{16,24},{24,32},{32,40},{40,48},{48,56},{56,64},{64,7... | collective-permute-start | bytes 491528 | tf_op jit(solution)/shard_map/ppermute | solution.py:638
  67.2 1.3 %collective-permute-start.7 = (bf16[640,128]{1,0:T(8,128)(2,1)S(1)}, bf16[640,128]{1,0:T(8,128)(2,1)S(1)}, u32[]{:S(2)}, u32[]{:S(2)}) collective-permute-start(bf16[640,128]{1,0:T(8,128)(2,1)S(1)} %get-tuple-element.36), channel_id=1, source_target_pairs={{8,0},{16,8},{24,16},{32,24},{40,32},{48,40},{56,48},{64,56},{72,6... | collective-permute-start | bytes 491528 | tf_op jit(solution)/shard_map/ppermute | solution.py:637
  68.5 8.8 %all-to-all-done.1.got_ref = bf16[128,16,128]{2,1,0:T(8,128)(2,1)S(1)} async-done(((bf16[128,16,128]{2,1,0:T(8,128)(2,1)}), bf16[128,16,128]{2,1,0:T(8,128)(2,1)S(1)}, u32[]{:S(2)}, u32[]{:S(2)}) %all-to-all-start.1) | async-done | bytes 524320 | tf_op jit(solution)/shard_map/all_to_all | solution.py:635
  77.2 1.0 total.1
  78.2 4.9 %all-to-all-start.2 = ((bf16[128,16,128]{2,1,0:T(8,128)(2,1)}), bf16[128,16,128]{2,1,0:T(8,128)(2,1)S(1)}, u32[]{:S(2)}, u32[]{:S(2)}) async-start(bf16[128,16,128]{2,1,0:T(8,128)(2,1)} %total.1), calls=%async_computation.2 | async-start | bytes 1048576 | tf_op jit(solution)/shard_map/all_to_all | solution.py:668
  83.1 0.0 collective-permute-done.6.above_ref
  83.1 0.0 collective-permute-done.7.below_ref
  83.1 1.5 %band.1 = (f32[2,128,128]{2,1,0:T(8,128)S(1)}, bf16[352,128]{1,0:T(8,128)(2,1)S(1)}, bf16[256,128]{1,0:T(8,128)(2,1)S(1)}, bf16[256,128]{1,0:T(8,128)(2,1)S(1)},...) custom-call(s32[3]{0:T(128)S(1)} %pad_add_fusion.1.pos_ref, ...), custom_call_target="tpu_custom_call" | custom-call | flops 4194304 | bytes 1048576 | tf_op jit(solution)/shard_map/band/pallas_call | solution.py:645
  84.6 1.6 %collective-permute-start.8 = (bf16[352,128]{1,0:T(8,128)(2,1)S(1)}, bf16[352,128]{1,0:T(8,128)(2,1)S(1)}, u32[]{:S(2)}, u32[]{:S(2)}) collective-permute-start(bf16[352,128]{1,0:T(8,128)(2,1)S(1)} %get-tuple-element.39), channel_id=1, source_target_pairs={{0,1},{1,2},{2,3},{3,4},{4,5},{5,6},{6,7},{7,0},{8,9},{9,10},{10,1... | collective-permute-start | bytes 270344 | tf_op jit(solution)/shard_map/ppermute | solution.py:656
  86.3 0.0 collective-permute-start.9
  86.3 1.1 %collective-permute-start.10 = (bf16[256,128]{1,0:T(8,128)(2,1)S(1)}, bf16[256,128]{1,0:T(8,128)(2,1)S(1)}, u32[]{:S(2)}, u32[]{:S(2)}) collective-permute-start(bf16[256,128]{1,0:T(8,128)(2,1)S(1)} %get-tuple-element.47), channel_id=1, source_target_pairs={{0,2},{1,3},{2,4},{3,5},{4,6},{5,7},{6,0},{7,1},{8,10},{9,11},{10,... | collective-permute-start | bytes 196616 | tf_op jit(solution)/shard_map/ppermute | solution.py:656
  87.4 3.3 %collective-permute-start.11 = (bf16[256,128]{1,0:T(8,128)(2,1)S(1)}, bf16[256,128]{1,0:T(8,128)(2,1)S(1)}, u32[]{:S(2)}, u32[]{:S(2)}) collective-permute-start(bf16[256,128]{1,0:T(8,128)(2,1)S(1)} %get-tuple-element.48), channel_id=1, source_target_pairs={{0,3},{1,4},{2,5},{3,6},{4,7},{5,0},{6,1},{7,2},{8,11},{9,12},{10,... | collective-permute-start | bytes 196616 | tf_op jit(solution)/shard_map/ppermute | solution.py:656
  90.7 0.8 collective-permute-start.12
  91.5 0.0 collective-permute-done.8.got_left_ref.refs_0_
  91.5 3.3 %collective-permute-start.13 = (bf16[256,128]{1,0:T(8,128)(2,1)S(1)}, bf16[256,128]{1,0:T(8,128)(2,1)S(1)}, u32[]{:S(2)}, u32[]{:S(2)}) collective-permute-start(bf16[256,128]{1,0:T(8,128)(2,1)S(1)} %get-tuple-element.50), channel_id=1, source_target_pairs={{0,5},{1,6},{2,7},{3,0},{4,1},{5,2},{6,3},{7,4},{8,13},{9,14},{10,... | collective-permute-start | bytes 196616 | tf_op jit(solution)/shard_map/ppermute | solution.py:656
  94.8 0.0 collective-permute-done.9.got_right_ref.refs_6_
  94.8 0.1 collective-permute-start.14
  94.9 7.5 %conv.1 = bf16[32,2,128,128]{3,2,1,0:T(8,128)(2,1)} custom-call(s32[3]{0:T(128)S(1)} %pad_add_fusion.1.pos_ref, bf16[64,128,128]{2,1,0:T(8,128)(2,1)} %get-tuple-element.34.smooth_hbm, bf16[640,128]{1,0:T(8,128)(2,1)S(1)} %collective-permute-done.6.above_ref, bf16[640,128]{1,0:T(8,128)(2,1)S(1)} %collective-permute-done.7.below_ref, ...), custom_call_target="tpu_custom_call" | custom-call | flops 3221225472 | bytes 8388608 | tf_op jit(solution)/shard_map/conv/pallas_call | solution.py:670
  102.4 0.0 collective-permute-done.10.refs_1_
  102.4 0.0 collective-permute-done.11.refs_2_
  102.5 0.0 collective-permute-done.12.refs_3_
  102.5 0.0 collective-permute-done.13.refs_4_
  102.5 0.0 collective-permute-done.14.refs_5_
  102.5 0.4 owner.1
  102.9 0.7 copy.22
  103.6 0.0 all-to-all-done.2
  103.6 0.9 finish.1
  (13 shorter events, 0.1 us)
Async XLA Ops:
  0.6 27.6 %copy-start.7 = (f32[128]{0:T(128)S(1)}, f32[128]{0:T(128)}, u32[]{:S(2)}) copy-start(f32[128]{0:T(128)} %param.13) | copy-start | bytes 1540
  0.6 28.4 %copy-start.6 = (bf16[70,128]{1,0:T(8,128)(2,1)S(1)}, bf16[70,128]{1,0:T(8,128)(2,1)}, u32[]{:S(2)}) copy-start(bf16[70,128]{1,0:T(8,128)(2,1)} %param.12) | copy-start | bytes 53764
  1.4 0.7 copy-start
  2.1 0.7 copy-start.2
  2.7 26.3 %copy-start.4 = (bf16[9,128,128]{2,1,0:T(8,128)(2,1)S(1)}, bf16[9,128,128]{2,1,0:T(8,128)(2,1)}, u32[]{:S(2)}) copy-start(bf16[9,128,128]{2,1,0:T(8,128)(2,1)} %w_ref.3) | copy-start | bytes 884740
  4.3 12.9 %collective-permute-start.3 = (bf16[144,128]{1,0:T(8,128)(2,1)S(1)}, bf16[144,128]{1,0:T(8,128)(2,1)S(1)}, u32[]{:S(2)}, u32[]{:S(2)}) collective-permute-start(bf16[144,128]{1,0:T(8,128)(2,1)S(1)} %get-tuple-element.33), channel_id=1, source_target_pairs={{8,0},{16,8},{24,16},{32,24},{40,32},{48,40},{56,48},{64,56},{72,6... | collective-permute-start | bytes 110600 | tf_op jit(solution)/shard_map/ppermute | solution.py:530
  5.6 11.6 %collective-permute-start.2 = (bf16[144,128]{1,0:T(8,128)(2,1)S(1)}, bf16[144,128]{1,0:T(8,128)(2,1)S(1)}, u32[]{:S(2)}, u32[]{:S(2)}) collective-permute-start(bf16[144,128]{1,0:T(8,128)(2,1)S(1)} %get-tuple-element.32), channel_id=1, source_target_pairs={{0,8},{8,16},{16,24},{24,32},{32,40},{40,48},{48,56},{56,64},{64,7... | collective-permute-start | bytes 110600 | tf_op jit(solution)/shard_map/ppermute | solution.py:529
  10.6 12.6 %all-to-all-start = ((bf16[8,160,128]{2,1,0:T(8,128)(2,1)}), bf16[8,160,128]{2,1,0:T(8,128)(2,1)S(1)}, u32[]{:S(2)}, u32[]{:S(2)}) async-start(bf16[8,160,128]{2,1,0:T(8,128)(2,1)} %get-tuple-element.31), calls=%async_computation | async-start | bytes 655360 | tf_op jit(solution)/shard_map/all_to_all | solution.py:528
  17.3 11.8 %collective-permute-start.4 = (bf16[96,128]{1,0:T(8,128)(2,1)S(1)}, bf16[96,128]{1,0:T(8,128)(2,1)S(1)}, u32[]{:S(2)}, u32[]{:S(2)}) collective-permute-start(bf16[96,128]{1,0:T(8,128)(2,1)S(1)} %pad_maximum_fusion), channel_id=1, source_target_pairs={{0,1},{1,2},{2,3},{3,4},{4,5},{5,6},{6,7},{8,9},{9,10},{10,11},{11... | collective-permute-start | bytes 73736 | tf_op jit(solution)/shard_map/ppermute | solution.py:541
  20.9 8.2 %collective-permute-start.5 = (bf16[96,128]{1,0:T(8,128)(2,1)S(1)}, bf16[96,128]{1,0:T(8,128)(2,1)S(1)}, u32[]{:S(2)}, u32[]{:S(2)}) collective-permute-start(bf16[96,128]{1,0:T(8,128)(2,1)S(1)} %pad_maximum_fusion.1), channel_id=1, source_target_pairs={{1,0},{2,1},{3,2},{4,3},{5,4},{6,5},{7,6},{9,8},{10,9},{11,10},{12... | collective-permute-start | bytes 73736 | tf_op jit(solution)/shard_map/ppermute | solution.py:542
  23.3 12.9 %collective-permute-start = (bf16[1280,128]{1,0:T(8,128)(2,1)S(1)}, bf16[1280,128]{1,0:T(8,128)(2,1)S(1)}, u32[]{:S(2)}, u32[]{:S(2)}) collective-permute-start(bf16[1280,128]{1,0:T(8,128)(2,1)S(1)} %bitcast.17), channel_id=1, source_target_pairs={{0,8},{8,16},{16,24},{24,32},{32,40},{40,48},{48,56},{56,64},{64,7... | collective-permute-start | bytes 983048 | tf_op jit(solution)/shard_map/ppermute | solution.py:543
  26.9 10.0 %collective-permute-start.1 = (bf16[1280,128]{1,0:T(8,128)(2,1)S(1)}, bf16[1280,128]{1,0:T(8,128)(2,1)S(1)}, u32[]{:S(2)}, u32[]{:S(2)}) collective-permute-start(bf16[1280,128]{1,0:T(8,128)(2,1)S(1)} %bitcast.18), channel_id=1, source_target_pairs={{8,0},{16,8},{24,16},{32,24},{40,32},{48,40},{56,48},{64,56},{72,6... | collective-permute-start | bytes 983048 | tf_op jit(solution)/shard_map/ppermute | solution.py:544
  29.0 7.9 %copy-start.1 = (s32[1,16]{1,0:T(1,128)S(1)}, s32[1,16]{1,0:T(1,128)}, u32[]{:S(2)}) copy-start(s32[1,16]{1,0:T(1,128)} %ids_ref.1) | copy-start | bytes 196
  29.0 7.8 %copy-start.3 = (s32[1,16]{1,0:T(1,128)S(1)}, s32[1,16]{1,0:T(1,128)}, u32[]{:S(2)}) copy-start(s32[1,16]{1,0:T(1,128)} %which_ref.1) | copy-start | bytes 196
  29.1 7.8 %copy-start.5 = (f32[64,128]{1,0:T(8,128)S(1)}, f32[64,128]{1,0:T(8,128)}, u32[]{:S(2)}) copy-start(f32[64,128]{1,0:T(8,128)} %noise_ref.1) | copy-start | bytes 98308
  50.1 27.1 %all-to-all-start.1 = ((bf16[128,16,128]{2,1,0:T(8,128)(2,1)}), bf16[128,16,128]{2,1,0:T(8,128)(2,1)S(1)}, u32[]{:S(2)}, u32[]{:S(2)}) async-start(bf16[128,16,128]{2,1,0:T(8,128)(2,1)} %bitcast.20), calls=%async_computation.1 | async-start | bytes 1048576 | tf_op jit(solution)/shard_map/all_to_all | solution.py:635
  63.8 19.4 %collective-permute-start.6 = (bf16[640,128]{1,0:T(8,128)(2,1)S(1)}, bf16[640,128]{1,0:T(8,128)(2,1)S(1)}, u32[]{:S(2)}, u32[]{:S(2)}) collective-permute-start(bf16[640,128]{1,0:T(8,128)(2,1)S(1)} %get-tuple-element.35), channel_id=1, source_target_pairs={{0,8},{8,16},{16,24},{24,32},{32,40},{40,48},{48,56},{56,64},{64,7... | collective-permute-start | bytes 491528 | tf_op jit(solution)/shard_map/ppermute | solution.py:638
  67.2 15.9 %collective-permute-start.7 = (bf16[640,128]{1,0:T(8,128)(2,1)S(1)}, bf16[640,128]{1,0:T(8,128)(2,1)S(1)}, u32[]{:S(2)}, u32[]{:S(2)}) collective-permute-start(bf16[640,128]{1,0:T(8,128)(2,1)S(1)} %get-tuple-element.36), channel_id=1, source_target_pairs={{8,0},{16,8},{24,16},{32,24},{40,32},{48,40},{56,48},{64,56},{72,6... | collective-permute-start | bytes 491528 | tf_op jit(solution)/shard_map/ppermute | solution.py:637
  78.2 25.4 %all-to-all-start.2 = ((bf16[128,16,128]{2,1,0:T(8,128)(2,1)}), bf16[128,16,128]{2,1,0:T(8,128)(2,1)S(1)}, u32[]{:S(2)}, u32[]{:S(2)}) async-start(bf16[128,16,128]{2,1,0:T(8,128)(2,1)} %total.1), calls=%async_computation.2 | async-start | bytes 1048576 | tf_op jit(solution)/shard_map/all_to_all | solution.py:668
  84.6 6.9 %collective-permute-start.8 = (bf16[352,128]{1,0:T(8,128)(2,1)S(1)}, bf16[352,128]{1,0:T(8,128)(2,1)S(1)}, u32[]{:S(2)}, u32[]{:S(2)}) collective-permute-start(bf16[352,128]{1,0:T(8,128)(2,1)S(1)} %get-tuple-element.39), channel_id=1, source_target_pairs={{0,1},{1,2},{2,3},{3,4},{4,5},{5,6},{6,7},{7,0},{8,9},{9,10},{10,1... | collective-permute-start | bytes 270344 | tf_op jit(solution)/shard_map/ppermute | solution.py:656
  86.3 8.5 %collective-permute-start.9 = (bf16[352,128]{1,0:T(8,128)(2,1)S(1)}, bf16[352,128]{1,0:T(8,128)(2,1)S(1)}, u32[]{:S(2)}, u32[]{:S(2)}) collective-permute-start(bf16[352,128]{1,0:T(8,128)(2,1)S(1)} %get-tuple-element.40), channel_id=1, source_target_pairs={{0,7},{1,0},{2,1},{3,2},{4,3},{5,4},{6,5},{7,6},{8,15},{9,8},{10,9... | collective-permute-start | bytes 270344 | tf_op jit(solution)/shard_map/ppermute | solution.py:656
  86.3 16.2 %collective-permute-start.10 = (bf16[256,128]{1,0:T(8,128)(2,1)S(1)}, bf16[256,128]{1,0:T(8,128)(2,1)S(1)}, u32[]{:S(2)}, u32[]{:S(2)}) collective-permute-start(bf16[256,128]{1,0:T(8,128)(2,1)S(1)} %get-tuple-element.47), channel_id=1, source_target_pairs={{0,2},{1,3},{2,4},{3,5},{4,6},{5,7},{6,0},{7,1},{8,10},{9,11},{10,... | collective-permute-start | bytes 196616 | tf_op jit(solution)/shard_map/ppermute | solution.py:656
  87.4 15.0 %collective-permute-start.11 = (bf16[256,128]{1,0:T(8,128)(2,1)S(1)}, bf16[256,128]{1,0:T(8,128)(2,1)S(1)}, u32[]{:S(2)}, u32[]{:S(2)}) collective-permute-start(bf16[256,128]{1,0:T(8,128)(2,1)S(1)} %get-tuple-element.48), channel_id=1, source_target_pairs={{0,3},{1,4},{2,5},{3,6},{4,7},{5,0},{6,1},{7,2},{8,11},{9,12},{10,... | collective-permute-start | bytes 196616 | tf_op jit(solution)/shard_map/ppermute | solution.py:656
  90.7 11.7 %collective-permute-start.12 = (bf16[256,128]{1,0:T(8,128)(2,1)S(1)}, bf16[256,128]{1,0:T(8,128)(2,1)S(1)}, u32[]{:S(2)}, u32[]{:S(2)}) collective-permute-start(bf16[256,128]{1,0:T(8,128)(2,1)S(1)} %get-tuple-element.49), channel_id=1, source_target_pairs={{0,4},{1,5},{2,6},{3,7},{4,0},{5,1},{6,2},{7,3},{8,12},{9,13},{10,... | collective-permute-start | bytes 196616 | tf_op jit(solution)/shard_map/ppermute | solution.py:656
  91.5 11.0 %collective-permute-start.13 = (bf16[256,128]{1,0:T(8,128)(2,1)S(1)}, bf16[256,128]{1,0:T(8,128)(2,1)S(1)}, u32[]{:S(2)}, u32[]{:S(2)}) collective-permute-start(bf16[256,128]{1,0:T(8,128)(2,1)S(1)} %get-tuple-element.50), channel_id=1, source_target_pairs={{0,5},{1,6},{2,7},{3,0},{4,1},{5,2},{6,3},{7,4},{8,13},{9,14},{10,... | collective-permute-start | bytes 196616 | tf_op jit(solution)/shard_map/ppermute | solution.py:656
  94.8 7.7 %collective-permute-start.14 = (bf16[256,128]{1,0:T(8,128)(2,1)S(1)}, bf16[256,128]{1,0:T(8,128)(2,1)S(1)}, u32[]{:S(2)}, u32[]{:S(2)}) collective-permute-start(bf16[256,128]{1,0:T(8,128)(2,1)S(1)} %get-tuple-element.51), channel_id=1, source_target_pairs={{0,6},{1,7},{2,0},{3,1},{4,2},{5,3},{6,4},{7,5},{8,14},{9,15},{10,... | collective-permute-start | bytes 196616 | tf_op jit(solution)/shard_map/ppermute | solution.py:656

commit v4 on v3

--- a/solution.py
+++ b/solution.py
@@ -90,14 +90,12 @@
 
 
 def pack_kernel(
-    coarse_ref, ids_hbm, which_hbm, cot_hbm, own_ref, all_ref, down_ref, up_ref,
-    work_ref, meta_ref, small_ref, sems,
+    coarse_ref, small_ref, cot_hbm, own_ref, all_ref, down_ref, up_ref,
+    work_ref, meta_ref, sems,
 ):
     per, variables, chans = coarse_ref.shape
     rows, cells = cot_hbm.shape[:2]
     copies = [
-        pltpu.make_async_copy(ids_hbm, small_ref.at[0], sems.at[2]),
-        pltpu.make_async_copy(which_hbm, small_ref.at[1], sems.at[3]),
         pltpu.make_async_copy(cot_hbm.at[rows - 1], down_ref.at[pl.ds(META, cells)], sems.at[0]),
         pltpu.make_async_copy(cot_hbm.at[0], up_ref.at[pl.ds(META, cells)], sems.at[1]),
     ]
@@ -110,12 +108,12 @@
     for target in range(all_ref.shape[0]):
         all_ref[target] = work
     meta_ref[...] = jnp.zeros_like(meta_ref)
-    wait_all(copies)
-    slots = small_ref.shape[2]
-    meta_ref[0:1, :slots] = small_ref[0].astype(F32)
-    meta_ref[1:2, :slots] = small_ref[1].astype(F32)
+    slots = small_ref.shape[1] // 2
+    meta_ref[0:1, :slots] = small_ref[:, :slots].astype(F32)
+    meta_ref[1:2, :slots] = small_ref[:, slots:].astype(F32)
     down_ref[:META, :] = meta_ref[...].astype(BF)
     up_ref[:META, :] = meta_ref[...].astype(BF)
+    wait_all(copies)
 
 
 def fill_columns(got_left, got_right, above_ref, below_ref, left_ref, right_ref, pad_ref):
@@ -514,17 +512,16 @@
             shape((META + cells, chans)),
             shape((META + cells, chans)),
         ),
-        in_specs=[VMEM, HBM, HBM, HBM],
+        in_specs=[VMEM, VMEM, HBM],
         out_specs=(VMEM,) * 4,
         scratch_shapes=[
             pltpu.VMEM((nown, chans), F32),
             pltpu.VMEM((META, chans), F32),
-            pltpu.VMEM((2, 1, slots), jnp.int32),
-            pltpu.SemaphoreType.DMA((4,)),
+            pltpu.SemaphoreType.DMA((2,)),
         ],
         compiler_params=params(LIMIT),
         name="pack",
-    )(coarse, block_ids, interp_index, cotangent)
+    )(coarse, jnp.concatenate([block_ids, interp_index], axis=1), cotangent)
     band_own = lax.all_to_all(spread, "gx", 0, 0, tiled=True).reshape(rowblk * VP, chans)
     from_above = lax.ppermute(to_below, "gy", down)
     from_below = lax.ppermute(to_above, "gy", up)

time: 105 us -> 104 us (level)
  local copies, waits for them, and re-layouts: 3.97 us -> 2.7 us
    unnamed x20 -> x16, local copies, waits for them, and re-layouts: 2.81 us -> 1.54 us
where the time goes in v4:
time: 104 us
  starting transfers between devices  55.5 us (53%)
  Pallas kernels  33.1 us (32%)
  waiting for transfers between devices  10 us (10%)
  local copies, waits for them, and re-layouts  2.7 us (3%)
  between operations  1.68 us (2%)
    all_to_all x1, starting transfers between devices, body(): lax.all_to_all(shared.reshape(n_dev, PACK, chans), both, 0, 0, tiled=True)  13.6 us
    pallas_call x1, Pallas kernels, body(): pl.pallas_call(main_kernel, out_shape=(shape(field), shape(field), shape(...  13.2 us
    ppermute x7, starting transfers between devices, body(): lax.ppermute(part, 'gx', [(i, (i + k) % n_gx) for i in range(n_gx)])  10.3 us
    all_to_all x1, waiting for transfers between devices, body(): lax.all_to_all(shared.reshape(n_dev, PACK, chans), both, 0, 0, tiled=True)  8.76 us
    pallas_call x1, Pallas kernels, body(): pl.pallas_call(conv_kernel, out_shape=shape(paired), in_specs=[SMEM, HBM]...  7.57 us
    pallas_call x1, Pallas kernels, body(): pl.pallas_call(back_kernel, out_shape=shape(paired), in_specs=[HBM] + [VM...  7.07 us
    all_to_all x1, starting transfers between devices, body(): lax.all_to_all(spread, 'gx', 0, 0, tiled=True).reshape(rowblk * VP, chans)  5.53 us
    ppermute x1, starting transfers between devices, body(): from_above = lax.ppermute(to_below, 'gy', down)  5 us
  transfers between devices with their start and end apart: 18, of which 3 were waited for; matrix products, arithmetic and copies ran while one was open for 2% of the time, Pallas kernels for 17%

profile of v4, /device:TPU:1, one launch (start us, length us, event | category | flops | bytes accessed | tf_op | source)
XLA Modules:
  0.0 103.8 jit_solution(4973027892107122455)
XLA Ops:
  0.6 0.0 copy-start.5
  0.6 0.0 copy-start.4
  0.7 0.0 copy-start.2
  0.7 0.8 copy.17.coarse_ref
  1.5 0.7 pad_add_fusion.2.small_ref
  2.2 1.5 %pack.1 = (bf16[160,128]{1,0:T(8,128)(2,1)S(1)}, bf16[8,160,128]{2,1,0:T(8,128)(2,1)}, bf16[144,128]{1,0:T(8,128)(2,1)S(1)}, bf16[144,128]{1,0:T(8,128)(2,1)S(1)}) custom-call(bf16[2,70,128]{2,1,0:T(8,128)(2,1)S(1)} %copy.17.coarse_ref, s32[1,32]{1,0:T(1,128)S(1)} %pad_add_fusion.2.small_ref, bf16[64,128,128]{2,1,0:T(8,128)(2,1)} %cot_hbm.5), custom_call_target="tpu_custom_call" | custom-call | tf_op jit(solution)/shard_map/pack/pallas_call | solution.py:507
  3.8 1.3 %collective-permute-start.3 = (bf16[144,128]{1,0:T(8,128)(2,1)S(1)}, bf16[144,128]{1,0:T(8,128)(2,1)S(1)}, u32[]{:S(2)}, u32[]{:S(2)}) collective-permute-start(bf16[144,128]{1,0:T(8,128)(2,1)S(1)} %get-tuple-element.33), channel_id=1, source_target_pairs={{8,0},{16,8},{24,16},{32,24},{40,32},{48,40},{56,48},{64,56},{72,6... | collective-permute-start | bytes 110600 | tf_op jit(solution)/shard_map/ppermute | solution.py:527
  5.1 5.0 %collective-permute-start.2 = (bf16[144,128]{1,0:T(8,128)(2,1)S(1)}, bf16[144,128]{1,0:T(8,128)(2,1)S(1)}, u32[]{:S(2)}, u32[]{:S(2)}) collective-permute-start(bf16[144,128]{1,0:T(8,128)(2,1)S(1)} %get-tuple-element.32), channel_id=1, source_target_pairs={{0,8},{8,16},{16,24},{24,32},{32,40},{40,48},{48,56},{56,64},{64,7... | collective-permute-start | bytes 110600 | tf_op jit(solution)/shard_map/ppermute | solution.py:526
  10.1 5.5 %all-to-all-start = ((bf16[8,160,128]{2,1,0:T(8,128)(2,1)}), bf16[8,160,128]{2,1,0:T(8,128)(2,1)S(1)}, u32[]{:S(2)}, u32[]{:S(2)}) async-start(bf16[8,160,128]{2,1,0:T(8,128)(2,1)} %get-tuple-element.31), calls=%async_computation | async-start | bytes 655360 | tf_op jit(solution)/shard_map/all_to_all | solution.py:525
  15.6 1.0 fusion
  16.7 0.0 collective-permute-done.3.below_ref
  16.7 0.0 collective-permute-done.2.above_ref
  16.7 3.5 %collective-permute-start.4 = (bf16[96,128]{1,0:T(8,128)(2,1)S(1)}, bf16[96,128]{1,0:T(8,128)(2,1)S(1)}, u32[]{:S(2)}, u32[]{:S(2)}) collective-permute-start(bf16[96,128]{1,0:T(8,128)(2,1)S(1)} %pad_maximum_fusion), channel_id=1, source_target_pairs={{0,1},{1,2},{2,3},{3,4},{4,5},{5,6},{6,7},{8,9},{9,10},{10,11},{11... | collective-permute-start | bytes 73736 | tf_op jit(solution)/shard_map/ppermute | solution.py:538
  20.3 1.9 %collective-permute-start.5 = (bf16[96,128]{1,0:T(8,128)(2,1)S(1)}, bf16[96,128]{1,0:T(8,128)(2,1)S(1)}, u32[]{:S(2)}, u32[]{:S(2)}) collective-permute-start(bf16[96,128]{1,0:T(8,128)(2,1)S(1)} %pad_maximum_fusion.1), channel_id=1, source_target_pairs={{1,0},{2,1},{3,2},{4,3},{5,4},{6,5},{7,6},{9,8},{10,9},{11,10},{12... | collective-permute-start | bytes 73736 | tf_op jit(solution)/shard_map/ppermute | solution.py:539
  22.2 0.5 all-to-all-done
  22.7 3.6 %collective-permute-start = (bf16[1280,128]{1,0:T(8,128)(2,1)S(1)}, bf16[1280,128]{1,0:T(8,128)(2,1)S(1)}, u32[]{:S(2)}, u32[]{:S(2)}) collective-permute-start(bf16[1280,128]{1,0:T(8,128)(2,1)S(1)} %bitcast.17), channel_id=1, source_target_pairs={{0,8},{8,16},{16,24},{24,32},{32,40},{40,48},{48,56},{56,64},{64,7... | collective-permute-start | bytes 983048 | tf_op jit(solution)/shard_map/ppermute | solution.py:540
  26.3 1.3 %collective-permute-start.1 = (bf16[1280,128]{1,0:T(8,128)(2,1)S(1)}, bf16[1280,128]{1,0:T(8,128)(2,1)S(1)}, u32[]{:S(2)}, u32[]{:S(2)}) collective-permute-start(bf16[1280,128]{1,0:T(8,128)(2,1)S(1)} %bitcast.18), channel_id=1, source_target_pairs={{8,0},{16,8},{24,16},{32,24},{40,32},{48,40},{56,48},{64,56},{72,6... | collective-permute-start | bytes 983048 | tf_op jit(solution)/shard_map/ppermute | solution.py:541
  27.6 0.1 pad_add_fusion.1.pos_ref
  27.7 0.0 copy-done.5
  27.7 0.1 copy.20.bias_col_ref
  28.4 0.0 copy-done.4
  28.5 0.0 copy-start
  28.5 0.0 copy-start.1
  28.5 0.0 copy-start.3
  28.5 0.0 collective-permute-done.4.left16_ref
  28.5 0.0 collective-permute-done.5.right16_ref
  28.5 0.0 copy-done.2
  28.5 7.1 %back.1 = bf16[32,2,128,128]{3,2,1,0:T(8,128)(2,1)} custom-call(bf16[64,128,128]{2,1,0:T(8,128)(2,1)} %cot_hbm.5, bf16[144,128]{1,0:T(8,128)(2,1)S(1)} %collective-permute-done.2.above_ref, bf16[144,128]{1,0:T(8,128)(2,1)S(1)} %collective-permute-done.3.below_ref, bf16[96,128]{1,0:T(8,128)(2,1)S(1)} %collective-permute-done.4.left16_ref, ...), custom_call_target="tpu_custom_call" | custom-call | flops 3221225472 | bytes 12582912 | tf_op jit(solution)/shard_map/back/pallas_call | solution.py:551
  35.6 0.0 collective-permute-done.band_above_ref
  35.6 0.7 collective-permute-done.1.band_below_ref
  36.3 0.0 copy-done
  36.3 0.0 copy-done.1
  36.3 0.0 copy-done.3
  36.3 13.2 %main.1 = (bf16[64,128,128]{2,1,0:T(8,128)(2,1)}, bf16[64,128,128]{2,1,0:T(8,128)(2,1)}, bf16[64,128,128]{2,1,0:T(8,128)(2,1)}, f32[2,64,128]{2,1,0:T(8,128)S(1)...) custom-call(s32[3]{0:T(128)S(1)} %pad_add_fusion.1.pos_ref, ...), custom_call_target="tpu_custom_call" | custom-call | flops 9663676416 | bytes 25165824 | tf_op jit(solution)/shard_map/main/pallas_call | solution.py:573
  49.5 13.6 %all-to-all-start.1 = ((bf16[128,16,128]{2,1,0:T(8,128)(2,1)}), bf16[128,16,128]{2,1,0:T(8,128)(2,1)S(1)}, u32[]{:S(2)}, u32[]{:S(2)}) async-start(bf16[128,16,128]{2,1,0:T(8,128)(2,1)} %bitcast.20), calls=%async_computation.1 | async-start | bytes 1048576 | tf_op jit(solution)/shard_map/all_to_all | solution.py:632
  63.1 3.4 %collective-permute-start.6 = (bf16[640,128]{1,0:T(8,128)(2,1)S(1)}, bf16[640,128]{1,0:T(8,128)(2,1)S(1)}, u32[]{:S(2)}, u32[]{:S(2)}) collective-permute-start(bf16[640,128]{1,0:T(8,128)(2,1)S(1)} %get-tuple-element.35), channel_id=1, source_target_pairs={{0,8},{8,16},{16,24},{24,32},{32,40},{40,48},{48,56},{56,64},{64,7... | collective-permute-start | bytes 491528 | tf_op jit(solution)/shard_map/ppermute | solution.py:635
  66.5 1.3 %collective-permute-start.7 = (bf16[640,128]{1,0:T(8,128)(2,1)S(1)}, bf16[640,128]{1,0:T(8,128)(2,1)S(1)}, u32[]{:S(2)}, u32[]{:S(2)}) collective-permute-start(bf16[640,128]{1,0:T(8,128)(2,1)S(1)} %get-tuple-element.36), channel_id=1, source_target_pairs={{8,0},{16,8},{24,16},{32,24},{40,32},{48,40},{56,48},{64,56},{72,6... | collective-permute-start | bytes 491528 | tf_op jit(solution)/shard_map/ppermute | solution.py:634
  67.8 8.8 %all-to-all-done.1.got_ref = bf16[128,16,128]{2,1,0:T(8,128)(2,1)S(1)} async-done(((bf16[128,16,128]{2,1,0:T(8,128)(2,1)}), bf16[128,16,128]{2,1,0:T(8,128)(2,1)S(1)}, u32[]{:S(2)}, u32[]{:S(2)}) %all-to-all-start.1) | async-done | bytes 524320 | tf_op jit(solution)/shard_map/all_to_all | solution.py:632
  76.6 1.0 total.1
  77.6 4.9 %all-to-all-start.2 = ((bf16[128,16,128]{2,1,0:T(8,128)(2,1)}), bf16[128,16,128]{2,1,0:T(8,128)(2,1)S(1)}, u32[]{:S(2)}, u32[]{:S(2)}) async-start(bf16[128,16,128]{2,1,0:T(8,128)(2,1)} %total.1), calls=%async_computation.2 | async-start | bytes 1048576 | tf_op jit(solution)/shard_map/all_to_all | solution.py:665
  82.5 0.0 collective-permute-done.6.above_ref
  82.5 0.0 collective-permute-done.7.below_ref
  82.5 1.5 %band.1 = (f32[2,128,128]{2,1,0:T(8,128)S(1)}, bf16[352,128]{1,0:T(8,128)(2,1)S(1)}, bf16[256,128]{1,0:T(8,128)(2,1)S(1)}, bf16[256,128]{1,0:T(8,128)(2,1)S(1)},...) custom-call(s32[3]{0:T(128)S(1)} %pad_add_fusion.1.pos_ref, ...), custom_call_target="tpu_custom_call" | custom-call | flops 4194304 | bytes 1048576 | tf_op jit(solution)/shard_map/band/pallas_call | solution.py:642
  84.0 1.7 %collective-permute-start.8 = (bf16[352,128]{1,0:T(8,128)(2,1)S(1)}, bf16[352,128]{1,0:T(8,128)(2,1)S(1)}, u32[]{:S(2)}, u32[]{:S(2)}) collective-permute-start(bf16[352,128]{1,0:T(8,128)(2,1)S(1)} %get-tuple-element.39), channel_id=1, source_target_pairs={{0,1},{1,2},{2,3},{3,4},{4,5},{5,6},{6,7},{7,0},{8,9},{9,10},{10,1... | collective-permute-start | bytes 270344 | tf_op jit(solution)/shard_map/ppermute | solution.py:653
  85.6 0.0 collective-permute-start.9
  85.6 1.2 %collective-permute-start.10 = (bf16[256,128]{1,0:T(8,128)(2,1)S(1)}, bf16[256,128]{1,0:T(8,128)(2,1)S(1)}, u32[]{:S(2)}, u32[]{:S(2)}) collective-permute-start(bf16[256,128]{1,0:T(8,128)(2,1)S(1)} %get-tuple-element.47), channel_id=1, source_target_pairs={{0,2},{1,3},{2,4},{3,5},{4,6},{5,7},{6,0},{7,1},{8,10},{9,11},{10,... | collective-permute-start | bytes 196616 | tf_op jit(solution)/shard_map/ppermute | solution.py:653
  86.8 3.2 %collective-permute-start.11 = (bf16[256,128]{1,0:T(8,128)(2,1)S(1)}, bf16[256,128]{1,0:T(8,128)(2,1)S(1)}, u32[]{:S(2)}, u32[]{:S(2)}) collective-permute-start(bf16[256,128]{1,0:T(8,128)(2,1)S(1)} %get-tuple-element.48), channel_id=1, source_target_pairs={{0,3},{1,4},{2,5},{3,6},{4,7},{5,0},{6,1},{7,2},{8,11},{9,12},{10,... | collective-permute-start | bytes 196616 | tf_op jit(solution)/shard_map/ppermute | solution.py:653
  90.1 0.8 collective-permute-start.12
  90.9 0.0 collective-permute-done.8.got_left_ref.refs_0_
  90.9 3.3 %collective-permute-start.13 = (bf16[256,128]{1,0:T(8,128)(2,1)S(1)}, bf16[256,128]{1,0:T(8,128)(2,1)S(1)}, u32[]{:S(2)}, u32[]{:S(2)}) collective-permute-start(bf16[256,128]{1,0:T(8,128)(2,1)S(1)} %get-tuple-element.50), channel_id=1, source_target_pairs={{0,5},{1,6},{2,7},{3,0},{4,1},{5,2},{6,3},{7,4},{8,13},{9,14},{10,... | collective-permute-start | bytes 196616 | tf_op jit(solution)/shard_map/ppermute | solution.py:653
  94.1 0.0 collective-permute-done.9.got_right_ref.refs_6_
  94.1 0.1 collective-permute-start.14
  94.3 7.6 %conv.1 = bf16[32,2,128,128]{3,2,1,0:T(8,128)(2,1)} custom-call(s32[3]{0:T(128)S(1)} %pad_add_fusion.1.pos_ref, bf16[64,128,128]{2,1,0:T(8,128)(2,1)} %get-tuple-element.34.smooth_hbm, bf16[640,128]{1,0:T(8,128)(2,1)S(1)} %collective-permute-done.6.above_ref, bf16[640,128]{1,0:T(8,128)(2,1)S(1)} %collective-permute-done.7.below_ref, ...), custom_call_target="tpu_custom_call" | custom-call | flops 3221225472 | bytes 8388608 | tf_op jit(solution)/shard_map/conv/pallas_call | solution.py:667
  101.8 0.0 collective-permute-done.10.refs_1_
  101.8 0.0 collective-permute-done.11.refs_2_
  101.9 0.0 collective-permute-done.12.refs_3_
  101.9 0.0 collective-permute-done.13.refs_4_
  101.9 0.0 collective-permute-done.14.refs_5_
  101.9 0.4 owner.1
  102.3 0.7 copy.22
  103.0 0.0 all-to-all-done.2
  103.0 0.9 finish.1
  (12 shorter events, 0.1 us)
Async XLA Ops:
  0.6 27.0 %copy-start.5 = (f32[128]{0:T(128)S(1)}, f32[128]{0:T(128)}, u32[]{:S(2)}) copy-start(f32[128]{0:T(128)} %param.13) | copy-start | bytes 1540
  0.6 27.8 %copy-start.4 = (bf16[70,128]{1,0:T(8,128)(2,1)S(1)}, bf16[70,128]{1,0:T(8,128)(2,1)}, u32[]{:S(2)}) copy-start(bf16[70,128]{1,0:T(8,128)(2,1)} %param.12) | copy-start | bytes 53764
  0.7 27.9 %copy-start.2 = (bf16[9,128,128]{2,1,0:T(8,128)(2,1)S(1)}, bf16[9,128,128]{2,1,0:T(8,128)(2,1)}, u32[]{:S(2)}) copy-start(bf16[9,128,128]{2,1,0:T(8,128)(2,1)} %w_ref.3) | copy-start | bytes 884740
  3.8 12.9 %collective-permute-start.3 = (bf16[144,128]{1,0:T(8,128)(2,1)S(1)}, bf16[144,128]{1,0:T(8,128)(2,1)S(1)}, u32[]{:S(2)}, u32[]{:S(2)}) collective-permute-start(bf16[144,128]{1,0:T(8,128)(2,1)S(1)} %get-tuple-element.33), channel_id=1, source_target_pairs={{8,0},{16,8},{24,16},{32,24},{40,32},{48,40},{56,48},{64,56},{72,6... | collective-permute-start | bytes 110600 | tf_op jit(solution)/shard_map/ppermute | solution.py:527
  5.1 11.6 %collective-permute-start.2 = (bf16[144,128]{1,0:T(8,128)(2,1)S(1)}, bf16[144,128]{1,0:T(8,128)(2,1)S(1)}, u32[]{:S(2)}, u32[]{:S(2)}) collective-permute-start(bf16[144,128]{1,0:T(8,128)(2,1)S(1)} %get-tuple-element.32), channel_id=1, source_target_pairs={{0,8},{8,16},{16,24},{24,32},{32,40},{40,48},{48,56},{56,64},{64,7... | collective-permute-start | bytes 110600 | tf_op jit(solution)/shard_map/ppermute | solution.py:526
  10.1 12.6 %all-to-all-start = ((bf16[8,160,128]{2,1,0:T(8,128)(2,1)}), bf16[8,160,128]{2,1,0:T(8,128)(2,1)S(1)}, u32[]{:S(2)}, u32[]{:S(2)}) async-start(bf16[8,160,128]{2,1,0:T(8,128)(2,1)} %get-tuple-element.31), calls=%async_computation | async-start | bytes 655360 | tf_op jit(solution)/shard_map/all_to_all | solution.py:525
  16.7 11.8 %collective-permute-start.4 = (bf16[96,128]{1,0:T(8,128)(2,1)S(1)}, bf16[96,128]{1,0:T(8,128)(2,1)S(1)}, u32[]{:S(2)}, u32[]{:S(2)}) collective-permute-start(bf16[96,128]{1,0:T(8,128)(2,1)S(1)} %pad_maximum_fusion), channel_id=1, source_target_pairs={{0,1},{1,2},{2,3},{3,4},{4,5},{5,6},{6,7},{8,9},{9,10},{10,11},{11... | collective-permute-start | bytes 73736 | tf_op jit(solution)/shard_map/ppermute | solution.py:538
  20.3 8.2 %collective-permute-start.5 = (bf16[96,128]{1,0:T(8,128)(2,1)S(1)}, bf16[96,128]{1,0:T(8,128)(2,1)S(1)}, u32[]{:S(2)}, u32[]{:S(2)}) collective-permute-start(bf16[96,128]{1,0:T(8,128)(2,1)S(1)} %pad_maximum_fusion.1), channel_id=1, source_target_pairs={{1,0},{2,1},{3,2},{4,3},{5,4},{6,5},{7,6},{9,8},{10,9},{11,10},{12... | collective-permute-start | bytes 73736 | tf_op jit(solution)/shard_map/ppermute | solution.py:539
  22.7 12.9 %collective-permute-start = (bf16[1280,128]{1,0:T(8,128)(2,1)S(1)}, bf16[1280,128]{1,0:T(8,128)(2,1)S(1)}, u32[]{:S(2)}, u32[]{:S(2)}) collective-permute-start(bf16[1280,128]{1,0:T(8,128)(2,1)S(1)} %bitcast.17), channel_id=1, source_target_pairs={{0,8},{8,16},{16,24},{24,32},{32,40},{40,48},{48,56},{56,64},{64,7... | collective-permute-start | bytes 983048 | tf_op jit(solution)/shard_map/ppermute | solution.py:540
  26.3 10.0 %collective-permute-start.1 = (bf16[1280,128]{1,0:T(8,128)(2,1)S(1)}, bf16[1280,128]{1,0:T(8,128)(2,1)S(1)}, u32[]{:S(2)}, u32[]{:S(2)}) collective-permute-start(bf16[1280,128]{1,0:T(8,128)(2,1)S(1)} %bitcast.18), channel_id=1, source_target_pairs={{8,0},{16,8},{24,16},{32,24},{40,32},{48,40},{56,48},{64,56},{72,6... | collective-permute-start | bytes 983048 | tf_op jit(solution)/shard_map/ppermute | solution.py:541
  28.5 7.9 %copy-start = (s32[1,16]{1,0:T(1,128)S(1)}, s32[1,16]{1,0:T(1,128)}, u32[]{:S(2)}) copy-start(s32[1,16]{1,0:T(1,128)} %ids_ref.1) | copy-start | bytes 196
  28.5 7.8 %copy-start.1 = (s32[1,16]{1,0:T(1,128)S(1)}, s32[1,16]{1,0:T(1,128)}, u32[]{:S(2)}) copy-start(s32[1,16]{1,0:T(1,128)} %which_ref.1) | copy-start | bytes 196
  28.5 7.8 %copy-start.3 = (f32[64,128]{1,0:T(8,128)S(1)}, f32[64,128]{1,0:T(8,128)}, u32[]{:S(2)}) copy-start(f32[64,128]{1,0:T(8,128)} %noise_ref.1) | copy-start | bytes 98308
  49.5 27.1 %all-to-all-start.1 = ((bf16[128,16,128]{2,1,0:T(8,128)(2,1)}), bf16[128,16,128]{2,1,0:T(8,128)(2,1)S(1)}, u32[]{:S(2)}, u32[]{:S(2)}) async-start(bf16[128,16,128]{2,1,0:T(8,128)(2,1)} %bitcast.20), calls=%async_computation.1 | async-start | bytes 1048576 | tf_op jit(solution)/shard_map/all_to_all | solution.py:632
  63.1 19.4 %collective-permute-start.6 = (bf16[640,128]{1,0:T(8,128)(2,1)S(1)}, bf16[640,128]{1,0:T(8,128)(2,1)S(1)}, u32[]{:S(2)}, u32[]{:S(2)}) collective-permute-start(bf16[640,128]{1,0:T(8,128)(2,1)S(1)} %get-tuple-element.35), channel_id=1, source_target_pairs={{0,8},{8,16},{16,24},{24,32},{32,40},{40,48},{48,56},{56,64},{64,7... | collective-permute-start | bytes 491528 | tf_op jit(solution)/shard_map/ppermute | solution.py:635
  66.5 15.9 %collective-permute-start.7 = (bf16[640,128]{1,0:T(8,128)(2,1)S(1)}, bf16[640,128]{1,0:T(8,128)(2,1)S(1)}, u32[]{:S(2)}, u32[]{:S(2)}) collective-permute-start(bf16[640,128]{1,0:T(8,128)(2,1)S(1)} %get-tuple-element.36), channel_id=1, source_target_pairs={{8,0},{16,8},{24,16},{32,24},{40,32},{48,40},{56,48},{64,56},{72,6... | collective-permute-start | bytes 491528 | tf_op jit(solution)/shard_map/ppermute | solution.py:634
  77.6 25.4 %all-to-all-start.2 = ((bf16[128,16,128]{2,1,0:T(8,128)(2,1)}), bf16[128,16,128]{2,1,0:T(8,128)(2,1)S(1)}, u32[]{:S(2)}, u32[]{:S(2)}) async-start(bf16[128,16,128]{2,1,0:T(8,128)(2,1)} %total.1), calls=%async_computation.2 | async-start | bytes 1048576 | tf_op jit(solution)/shard_map/all_to_all | solution.py:665
  84.0 6.9 %collective-permute-start.8 = (bf16[352,128]{1,0:T(8,128)(2,1)S(1)}, bf16[352,128]{1,0:T(8,128)(2,1)S(1)}, u32[]{:S(2)}, u32[]{:S(2)}) collective-permute-start(bf16[352,128]{1,0:T(8,128)(2,1)S(1)} %get-tuple-element.39), channel_id=1, source_target_pairs={{0,1},{1,2},{2,3},{3,4},{4,5},{5,6},{6,7},{7,0},{8,9},{9,10},{10,1... | collective-permute-start | bytes 270344 | tf_op jit(solution)/shard_map/ppermute | solution.py:653
  85.6 8.5 %collective-permute-start.9 = (bf16[352,128]{1,0:T(8,128)(2,1)S(1)}, bf16[352,128]{1,0:T(8,128)(2,1)S(1)}, u32[]{:S(2)}, u32[]{:S(2)}) collective-permute-start(bf16[352,128]{1,0:T(8,128)(2,1)S(1)} %get-tuple-element.40), channel_id=1, source_target_pairs={{0,7},{1,0},{2,1},{3,2},{4,3},{5,4},{6,5},{7,6},{8,15},{9,8},{10,9... | collective-permute-start | bytes 270344 | tf_op jit(solution)/shard_map/ppermute | solution.py:653
  85.6 16.2 %collective-permute-start.10 = (bf16[256,128]{1,0:T(8,128)(2,1)S(1)}, bf16[256,128]{1,0:T(8,128)(2,1)S(1)}, u32[]{:S(2)}, u32[]{:S(2)}) collective-permute-start(bf16[256,128]{1,0:T(8,128)(2,1)S(1)} %get-tuple-element.47), channel_id=1, source_target_pairs={{0,2},{1,3},{2,4},{3,5},{4,6},{5,7},{6,0},{7,1},{8,10},{9,11},{10,... | collective-permute-start | bytes 196616 | tf_op jit(solution)/shard_map/ppermute | solution.py:653
  86.8 15.0 %collective-permute-start.11 = (bf16[256,128]{1,0:T(8,128)(2,1)S(1)}, bf16[256,128]{1,0:T(8,128)(2,1)S(1)}, u32[]{:S(2)}, u32[]{:S(2)}) collective-permute-start(bf16[256,128]{1,0:T(8,128)(2,1)S(1)} %get-tuple-element.48), channel_id=1, source_target_pairs={{0,3},{1,4},{2,5},{3,6},{4,7},{5,0},{6,1},{7,2},{8,11},{9,12},{10,... | collective-permute-start | bytes 196616 | tf_op jit(solution)/shard_map/ppermute | solution.py:653
  90.1 11.8 %collective-permute-start.12 = (bf16[256,128]{1,0:T(8,128)(2,1)S(1)}, bf16[256,128]{1,0:T(8,128)(2,1)S(1)}, u32[]{:S(2)}, u32[]{:S(2)}) collective-permute-start(bf16[256,128]{1,0:T(8,128)(2,1)S(1)} %get-tuple-element.49), channel_id=1, source_target_pairs={{0,4},{1,5},{2,6},{3,7},{4,0},{5,1},{6,2},{7,3},{8,12},{9,13},{10,... | collective-permute-start | bytes 196616 | tf_op jit(solution)/shard_map/ppermute | solution.py:653
  90.9 11.0 %collective-permute-start.13 = (bf16[256,128]{1,0:T(8,128)(2,1)S(1)}, bf16[256,128]{1,0:T(8,128)(2,1)S(1)}, u32[]{:S(2)}, u32[]{:S(2)}) collective-permute-start(bf16[256,128]{1,0:T(8,128)(2,1)S(1)} %get-tuple-element.50), channel_id=1, source_target_pairs={{0,5},{1,6},{2,7},{3,0},{4,1},{5,2},{6,3},{7,4},{8,13},{9,14},{10,... | collective-permute-start | bytes 196616 | tf_op jit(solution)/shard_map/ppermute | solution.py:653
  94.1 7.8 %collective-permute-start.14 = (bf16[256,128]{1,0:T(8,128)(2,1)S(1)}, bf16[256,128]{1,0:T(8,128)(2,1)S(1)}, u32[]{:S(2)}, u32[]{:S(2)}) collective-permute-start(bf16[256,128]{1,0:T(8,128)(2,1)S(1)} %get-tuple-element.51), channel_id=1, source_target_pairs={{0,6},{1,7},{2,0},{3,1},{4,2},{5,3},{6,4},{7,5},{8,14},{9,15},{10,... | collective-permute-start | bytes 196616 | tf_op jit(solution)/shard_map/ppermute | solution.py:653

commit v5 on v4

--- a/solution.py
+++ b/solution.py
@@ -126,22 +126,17 @@
 
 
 def back_kernel(
-    cot_hbm, above_ref, below_ref, left16_ref, right16_ref, w_ref,
-    back_hbm, cot_ref, back_ref, pad_ref, taps_ref, left_ref, right_ref, in_sems, out_sems,
+    cot_ref, above_ref, below_ref, left16_ref, right16_ref, w_ref,
+    back_hbm, back_ref, pad_ref, taps_ref, left_ref, right_ref, out_sems,
 ):
     pairs, _, cells, chans = back_ref.shape
     count = PAIRS
     groups = pairs // count
 
-    def fetch(g):
-        at = pl.ds(g * 2 * count, 2 * count)
-        return pltpu.make_async_copy(cot_hbm.at[at], cot_ref.at[at], in_sems.at[g])
-
     def send(g):
         at = pl.ds(g * count, count)
         return pltpu.make_async_copy(back_ref.at[at], back_hbm.at[at], out_sems.at[g])
 
-    start_all([fetch(g) for g in range(groups)])
     taps_ref[...] = jnp.zeros_like(taps_ref)
     for dy in range(3):
         for dx in range(3):
@@ -153,7 +148,6 @@
     )
 
     def pad(g, _):
-        fetch(g).wait()
         put_pairs(cot_ref, g * count, count, left_ref, right_ref, pad_ref)
         return 0
 
@@ -551,19 +545,17 @@
     back = pl.pallas_call(
         back_kernel,
         out_shape=shape(paired),
-        in_specs=[HBM] + [VMEM] * 5,
+        in_specs=[VMEM] * 6,
         out_specs=HBM,
         scratch_shapes=[
-            pltpu.VMEM(field, BF),
             pltpu.VMEM(paired, BF),
             pltpu.VMEM(pad_shape, BF),
             pltpu.VMEM((2 * chans, 12 * chans), BF),
             columns,
             columns,
             pltpu.SemaphoreType.DMA((groups,)),
-            pltpu.SemaphoreType.DMA((groups,)),
         ],
-        compiler_params=params(LIMIT),
+        compiler_params=params(20),
         cost_estimate=cost(conv_flops, 12 << 20),
         name="back",
     )(cotangent, from_above, from_below, cot_left, cot_right, conv_weight)

time: 104 us -> 105 us (level)
  Pallas kernels: 33.1 us -> 31.5 us
  local copies, waits for them, and re-layouts: 2.7 us -> 4.11 us
    unnamed x16 -> x22, local copies, waits for them, and re-layouts: 1.54 us -> 3.91 us
    pallas_call x1, Pallas kernels: 7.07 us -> 5.54 us  [body(): pl.pallas_call(back_kernel, out_shape=shape(paired), in_specs=[VMEM] * 6,...]
  transfers between devices with their start and end apart: 18 -> 18, of which waited for: 3 -> 2; matrix products, arithmetic and copies ran while one was open for 2% -> 1% of each run, Pallas kernels for 17% -> 15%
where the time goes in v5:
time: 105 us; the launch traced here: 104 us
  starting transfers between devices  55.4 us (53%)
  Pallas kernels  31.5 us (30%)
  waiting for transfers between devices  10.3 us (10%)
  local copies, waits for them, and re-layouts  4.11 us (4%)
  between operations  1.71 us (2%)
    all_to_all x1, starting transfers between devices, body(): lax.all_to_all(shared.reshape(n_dev, PACK, chans), both, 0, 0, tiled=True)  13.4 us
    pallas_call x1, Pallas kernels, body(): pl.pallas_call(main_kernel, out_shape=(shape(field), shape(field), shape(...  13.2 us
    ppermute x7, starting transfers between devices, body(): lax.ppermute(part, 'gx', [(i, (i + k) % n_gx) for i in range(n_gx)])  10.3 us
    all_to_all x1, waiting for transfers between devices, body(): lax.all_to_all(shared.reshape(n_dev, PACK, chans), both, 0, 0, tiled=True)  8.76 us
    pallas_call x1, Pallas kernels, body(): pl.pallas_call(conv_kernel, out_shape=shape(paired), in_specs=[SMEM, HBM]...  7.57 us
    pallas_call x1, Pallas kernels, body(): pl.pallas_call(back_kernel, out_shape=shape(paired), in_specs=[VMEM] * 6,...  5.54 us
    all_to_all x1, starting transfers between devices, body(): lax.all_to_all(spread, 'gx', 0, 0, tiled=True).reshape(rowblk * VP, chans)  5.53 us
    ppermute x1, starting transfers between devices, body(): from_above = lax.ppermute(to_below, 'gy', down)  5 us
  transfers between devices with their start and end apart: 18, of which 2 were waited for; matrix products, arithmetic and copies ran while one was open for 1% of the time, Pallas kernels for 15%

profile of v5, /device:TPU:1, one launch (start us, length us, event | category | flops | bytes accessed | tf_op | source)
XLA Modules:
  0.0 103.9 jit_solution(16992288916700977214)
XLA Ops:
  0.6 0.0 copy-start
  0.6 0.0 copy-start.8
  0.7 0.0 copy-start.7
  0.7 0.9 copy.17.coarse_ref
  1.6 0.7 pad_add_fusion.2.small_ref
  2.3 1.5 %pack.1 = (bf16[160,128]{1,0:T(8,128)(2,1)S(1)}, bf16[8,160,128]{2,1,0:T(8,128)(2,1)}, bf16[144,128]{1,0:T(8,128)(2,1)S(1)}, bf16[144,128]{1,0:T(8,128)(2,1)S(1)}) custom-call(bf16[2,70,128]{2,1,0:T(8,128)(2,1)S(1)} %copy.17.coarse_ref, s32[1,32]{1,0:T(1,128)S(1)} %pad_add_fusion.2.small_ref, bf16[64,128,128]{2,1,0:T(8,128)(2,1)} %cot_hbm.3), custom_call_target="tpu_custom_call" | custom-call | tf_op jit(solution)/shard_map/pack/pallas_call | solution.py:501
  3.9 1.3 %collective-permute-start.3 = (bf16[144,128]{1,0:T(8,128)(2,1)S(1)}, bf16[144,128]{1,0:T(8,128)(2,1)S(1)}, u32[]{:S(2)}, u32[]{:S(2)}) collective-permute-start(bf16[144,128]{1,0:T(8,128)(2,1)S(1)} %get-tuple-element.33), channel_id=1, source_target_pairs={{8,0},{16,8},{24,16},{32,24},{40,32},{48,40},{56,48},{64,56},{72,6... | collective-permute-start | bytes 110600 | tf_op jit(solution)/shard_map/ppermute | solution.py:521
  5.2 5.0 %collective-permute-start.2 = (bf16[144,128]{1,0:T(8,128)(2,1)S(1)}, bf16[144,128]{1,0:T(8,128)(2,1)S(1)}, u32[]{:S(2)}, u32[]{:S(2)}) collective-permute-start(bf16[144,128]{1,0:T(8,128)(2,1)S(1)} %get-tuple-element.32), channel_id=1, source_target_pairs={{0,8},{8,16},{16,24},{24,32},{32,40},{40,48},{48,56},{56,64},{64,7... | collective-permute-start | bytes 110600 | tf_op jit(solution)/shard_map/ppermute | solution.py:520
  10.2 5.5 %all-to-all-start = ((bf16[8,160,128]{2,1,0:T(8,128)(2,1)}), bf16[8,160,128]{2,1,0:T(8,128)(2,1)S(1)}, u32[]{:S(2)}, u32[]{:S(2)}) async-start(bf16[8,160,128]{2,1,0:T(8,128)(2,1)} %get-tuple-element.31), calls=%async_computation | async-start | bytes 655360 | tf_op jit(solution)/shard_map/all_to_all | solution.py:519
  15.7 0.0 copy-done
  15.7 0.1 fusion
  15.8 0.0 collective-permute-done.3.below_ref
  15.8 0.0 collective-permute-done.2.above_ref
  15.9 3.5 %collective-permute-start.4 = (bf16[96,128]{1,0:T(8,128)(2,1)S(1)}, bf16[96,128]{1,0:T(8,128)(2,1)S(1)}, u32[]{:S(2)}, u32[]{:S(2)}) collective-permute-start(bf16[96,128]{1,0:T(8,128)(2,1)S(1)} %pad_maximum_fusion), channel_id=1, source_target_pairs={{0,1},{1,2},{2,3},{3,4},{4,5},{5,6},{6,7},{8,9},{9,10},{10,11},{11... | collective-permute-start | bytes 73736 | tf_op jit(solution)/shard_map/ppermute | solution.py:532
  19.4 1.9 %collective-permute-start.5 = (bf16[96,128]{1,0:T(8,128)(2,1)S(1)}, bf16[96,128]{1,0:T(8,128)(2,1)S(1)}, u32[]{:S(2)}, u32[]{:S(2)}) collective-permute-start(bf16[96,128]{1,0:T(8,128)(2,1)S(1)} %pad_maximum_fusion.1), channel_id=1, source_target_pairs={{1,0},{2,1},{3,2},{4,3},{5,4},{6,5},{7,6},{9,8},{10,9},{11,10},{12... | collective-permute-start | bytes 73736 | tf_op jit(solution)/shard_map/ppermute | solution.py:533
  21.3 1.5 %all-to-all-done = bf16[8,160,128]{2,1,0:T(8,128)(2,1)S(1)} async-done(((bf16[8,160,128]{2,1,0:T(8,128)(2,1)}), bf16[8,160,128]{2,1,0:T(8,128)(2,1)S(1)}, u32[]{:S(2)}, u32[]{:S(2)}) %all-to-all-start) | async-done | bytes 327712 | tf_op jit(solution)/shard_map/all_to_all | solution.py:519
  22.9 3.6 %collective-permute-start = (bf16[1280,128]{1,0:T(8,128)(2,1)S(1)}, bf16[1280,128]{1,0:T(8,128)(2,1)S(1)}, u32[]{:S(2)}, u32[]{:S(2)}) collective-permute-start(bf16[1280,128]{1,0:T(8,128)(2,1)S(1)} %bitcast.17), channel_id=1, source_target_pairs={{0,8},{8,16},{16,24},{24,32},{32,40},{40,48},{48,56},{56,64},{64,7... | collective-permute-start | bytes 983048 | tf_op jit(solution)/shard_map/ppermute | solution.py:534
  26.4 1.3 %collective-permute-start.1 = (bf16[1280,128]{1,0:T(8,128)(2,1)S(1)}, bf16[1280,128]{1,0:T(8,128)(2,1)S(1)}, u32[]{:S(2)}, u32[]{:S(2)}) collective-permute-start(bf16[1280,128]{1,0:T(8,128)(2,1)S(1)} %bitcast.18), channel_id=1, source_target_pairs={{8,0},{16,8},{24,16},{32,24},{40,32},{48,40},{56,48},{64,56},{72,6... | collective-permute-start | bytes 983048 | tf_op jit(solution)/shard_map/ppermute | solution.py:535
  27.7 0.1 pad_add_fusion.1.pos_ref
  27.8 0.0 copy-done.8
  27.8 0.1 copy.20.bias_col_ref
  28.6 0.0 copy-done.7
  28.6 0.0 copy-start.5
  28.6 0.0 copy-start.1
  28.6 0.0 copy-start.2
  28.6 0.0 collective-permute-done.4.left16_ref
  28.6 0.0 collective-permute-done.5.right16_ref
  28.7 0.0 copy-start.3
  28.7 1.0 copy-done.3
  29.6 5.5 %back.1 = bf16[32,2,128,128]{3,2,1,0:T(8,128)(2,1)S(1)} custom-call(bf16[64,128,128]{2,1,0:T(8,128)(2,1)S(1)} %copy-done, bf16[144,128]{1,0:T(8,128)(2,1)S(1)} %collective-permute-done.2.above_ref, bf16[144,128]{1,0:T(8,128)(2,1)S(1)} %collective-permute-done.3.below_ref, bf16[96,128]{1,0:T(8,128)(2,1)S(1)} %collective-permute-done.4.left16_ref, ...), custom_call_target="tpu_custom_call" | custom-call | flops 3221225472 | bytes 12582912 | tf_op jit(solution)/shard_map/back/pallas_call | solution.py:545
  35.2 0.0 copy-start.6
  35.2 1.3 %copy-done.6 = bf16[32,2,128,128]{3,2,1,0:T(8,128)(2,1)} copy-done((bf16[32,2,128,128]{3,2,1,0:T(8,128)(2,1)}, bf16[32,2,128,128]{3,2,1,0:T(8,128)(2,1)S(1)}, u32[]{:S(2)}) %copy-start.6) | copy-done | bytes 2097176
  36.5 0.0 collective-permute-done.band_above_ref
  36.5 0.0 collective-permute-done.1.band_below_ref
  36.5 13.2 %main.1 = (bf16[64,128,128]{2,1,0:T(8,128)(2,1)}, bf16[64,128,128]{2,1,0:T(8,128)(2,1)}, bf16[64,128,128]{2,1,0:T(8,128)(2,1)}, f32[2,64,128]{2,1,0:T(8,128)S(1)...) custom-call(s32[3]{0:T(128)S(1)} %pad_add_fusion.1.pos_ref, ...), custom_call_target="tpu_custom_call" | custom-call | flops 9663676416 | bytes 25165824 | tf_op jit(solution)/shard_map/main/pallas_call | solution.py:565
  49.7 0.0 copy-start.4
  49.7 13.4 %all-to-all-start.1 = ((bf16[128,16,128]{2,1,0:T(8,128)(2,1)}), bf16[128,16,128]{2,1,0:T(8,128)(2,1)S(1)}, u32[]{:S(2)}, u32[]{:S(2)}) async-start(bf16[128,16,128]{2,1,0:T(8,128)(2,1)} %bitcast.21), calls=%async_computation.1 | async-start | bytes 1048576 | tf_op jit(solution)/shard_map/all_to_all | solution.py:624
  63.2 3.4 %collective-permute-start.6 = (bf16[640,128]{1,0:T(8,128)(2,1)S(1)}, bf16[640,128]{1,0:T(8,128)(2,1)S(1)}, u32[]{:S(2)}, u32[]{:S(2)}) collective-permute-start(bf16[640,128]{1,0:T(8,128)(2,1)S(1)} %get-tuple-element.35), channel_id=1, source_target_pairs={{0,8},{8,16},{16,24},{24,32},{32,40},{40,48},{48,56},{56,64},{64,7... | collective-permute-start | bytes 491528 | tf_op jit(solution)/shard_map/ppermute | solution.py:627
  66.6 1.3 %collective-permute-start.7 = (bf16[640,128]{1,0:T(8,128)(2,1)S(1)}, bf16[640,128]{1,0:T(8,128)(2,1)S(1)}, u32[]{:S(2)}, u32[]{:S(2)}) collective-permute-start(bf16[640,128]{1,0:T(8,128)(2,1)S(1)} %get-tuple-element.36), channel_id=1, source_target_pairs={{8,0},{16,8},{24,16},{32,24},{40,32},{48,40},{56,48},{64,56},{72,6... | collective-permute-start | bytes 491528 | tf_op jit(solution)/shard_map/ppermute | solution.py:626
  67.9 8.8 %all-to-all-done.1.got_ref = bf16[128,16,128]{2,1,0:T(8,128)(2,1)S(1)} async-done(((bf16[128,16,128]{2,1,0:T(8,128)(2,1)}), bf16[128,16,128]{2,1,0:T(8,128)(2,1)S(1)}, u32[]{:S(2)}, u32[]{:S(2)}) %all-to-all-start.1) | async-done | bytes 524320 | tf_op jit(solution)/shard_map/all_to_all | solution.py:624
  76.7 1.0 total.1
  77.6 4.9 %all-to-all-start.2 = ((bf16[128,16,128]{2,1,0:T(8,128)(2,1)}), bf16[128,16,128]{2,1,0:T(8,128)(2,1)S(1)}, u32[]{:S(2)}, u32[]{:S(2)}) async-start(bf16[128,16,128]{2,1,0:T(8,128)(2,1)} %total.1), calls=%async_computation.2 | async-start | bytes 1048576 | tf_op jit(solution)/shard_map/all_to_all | solution.py:657
  82.5 0.0 collective-permute-done.6.above_ref
  82.5 0.0 collective-permute-done.7.below_ref
  82.5 1.5 %band.1 = (f32[2,128,128]{2,1,0:T(8,128)S(1)}, bf16[352,128]{1,0:T(8,128)(2,1)S(1)}, bf16[256,128]{1,0:T(8,128)(2,1)S(1)}, bf16[256,128]{1,0:T(8,128)(2,1)S(1)},...) custom-call(s32[3]{0:T(128)S(1)} %pad_add_fusion.1.pos_ref, ...), custom_call_target="tpu_custom_call" | custom-call | flops 4194304 | bytes 1048576 | tf_op jit(solution)/shard_map/band/pallas_call | solution.py:634
  84.0 1.7 %collective-permute-start.8 = (bf16[352,128]{1,0:T(8,128)(2,1)S(1)}, bf16[352,128]{1,0:T(8,128)(2,1)S(1)}, u32[]{:S(2)}, u32[]{:S(2)}) collective-permute-start(bf16[352,128]{1,0:T(8,128)(2,1)S(1)} %get-tuple-element.39), channel_id=1, source_target_pairs={{0,1},{1,2},{2,3},{3,4},{4,5},{5,6},{6,7},{7,0},{8,9},{9,10},{10,1... | collective-permute-start | bytes 270344 | tf_op jit(solution)/shard_map/ppermute | solution.py:645
  85.7 0.0 collective-permute-start.9
  85.7 1.2 %collective-permute-start.10 = (bf16[256,128]{1,0:T(8,128)(2,1)S(1)}, bf16[256,128]{1,0:T(8,128)(2,1)S(1)}, u32[]{:S(2)}, u32[]{:S(2)}) collective-permute-start(bf16[256,128]{1,0:T(8,128)(2,1)S(1)} %get-tuple-element.47), channel_id=1, source_target_pairs={{0,2},{1,3},{2,4},{3,5},{4,6},{5,7},{6,0},{7,1},{8,10},{9,11},{10,... | collective-permute-start | bytes 196616 | tf_op jit(solution)/shard_map/ppermute | solution.py:645
  86.8 3.3 %collective-permute-start.11 = (bf16[256,128]{1,0:T(8,128)(2,1)S(1)}, bf16[256,128]{1,0:T(8,128)(2,1)S(1)}, u32[]{:S(2)}, u32[]{:S(2)}) collective-permute-start(bf16[256,128]{1,0:T(8,128)(2,1)S(1)} %get-tuple-element.48), channel_id=1, source_target_pairs={{0,3},{1,4},{2,5},{3,6},{4,7},{5,0},{6,1},{7,2},{8,11},{9,12},{10,... | collective-permute-start | bytes 196616 | tf_op jit(solution)/shard_map/ppermute | solution.py:645
  90.1 0.8 collective-permute-start.12
  90.9 0.0 collective-permute-done.8.got_left_ref.refs_0_
  90.9 3.2 %collective-permute-start.13 = (bf16[256,128]{1,0:T(8,128)(2,1)S(1)}, bf16[256,128]{1,0:T(8,128)(2,1)S(1)}, u32[]{:S(2)}, u32[]{:S(2)}) collective-permute-start(bf16[256,128]{1,0:T(8,128)(2,1)S(1)} %get-tuple-element.50), channel_id=1, source_target_pairs={{0,5},{1,6},{2,7},{3,0},{4,1},{5,2},{6,3},{7,4},{8,13},{9,14},{10,... | collective-permute-start | bytes 196616 | tf_op jit(solution)/shard_map/ppermute | solution.py:645
  94.1 0.0 collective-permute-done.9.got_right_ref.refs_6_
  94.2 0.2 collective-permute-start.14
  94.3 7.6 %conv.1 = bf16[32,2,128,128]{3,2,1,0:T(8,128)(2,1)} custom-call(s32[3]{0:T(128)S(1)} %pad_add_fusion.1.pos_ref, bf16[64,128,128]{2,1,0:T(8,128)(2,1)} %get-tuple-element.34.smooth_hbm, bf16[640,128]{1,0:T(8,128)(2,1)S(1)} %collective-permute-done.6.above_ref, bf16[640,128]{1,0:T(8,128)(2,1)S(1)} %collective-permute-done.7.below_ref, ...), custom_call_target="tpu_custom_call" | custom-call | flops 3221225472 | bytes 8388608 | tf_op jit(solution)/shard_map/conv/pallas_call | solution.py:659
  101.9 0.0 collective-permute-done.10.refs_1_
  101.9 0.0 collective-permute-done.11.refs_2_
  101.9 0.0 collective-permute-done.12.refs_3_
  101.9 0.0 collective-permute-done.13.refs_4_
  101.9 0.0 collective-permute-done.14.refs_5_
  101.9 0.4 owner.1
  102.4 0.7 copy.22
  103.0 0.0 all-to-all-done.2
  103.0 0.9 finish.1
  (16 shorter events, 0.1 us)
Async XLA Ops:
  0.6 15.1 %copy-start = (bf16[64,128,128]{2,1,0:T(8,128)(2,1)S(1)}, bf16[64,128,128]{2,1,0:T(8,128)(2,1)}, u32[]{:S(2)}) copy-start(bf16[64,128,128]{2,1,0:T(8,128)(2,1)} %cot_hbm.3) | copy-start | bytes 6291460
  0.6 27.2 %copy-start.8 = (f32[128]{0:T(128)S(1)}, f32[128]{0:T(128)}, u32[]{:S(2)}) copy-start(f32[128]{0:T(128)} %param.13) | copy-start | bytes 1540
  0.7 27.9 %copy-start.7 = (bf16[70,128]{1,0:T(8,128)(2,1)S(1)}, bf16[70,128]{1,0:T(8,128)(2,1)}, u32[]{:S(2)}) copy-start(bf16[70,128]{1,0:T(8,128)(2,1)} %param.12) | copy-start | bytes 53764
  3.9 11.9 %collective-permute-start.3 = (bf16[144,128]{1,0:T(8,128)(2,1)S(1)}, bf16[144,128]{1,0:T(8,128)(2,1)S(1)}, u32[]{:S(2)}, u32[]{:S(2)}) collective-permute-start(bf16[144,128]{1,0:T(8,128)(2,1)S(1)} %get-tuple-element.33), channel_id=1, source_target_pairs={{8,0},{16,8},{24,16},{32,24},{40,32},{48,40},{56,48},{64,56},{72,6... | collective-permute-start | bytes 110600 | tf_op jit(solution)/shard_map/ppermute | solution.py:521
  5.2 10.7 %collective-permute-start.2 = (bf16[144,128]{1,0:T(8,128)(2,1)S(1)}, bf16[144,128]{1,0:T(8,128)(2,1)S(1)}, u32[]{:S(2)}, u32[]{:S(2)}) collective-permute-start(bf16[144,128]{1,0:T(8,128)(2,1)S(1)} %get-tuple-element.32), channel_id=1, source_target_pairs={{0,8},{8,16},{16,24},{24,32},{32,40},{40,48},{48,56},{56,64},{64,7... | collective-permute-start | bytes 110600 | tf_op jit(solution)/shard_map/ppermute | solution.py:520
  10.2 12.7 %all-to-all-start = ((bf16[8,160,128]{2,1,0:T(8,128)(2,1)}), bf16[8,160,128]{2,1,0:T(8,128)(2,1)S(1)}, u32[]{:S(2)}, u32[]{:S(2)}) async-start(bf16[8,160,128]{2,1,0:T(8,128)(2,1)} %get-tuple-element.31), calls=%async_computation | async-start | bytes 655360 | tf_op jit(solution)/shard_map/all_to_all | solution.py:519
  15.9 12.8 %collective-permute-start.4 = (bf16[96,128]{1,0:T(8,128)(2,1)S(1)}, bf16[96,128]{1,0:T(8,128)(2,1)S(1)}, u32[]{:S(2)}, u32[]{:S(2)}) collective-permute-start(bf16[96,128]{1,0:T(8,128)(2,1)S(1)} %pad_maximum_fusion), channel_id=1, source_target_pairs={{0,1},{1,2},{2,3},{3,4},{4,5},{5,6},{6,7},{8,9},{9,10},{10,11},{11... | collective-permute-start | bytes 73736 | tf_op jit(solution)/shard_map/ppermute | solution.py:532
  19.4 9.2 %collective-permute-start.5 = (bf16[96,128]{1,0:T(8,128)(2,1)S(1)}, bf16[96,128]{1,0:T(8,128)(2,1)S(1)}, u32[]{:S(2)}, u32[]{:S(2)}) collective-permute-start(bf16[96,128]{1,0:T(8,128)(2,1)S(1)} %pad_maximum_fusion.1), channel_id=1, source_target_pairs={{1,0},{2,1},{3,2},{4,3},{5,4},{6,5},{7,6},{9,8},{10,9},{11,10},{12... | collective-permute-start | bytes 73736 | tf_op jit(solution)/shard_map/ppermute | solution.py:533
  22.9 13.6 %collective-permute-start = (bf16[1280,128]{1,0:T(8,128)(2,1)S(1)}, bf16[1280,128]{1,0:T(8,128)(2,1)S(1)}, u32[]{:S(2)}, u32[]{:S(2)}) collective-permute-start(bf16[1280,128]{1,0:T(8,128)(2,1)S(1)} %bitcast.17), channel_id=1, source_target_pairs={{0,8},{8,16},{16,24},{24,32},{32,40},{40,48},{48,56},{56,64},{64,7... | collective-permute-start | bytes 983048 | tf_op jit(solution)/shard_map/ppermute | solution.py:534
  26.4 10.1 %collective-permute-start.1 = (bf16[1280,128]{1,0:T(8,128)(2,1)S(1)}, bf16[1280,128]{1,0:T(8,128)(2,1)S(1)}, u32[]{:S(2)}, u32[]{:S(2)}) collective-permute-start(bf16[1280,128]{1,0:T(8,128)(2,1)S(1)} %bitcast.18), channel_id=1, source_target_pairs={{8,0},{16,8},{24,16},{32,24},{40,32},{48,40},{56,48},{64,56},{72,6... | collective-permute-start | bytes 983048 | tf_op jit(solution)/shard_map/ppermute | solution.py:535
  28.6 7.9 %copy-start.5 = (f32[64,128]{1,0:T(8,128)S(1)}, f32[64,128]{1,0:T(8,128)}, u32[]{:S(2)}) copy-start(f32[64,128]{1,0:T(8,128)} %noise_ref.1) | copy-start | bytes 98308
  28.6 7.9 %copy-start.1 = (s32[1,16]{1,0:T(1,128)S(1)}, s32[1,16]{1,0:T(1,128)}, u32[]{:S(2)}) copy-start(s32[1,16]{1,0:T(1,128)} %ids_ref.1) | copy-start | bytes 196
  28.6 7.9 %copy-start.2 = (s32[1,16]{1,0:T(1,128)S(1)}, s32[1,16]{1,0:T(1,128)}, u32[]{:S(2)}) copy-start(s32[1,16]{1,0:T(1,128)} %which_ref.1) | copy-start | bytes 196
  28.7 1.0 copy-start.3
  35.2 1.3 %copy-start.6 = (bf16[32,2,128,128]{3,2,1,0:T(8,128)(2,1)}, bf16[32,2,128,128]{3,2,1,0:T(8,128)(2,1)S(1)}, u32[]{:S(2)}) copy-start(bf16[32,2,128,128]{3,2,1,0:T(8,128)(2,1)S(1)} %back.1) | copy-start | bytes 6291460
  49.7 44.6 %copy-start.4 = (bf16[9,128,128]{2,1,0:T(8,128)(2,1)S(1)}, bf16[9,128,128]{2,1,0:T(8,128)(2,1)}, u32[]{:S(2)}) copy-start(bf16[9,128,128]{2,1,0:T(8,128)(2,1)} %w_ref.3) | copy-start | bytes 884740
  49.7 26.9 %all-to-all-start.1 = ((bf16[128,16,128]{2,1,0:T(8,128)(2,1)}), bf16[128,16,128]{2,1,0:T(8,128)(2,1)S(1)}, u32[]{:S(2)}, u32[]{:S(2)}) async-start(bf16[128,16,128]{2,1,0:T(8,128)(2,1)} %bitcast.21), calls=%async_computation.1 | async-start | bytes 1048576 | tf_op jit(solution)/shard_map/all_to_all | solution.py:624
  63.2 19.4 %collective-permute-start.6 = (bf16[640,128]{1,0:T(8,128)(2,1)S(1)}, bf16[640,128]{1,0:T(8,128)(2,1)S(1)}, u32[]{:S(2)}, u32[]{:S(2)}) collective-permute-start(bf16[640,128]{1,0:T(8,128)(2,1)S(1)} %get-tuple-element.35), channel_id=1, source_target_pairs={{0,8},{8,16},{16,24},{24,32},{32,40},{40,48},{48,56},{56,64},{64,7... | collective-permute-start | bytes 491528 | tf_op jit(solution)/shard_map/ppermute | solution.py:627
  66.6 15.9 %collective-permute-start.7 = (bf16[640,128]{1,0:T(8,128)(2,1)S(1)}, bf16[640,128]{1,0:T(8,128)(2,1)S(1)}, u32[]{:S(2)}, u32[]{:S(2)}) collective-permute-start(bf16[640,128]{1,0:T(8,128)(2,1)S(1)} %get-tuple-element.36), channel_id=1, source_target_pairs={{8,0},{16,8},{24,16},{32,24},{40,32},{48,40},{56,48},{64,56},{72,6... | collective-permute-start | bytes 491528 | tf_op jit(solution)/shard_map/ppermute | solution.py:626
  77.6 25.4 %all-to-all-start.2 = ((bf16[128,16,128]{2,1,0:T(8,128)(2,1)}), bf16[128,16,128]{2,1,0:T(8,128)(2,1)S(1)}, u32[]{:S(2)}, u32[]{:S(2)}) async-start(bf16[128,16,128]{2,1,0:T(8,128)(2,1)} %total.1), calls=%async_computation.2 | async-start | bytes 1048576 | tf_op jit(solution)/shard_map/all_to_all | solution.py:657
  84.0 6.9 %collective-permute-start.8 = (bf16[352,128]{1,0:T(8,128)(2,1)S(1)}, bf16[352,128]{1,0:T(8,128)(2,1)S(1)}, u32[]{:S(2)}, u32[]{:S(2)}) collective-permute-start(bf16[352,128]{1,0:T(8,128)(2,1)S(1)} %get-tuple-element.39), channel_id=1, source_target_pairs={{0,1},{1,2},{2,3},{3,4},{4,5},{5,6},{6,7},{7,0},{8,9},{9,10},{10,1... | collective-permute-start | bytes 270344 | tf_op jit(solution)/shard_map/ppermute | solution.py:645
  85.7 8.5 %collective-permute-start.9 = (bf16[352,128]{1,0:T(8,128)(2,1)S(1)}, bf16[352,128]{1,0:T(8,128)(2,1)S(1)}, u32[]{:S(2)}, u32[]{:S(2)}) collective-permute-start(bf16[352,128]{1,0:T(8,128)(2,1)S(1)} %get-tuple-element.40), channel_id=1, source_target_pairs={{0,7},{1,0},{2,1},{3,2},{4,3},{5,4},{6,5},{7,6},{8,15},{9,8},{10,9... | collective-permute-start | bytes 270344 | tf_op jit(solution)/shard_map/ppermute | solution.py:645
  85.7 16.2 %collective-permute-start.10 = (bf16[256,128]{1,0:T(8,128)(2,1)S(1)}, bf16[256,128]{1,0:T(8,128)(2,1)S(1)}, u32[]{:S(2)}, u32[]{:S(2)}) collective-permute-start(bf16[256,128]{1,0:T(8,128)(2,1)S(1)} %get-tuple-element.47), channel_id=1, source_target_pairs={{0,2},{1,3},{2,4},{3,5},{4,6},{5,7},{6,0},{7,1},{8,10},{9,11},{10,... | collective-permute-start | bytes 196616 | tf_op jit(solution)/shard_map/ppermute | solution.py:645
  86.8 15.1 %collective-permute-start.11 = (bf16[256,128]{1,0:T(8,128)(2,1)S(1)}, bf16[256,128]{1,0:T(8,128)(2,1)S(1)}, u32[]{:S(2)}, u32[]{:S(2)}) collective-permute-start(bf16[256,128]{1,0:T(8,128)(2,1)S(1)} %get-tuple-element.48), channel_id=1, source_target_pairs={{0,3},{1,4},{2,5},{3,6},{4,7},{5,0},{6,1},{7,2},{8,11},{9,12},{10,... | collective-permute-start | bytes 196616 | tf_op jit(solution)/shard_map/ppermute | solution.py:645
  90.1 11.8 %collective-permute-start.12 = (bf16[256,128]{1,0:T(8,128)(2,1)S(1)}, bf16[256,128]{1,0:T(8,128)(2,1)S(1)}, u32[]{:S(2)}, u32[]{:S(2)}) collective-permute-start(bf16[256,128]{1,0:T(8,128)(2,1)S(1)} %get-tuple-element.49), channel_id=1, source_target_pairs={{0,4},{1,5},{2,6},{3,7},{4,0},{5,1},{6,2},{7,3},{8,12},{9,13},{10,... | collective-permute-start | bytes 196616 | tf_op jit(solution)/shard_map/ppermute | solution.py:645
  90.9 11.0 %collective-permute-start.13 = (bf16[256,128]{1,0:T(8,128)(2,1)S(1)}, bf16[256,128]{1,0:T(8,128)(2,1)S(1)}, u32[]{:S(2)}, u32[]{:S(2)}) collective-permute-start(bf16[256,128]{1,0:T(8,128)(2,1)S(1)} %get-tuple-element.50), channel_id=1, source_target_pairs={{0,5},{1,6},{2,7},{3,0},{4,1},{5,2},{6,3},{7,4},{8,13},{9,14},{10,... | collective-permute-start | bytes 196616 | tf_op jit(solution)/shard_map/ppermute | solution.py:645
  94.2 7.8 %collective-permute-start.14 = (bf16[256,128]{1,0:T(8,128)(2,1)S(1)}, bf16[256,128]{1,0:T(8,128)(2,1)S(1)}, u32[]{:S(2)}, u32[]{:S(2)}) collective-permute-start(bf16[256,128]{1,0:T(8,128)(2,1)S(1)} %get-tuple-element.51), channel_id=1, source_target_pairs={{0,6},{1,7},{2,0},{3,1},{4,2},{5,3},{6,4},{7,5},{8,14},{9,15},{10,... | collective-permute-start | bytes 196616 | tf_op jit(solution)/shard_map/ppermute | solution.py:645
